TPU v7x, 512 devices: a whole 4x8x8 slice. The times are simulated.
512 devices in a mesh: dp: 32 (over y_hi, z, core), fsdp: 16 (over y_lo, x).
Axes of the slice: x: 4, y: 8 (y_hi: 2, y_lo: 4; y = y_hi * 4 + y_lo), z: 8, core: 2. Of those that a mesh axis runs over, the one named last changes fastest.
Arguments:
- state0: float32 [65536, 2640], P(('dp', 'fsdp')), may hold values from -6 to 6
- injected: bfloat16 [65536, 2640], P(('dp', 'fsdp')), may hold values from -6 to 6
- core_weight: bfloat16 [2640, 2640], P('fsdp'), may hold values from -0.125 to 0.125
- gain: float32 [2640], replicated, may hold values from 0.1 to 1.9
- counts: int32 [512], P(('dp', 'fsdp')), may hold values from 1 to 2, as said below
- cotangent: float32 [65536, 2640], P(('dp', 'fsdp')), may hold values from -6 to 6
Outputs:
- final_state: bfloat16 [65536, 2640], P(('dp', 'fsdp'))
- injected_grad: bfloat16 [65536, 2640], P(('dp', 'fsdp'))
- gain_grad: float32 [2640], replicated
Inputs may be any that keep to these rules, and one draw needn't show every extreme that they name: Group j runs counts[j] iterations; in every draw some group runs 2 and some group runs 1.
All inputs are finite; a program needn't handle non-finite values.
Results may differ from a plain program's by a relative error of at most 0.0045.
Values may be sent and summed in bfloat16 or wider, within the bound.
No kernel may reach another device: no remote copies, remote signals or barrier semaphores. Data moves between devices by JAX's collectives and lax.ppermute only.
A program may use at most 128 MiB of HBM per device.

v0:
```python
import jax
import jax.numpy as jnp
from jax import lax
from jax.sharding import PartitionSpec as P

epsilon = 1e-06


def normalize(state):
    inv_rms = lax.rsqrt(jnp.mean(state * state, axis=-1, keepdims=True) + epsilon)
    return (state * inv_rms, inv_rms)


def advance(state, gain, weight, inject):
    normed_rows, inv_rms = normalize(state)
    operand = (normed_rows * gain).astype(jnp.bfloat16)
    return jnp.dot(operand, weight, preferred_element_type=jnp.float32) + inject.astype(jnp.float32)


def retreat(state, upstream, gain, weight):
    normed_rows, inv_rms = normalize(state)
    up_bf = upstream.astype(jnp.bfloat16)
    back_proj = lax.dot_general(
        up_bf, weight, (((1,), (1,)), ((), ())), preferred_element_type=jnp.float32
    )
    gain_part = jnp.sum(back_proj * normed_rows, axis=0)
    scaled = back_proj * gain
    state_grad = inv_rms * (
        scaled - normed_rows * jnp.mean(scaled * normed_rows, axis=-1, keepdims=True)
    )
    return (state_grad, gain_part)


def finish(start, first, inject, upstream, rounds, gain, weight):

    def step_once(step_index, states):
        earlier, before, latest = states
        return (before, latest, advance(latest, gain, weight, inject))

    earlier, before, latest = lax.fori_loop(1, rounds, step_once, (start, start, first))
    state_grad, gain_part = retreat(before, upstream, gain, weight)

    def deeper():
        unused, second_part = retreat(earlier, state_grad, gain, weight)
        return (gain_part + second_part, upstream + state_grad)

    def shallow():
        return (gain_part, upstream)

    total_part, inject_grad = lax.cond(rounds >= 2, deeper, shallow)
    return (latest.astype(jnp.bfloat16), inject_grad.astype(jnp.bfloat16), total_part)


def shards(state0, injected, core_weight, gain, counts, cotangent):
    rounds = counts[0]
    work_state, work_inject, work_upstream = (state0, injected, cotangent)
    resident = lax.all_gather(core_weight, "fsdp", axis=0, tiled=True)
    first = advance(work_state, gain, resident, work_inject)
    final_rows, inject_grad, total_part = finish(
        work_state, first, work_inject, work_upstream, rounds, gain, resident
    )
    gain_grad = lax.psum(total_part, ("dp", "fsdp"))
    return (final_rows, inject_grad, gain_grad)


def solution(mesh):
    in_specs = (
        P(("dp", "fsdp"), None),
        P(("dp", "fsdp"), None),
        P("fsdp", None),
        P(),
        P(("dp", "fsdp")),
        P(("dp", "fsdp"), None),
    )
    out_specs = (P(("dp", "fsdp"), None), P(("dp", "fsdp"), None), P())
    return jax.shard_map(shards, mesh=mesh, in_specs=in_specs, out_specs=out_specs, check_vma=False)
```

profile of v0, /device:TPU:1, one launch (start us, length us, event | category | flops | bytes accessed | tf_op | source)
XLA Modules:
  0.0 363.6 jit_solution(12951289532714270778)
XLA Ops:
  7.2 0.0 all-gather.3.cloned.1.call-start
  7.2 1.3 copy.51
  8.5 0.0 copy-start
  8.5 0.0 all-gather.3.cloned.1.call-update
  8.6 1.6 copy.21
  10.2 0.1 copy.31
  10.9 0.0 copy-done
  10.9 0.4 multiply_reduce_fusion.6
  11.3 0.0 copy-start.4
  11.3 0.0 copy-start.7
  11.3 170.2 %all-gather.3.cloned.1.call-done = bf16[16,165,2640]{2,1,0:T(8,128)(2,1)} async-done(((bf16[1,165,2640]{2,1,0:T(8,128)(2,1)}), bf16[16,165,2640]{2,1,0:T(8,128)(2,1)}) %all-gather.3.cloned.1.call-update) | async-done | bytes 13939216 | tf_op jit(solution)/shard_map/all_gather | solution.py:57
  181.5 18.7 %reshape.48 = bf16[2640,2640]{1,0:T(8,128)(2,1)} reshape(bf16[16,165,2640]{2,1,0:T(8,128)(2,1)} %all-gather.3.cloned.1.call-done) | data formatting | bytes 27878400
  200.2 0.0 copy-done.4
  200.2 0.0 copy-done.7
  200.2 9.6 %multiply_reduce_fusion.3 = (f32[128]{0:T(128)S(1)}, f32[128,2640]{0,1:T(8,128)S(1)}) fusion(bf16[128,2640]{0,1:T(8,128)(2,1)S(1)} %copy-done.4, bf16[2640,2640]{1,0:T(8,128)(2,1)} %reshape.48, f32[128,2640]{1,0:T(8,128)} %copy.21, f32[2640]{0:T(1024)S(1)} %copy-done.7, f32[128]{0:T(128)S(1)} %add_rsqrt_fusion.3), kind=kOutput, calls=%fused_computation.17 | convolution fusion | flops 1786582912 | bytes 17329984 | tf_op jit(solution)/shard_map/dot_general | solution.py:17
  209.9 0.8 while.14
  210.7 0.4 multiply_reduce_fusion.5
  211.1 10.9 %multiply_reduce_fusion.4 = (f32[2640]{0:T(1024)S(1)}, f32[128,2640]{0,1:T(8,128)}, f32[128,2640]{0,1:T(8,128)}) fusion(f32[128,2640]{0,1:T(8,128)S(1)} %get-tuple-element.125, f32[128]{0:T(128)S(1)} %add_rsqrt_fusion.2, bf16[2640,2640]{1,0:T(8,128)(2,1)} %get-tuple-element.335, f32[128,2640]{0,1:T(8,128)} %param.15), kind=kOutput, calls=%fused_computation.18 | convolution fusion | flops 1785566592 | bytes 19356992 | tf_op jit(solution)/shard_map/dot_general | solution.py:23
  222.0 0.0 copy-start.1
  222.0 1.2 mul.112
  223.1 0.7 copy-done.1
  223.8 2.0 conditional.1
  223.8 1.7 copy.22
  225.5 0.3 copy.27
  225.8 0.0 copy-start.6
  225.8 130.0 %psum.7 = f32[2640]{0:T(1024)} all-reduce(f32[2640]{0:T(1024)S(1)} %get-tuple-element.128), channel_id=1, replica_groups=mesh['dp'=32,'fsdp'=16] {'dp','fsdp'}, use_global_device_ids=true, to_apply=%region_11.0 | all-reduce | flops 2640 | bytes 21120 | tf_op jit(solution)/shard_map/psum | solution.py:62
  355.8 0.9 convert_element_type.37
  356.7 0.0 copy-done.6
  (2 shorter events, 0.0 us)
Async XLA Ops:
  7.2 174.4 %all-gather.3.cloned.1.call-start = ((), (), s32[]{:S(2)}) async-start(), calls=%async_computation | async-start | bytes 15353856 | tf_op jit(solution)/shard_map/all_gather | solution.py:57
  8.5 2.4 copy-start
  11.3 189.0 %copy-start.4 = (bf16[128,2640]{0,1:T(8,128)(2,1)S(1)}, bf16[128,2640]{0,1:T(8,128)(2,1)}, u32[]{:S(2)}) copy-start(bf16[128,2640]{0,1:T(8,128)(2,1)} %param.11) | copy-start | bytes 2027524
  11.3 188.9 %copy-start.7 = (f32[2640]{0:T(1024)S(1)}, f32[2640]{0:T(1024)}, u32[]{:S(2)}) copy-start(f32[2640]{0:T(1024)} %param.13) | copy-start | bytes 31684
  222.0 1.8 copy-start.1
  225.8 130.9 %copy-start.6 = (bf16[128,2640]{0,1:T(8,128)(2,1)}, bf16[128,2640]{0,1:T(8,128)(2,1)S(1)}, u32[]{:S(2)}) copy-start(bf16[128,2640]{0,1:T(8,128)(2,1)S(1)} %get-tuple-element.171) | copy-start | bytes 2027524
Sparse Core Ops, SparseCore 0:
  10.1 171.4 all-gather.2
where the time goes:
time: 364 us
  waiting for transfers between devices  170 us (47%)
  blocking collectives  130 us (36%)
  local copies, waits for them, and re-layouts  25.6 us (7%)
  matrix products  20.5 us (6%)
  between operations  14.7 us (4%)
    all_gather x1, waiting for transfers between devices, shards(): resident = lax.all_gather(core_weight, 'fsdp', axis=0, tiled=True)  170 us
    psum x1, blocking collectives, shards(): gain_grad = lax.psum(total_part, ('dp', 'fsdp'))  130 us
    unnamed x14, local copies, waits for them, and re-layouts  22.4 us
    dot_general x1, matrix products, retreat(): lax.dot_general(up_bf, weight, (((1,), (1,)), ((), ())), preferred_elemen...  10.9 us
    dot_general x1, matrix products, advance(): jnp.dot(operand, weight, preferred_element_type=jnp.float32)  9.62 us
  transfers between devices with their start and end apart: 1, of which 1 were waited for; matrix products, arithmetic and copies ran while one was open for 1% of the time, Pallas kernels for 0%

commit v1 on v0

v1 whole, which is shorter than its diff:
```python
import itertools

import jax
import jax.numpy as jnp
from jax import lax
from jax.experimental import pallas as pl
from jax.experimental.pallas import tpu as pltpu
from jax.sharding import PartitionSpec as P

AXES = ("dp", "fsdp")
NX, NY, NZ, NC = 4, 8, 8, 2
YL = 4
W = 2640
SH = 165
SP = 176
WP = 16 * SP
HALF = WP // 2
TOK = 128
TILE = 256
EPS = 1e-06
BF = jnp.bfloat16
F32 = jnp.float32


def line(x, y, z, c):
    x, y, z, c = x % NX, y % NY, z % NZ, c % NC
    return ((y // YL) * NZ * NC + z * NC + c) * 16 + (y % YL) * NX + x


def chips():
    return itertools.product(range(NX), range(NY), range(NZ), range(NC))


def along(first, step):
    pairs = []
    for x, y, z, c in chips():
        in_x = (c == 0) == first
        pairs.append((line(x, y, z, c), line(x + step * in_x, y + step * (not in_x), z, c)))
    return pairs


SWAP = [(line(x, y, z, c), line(x, y, z, 1 - c)) for x, y, z, c in chips()]


def send(array, pairs):
    return lax.ppermute(array, AXES, pairs)


def nt(a, b):
    return lax.dot_general(a, b, (((1,), (1,)), ((), ())), preferred_element_type=F32)


def core_kernel(place, op0_ref, cb_ref, n0_ref, inj_ref, cot_ref, gain_ref, *rest):
    pieces = rest[:10]
    final_ref, injg_ref, part_ref = rest[10:13]
    w_ref, s1_ref, back_ref, op1_ref, db_ref, sems = rest[13:]
    px, py, pc, rounds = place[0], place[1], place[2], place[3]
    copies = []
    for who in range(2):
        core = pc if who == 0 else 1 - pc
        base = 5 * who
        for k in range(4):
            for j in range(4):
                sx = jnp.where(core == 0, px + 4 - j, px + 4 - k) % 4
                sy = jnp.where(core == 0, py + 4 - k, py + 4 - j) % 4
                row = pl.multiple_of((sy * 4 + sx) * SP, SP)
                if k == 0:
                    src = pieces[base].at[j]
                elif k == 1:
                    src = pieces[base + 1].at[j]
                elif k == 3:
                    src = pieces[base + 2].at[j]
                elif j < 2:
                    src = pieces[base + 3].at[j]
                else:
                    src = pieces[base + 4].at[j - 2]
                dst = w_ref.at[pl.ds(row, SP), pl.ds(pl.multiple_of(core * HALF, 128), HALF)]
                copies.append(pltpu.make_async_copy(src, dst, sems.at[len(copies)]))
    for c in copies:
        c.start()
    for c in copies:
        c.wait()
    deep = rounds >= 2

    def first(t, ssq):
        cols = pl.ds(pl.multiple_of(t * TILE, TILE), TILE)
        s1 = jnp.dot(op0_ref[...], w_ref[:, cols], preferred_element_type=F32) + inj_ref[:, cols].astype(F32)
        s1_ref[:, cols] = s1
        back_ref[:, cols] = nt(cb_ref[...], w_ref[cols, :])
        return ssq + jnp.sum(s1 * s1, axis=1, keepdims=True)

    ssq = lax.fori_loop(0, WP // TILE, first, jnp.zeros((TOK, 1), F32))
    inv1 = lax.rsqrt(ssq / W + EPS)

    def second(t, dots):
        cols = pl.ds(pl.multiple_of(t * TILE, TILE), TILE)
        n1 = s1_ref[:, cols] * inv1
        back = back_ref[:, cols]
        gain = gain_ref[:, cols]
        op1_ref[:, cols] = (n1 * gain).astype(BF)
        v = jnp.where(deep, n1, n0_ref[:, cols])
        part_ref[:, cols] = jnp.sum(back * v, axis=0, keepdims=True)
        return dots + jnp.sum(back * gain * n1, axis=1, keepdims=True)

    dots = lax.fori_loop(0, WP // TILE, second, jnp.zeros((TOK, 1), F32))
    mean1 = dots / W

    def third(t, carry):
        cols = pl.ds(pl.multiple_of(t * TILE, TILE), TILE)
        n1 = s1_ref[:, cols] * inv1
        d1 = inv1 * (back_ref[:, cols] * gain_ref[:, cols] - n1 * mean1)
        db_ref[:, cols] = d1.astype(BF)
        cot = cot_ref[:, cols]
        injg_ref[:, cols] = jnp.where(deep, cot + d1, cot).astype(BF)
        return carry

    lax.fori_loop(0, WP // TILE, third, 0)

    def fourth(t, carry):
        cols = pl.ds(pl.multiple_of(t * TILE, TILE), TILE)
        s2 = jnp.dot(op1_ref[...], w_ref[:, cols], preferred_element_type=F32) + inj_ref[:, cols].astype(F32)
        final_ref[:, cols] = jnp.where(deep, s2, s1_ref[:, cols]).astype(BF)
        back = nt(db_ref[...], w_ref[cols, :])
        part2 = jnp.sum(back * n0_ref[:, cols], axis=0, keepdims=True)
        part_ref[:, cols] += jnp.where(deep, part2, jnp.zeros_like(part2))
        return carry

    lax.fori_loop(0, WP // TILE, fourth, 0)


def core_call(place, op0, cb, n0, inj, cot, gain, pieces):
    vm = pl.BlockSpec(memory_space=pltpu.VMEM)
    return pl.pallas_call(
        core_kernel,
        out_shape=(
            jax.ShapeDtypeStruct((TOK, WP), BF),
            jax.ShapeDtypeStruct((TOK, WP), BF),
            jax.ShapeDtypeStruct((1, WP), F32),
        ),
        in_specs=[pl.BlockSpec(memory_space=pltpu.SMEM)] + [vm] * 6 + [pl.BlockSpec(memory_space=pl.ANY)] * 10,
        out_specs=(vm, vm, vm),
        scratch_shapes=[
            pltpu.VMEM((WP, WP), BF),
            pltpu.VMEM((TOK, WP), F32),
            pltpu.VMEM((TOK, WP), F32),
            pltpu.VMEM((TOK, WP), BF),
            pltpu.VMEM((TOK, WP), BF),
            pltpu.SemaphoreType.DMA((32,)),
        ],
        compiler_params=pltpu.CompilerParams(vmem_limit_bytes=48 * 2**20),
        cost_estimate=pl.CostEstimate(flops=8 * TOK * WP * WP, bytes_accessed=2 * WP * WP, transcendentals=0),
    )(place, op0, cb, n0, inj, cot, gain, *pieces)


def widen(array):
    flipped = array.T.reshape(16, SH, TOK)
    return jnp.pad(flipped, ((0, 0), (0, SP - SH), (0, 0))).reshape(WP, TOK).T


def narrow(array):
    return array.T.reshape(16, SP, -1)[:, :SH].reshape(W, -1).T


def gather(weight, pc):
    wide = jnp.pad(weight.reshape(SH, 16, SH), ((0, SP - SH), (0, 0), (0, SP - SH))).reshape(SP, WP)
    own = jnp.where(pc == 0, wide[:, :HALF], wide[:, HALF:])
    m1 = send(own, along(True, 1))
    m3 = send(own, along(True, -1))
    m2 = send(m1, along(True, 1))
    row = jnp.stack([own, m1, m2, m3])
    n1 = send(row, along(False, 1))
    n3 = send(row, along(False, -1))
    n2a = send(n1[:2], along(False, 1))
    n2b = send(n3[2:], along(False, -1))
    mine = (row, n1, n3, n2a, n2b)
    return mine + tuple(send(a, SWAP) for a in mine)


def total(part):
    dp_groups = [[yh * 16 + z * 2 + c for z in range(8) for c in range(2)] for yh in range(2)]
    got = lax.all_to_all(jnp.broadcast_to(part, (16, WP)), "dp", 0, 0, axis_index_groups=dp_groups)
    part = jnp.sum(got.reshape(16, WP), axis=0, keepdims=True)
    planes = [[line(x, y, z, c) for y in range(NY) for x in range(NX)] for z in range(NZ) for c in range(NC)]
    got = lax.all_to_all(jnp.broadcast_to(part, (32, WP)), AXES, 0, 0, axis_index_groups=planes)
    return jnp.sum(got.reshape(32, WP), axis=0, keepdims=True)


def shards(state0, injected, core_weight, gain, counts, cotangent):
    dp, fs = lax.axis_index("dp"), lax.axis_index("fsdp")
    pc = dp % 2
    place = jnp.stack([fs % 4, fs // 4, pc, counts[0]]).astype(jnp.int32)
    pieces = gather(core_weight, pc)
    gain_w = widen(jnp.broadcast_to(gain, (TOK, W)))[:1]
    start = widen(state0)
    inv = lax.rsqrt(jnp.sum(start * start, axis=-1, keepdims=True) / W + EPS)
    n0 = start * inv
    op0 = (n0 * gain_w).astype(BF)
    cot = widen(cotangent)
    final, injg, part = core_call(place, op0, cot.astype(BF), n0, widen(injected), cot, gain_w, pieces)
    return (narrow(final), narrow(injg), narrow(total(part)).reshape(W))


def solution(mesh):
    rows = P(AXES, None)
    return jax.shard_map(
        shards,
        mesh=mesh,
        in_specs=(rows, rows, P("fsdp", None), P(), P(AXES), rows),
        out_specs=(rows, rows, P()),
        check_vma=False,
    )
```

time: 364 us -> 179 us (0.49)
  waiting for transfers between devices: 170 us -> 35.1 us
  blocking collectives: 130 us -> 17.5 us
  starting transfers between devices: 0.04 us -> 53.4 us
  Pallas kernels: 0 us -> 25.7 us
  matrix products: 20.5 us -> 0 us
  between operations: 14.7 us -> 1.68 us
  local copies, waits for them, and re-layouts: 25.6 us -> 38.5 us
  other arithmetic: 1.65 us -> 6.27 us
    all_gather x1 -> x0, waiting for transfers between devices: 170 us -> none  [shards(): resident = lax.all_gather(core_weight, 'fsdp', axis=0, tiled=True)]
    psum x1 -> x0, blocking collectives: 130 us -> none  [shards(): gain_grad = lax.psum(total_part, ('dp', 'fsdp'))]
    ppermute x0 -> x12, starting transfers between devices: none -> 47.8 us  [send(): return lax.ppermute(array, AXES, pairs)]
    pallas_call x0 -> x1, Pallas kernels: none -> 25.7 us  [core_call(): pl.pallas_call(core_kernel, out_shape=(jax.ShapeDtypeStruct((TOK, WP), BF...]
    ppermute x0 -> x12, waiting for transfers between devices: none -> 23.9 us  [send(): return lax.ppermute(array, AXES, pairs)]
    reshape x0 -> x11, local copies, waits for them, and re-layouts: none -> 22.1 us  [the longest x4 9.09 us: widen(): return jnp.pad(flipped, ((0, 0), (0, SP - SH), (0, 0))).reshape(WP, TOK).T]
    dot_general x2 -> x0, matrix products: 20.5 us -> none  [the longest x1 10.9 us: retreat(): lax.dot_general(up_bf, weight, (((1,), (1,)), ((), ())), preferred_elemen...]
    unnamed x14 -> x18, local copies, waits for them, and re-layouts: 22.4 us -> 2.18 us
  transfers between devices with their start and end apart: 1 -> 13, of which waited for: 1 -> 5; matrix products, arithmetic and copies ran while one was open for 1% -> 16% of each run, Pallas kernels for 0% -> 0%
where the time goes in v1:
time: 179 us; the launch traced here: 178 us
  starting transfers between devices  53.4 us (30%)
  local copies, waits for them, and re-layouts  38.5 us (22%)
  waiting for transfers between devices  35.1 us (20%)
  Pallas kernels  25.7 us (14%)
  blocking collectives  17.5 us (10%)
  other arithmetic  6.27 us (4%)
    ppermute x12, starting transfers between devices, send(): return lax.ppermute(array, AXES, pairs)  47.8 us
    pallas_call x1, Pallas kernels, core_call(): pl.pallas_call(core_kernel, out_shape=(jax.ShapeDtypeStruct((TOK, WP), BF...  25.7 us
    ppermute x12, waiting for transfers between devices, send(): return lax.ppermute(array, AXES, pairs)  23.9 us
    all_to_all x1, blocking collectives, total(): lax.all_to_all(jnp.broadcast_to(part, (16, WP)), 'dp', 0, 0, axis_index_g...  17.5 us
    all_to_all x1, waiting for transfers between devices, total(): lax.all_to_all(jnp.broadcast_to(part, (32, WP)), AXES, 0, 0, axis_index_g...  11.2 us
    reshape x4, local copies, waits for them, and re-layouts, widen(): return jnp.pad(flipped, ((0, 0), (0, SP - SH), (0, 0))).reshape(WP, TOK).T  9.09 us
    reshape x1, local copies, waits for them, and re-layouts, gather(): weight.reshape(SH, 16, SH)  5.79 us
    all_to_all x1, starting transfers between devices, total(): lax.all_to_all(jnp.broadcast_to(part, (32, WP)), AXES, 0, 0, axis_index_g...  5.55 us
  transfers between devices with their start and end apart: 13, of which 5 were waited for; matrix products, arithmetic and copies ran while one was open for 16% of the time, Pallas kernels for 0%

profile of v1, /device:TPU:1, one launch (start us, length us, event | category | flops | bytes accessed | tf_op | source)
XLA Modules:
  0.0 178.2 jit_solution(2098290172445087942)
XLA Ops:
  0.6 5.8 %reshape.77 = bf16[165,16,165]{2,1,0:T(8,128)(2,1)} reshape(bf16[165,2640]{1,0:T(8,128)(2,1)} %param.8) | data formatting | bytes 1742400 | tf_op jit(solution)/shard_map/reshape | solution.py:165
  6.4 1.6 pad.22
  8.0 2.2 %reshape.78 = bf16[176,2816]{1,0:T(8,128)(2,1)S(1)} reshape(bf16[176,16,176]{2,1,0:T(8,128)(2,1)S(1)} %pad.22) | data formatting | bytes 1982464 | tf_op jit(solution)/shard_map/reshape | solution.py:165
  10.3 4.0 %collective-permute-start = (bf16[176,1408]{1,0:T(8,128)(2,1)S(1)}, bf16[176,1408]{1,0:T(8,128)(2,1)S(1)}, u32[]{:S(2)}, u32[]{:S(2)}) collective-permute-start(bf16[176,1408]{1,0:T(8,128)(2,1)S(1)} %slice_select_fusion), channel_id=1, source_target_pairs={{0,1},{16,20},{32,33},{48,52},{64,65},{80,84},{96,97},{112,116},{1... | collective-permute-start | bytes 1486856 | tf_op jit(solution)/shard_map/ppermute | solution.py:46
  14.4 3.8 %collective-permute-start.2 = (bf16[176,1408]{1,0:T(8,128)(2,1)S(1)}, bf16[176,1408]{1,0:T(8,128)(2,1)S(1)}, u32[]{:S(2)}, u32[]{:S(2)}) collective-permute-start(bf16[176,1408]{1,0:T(8,128)(2,1)S(1)} %slice_select_fusion), channel_id=1, source_target_pairs={{0,3},{16,284},{32,35},{48,316},{64,67},{80,348},{96,99},{112,380}... | collective-permute-start | bytes 1486856 | tf_op jit(solution)/shard_map/ppermute | solution.py:46
  18.2 4.3 %collective-permute-done = bf16[176,1408]{1,0:T(8,128)(2,1)S(1)} collective-permute-done((bf16[176,1408]{1,0:T(8,128)(2,1)S(1)}, bf16[176,1408]{1,0:T(8,128)(2,1)S(1)}, u32[]{:S(2)}, u32[]{:S(2)}) %collective-permute-start) | collective-permute-done | bytes 495648 | tf_op jit(solution)/shard_map/ppermute | solution.py:46
  22.5 1.9 %collective-permute-start.1 = (bf16[176,1408]{1,0:T(8,128)(2,1)S(1)}, bf16[176,1408]{1,0:T(8,128)(2,1)S(1)}, u32[]{:S(2)}, u32[]{:S(2)}) collective-permute-start(bf16[176,1408]{1,0:T(8,128)(2,1)S(1)} %collective-permute-done), channel_id=1, source_target_pairs={{0,1},{16,20},{32,33},{48,52},{64,65},{80,84},{96,97},{112,116},{1... | collective-permute-start | bytes 1486856 | tf_op jit(solution)/shard_map/ppermute | solution.py:46
  24.5 8.8 %collective-permute-done.1 = bf16[176,1408]{1,0:T(8,128)(2,1)S(1)} collective-permute-done((bf16[176,1408]{1,0:T(8,128)(2,1)S(1)}, bf16[176,1408]{1,0:T(8,128)(2,1)S(1)}, u32[]{:S(2)}, u32[]{:S(2)}) %collective-permute-start.1) | collective-permute-done | bytes 495648 | tf_op jit(solution)/shard_map/ppermute | solution.py:46
  33.3 1.6 pad_maximum_fusion.rest_0_
  34.9 4.4 %collective-permute-start.4 = (bf16[4,176,1408]{2,1,0:T(8,128)(2,1)}, bf16[4,176,1408]{2,1,0:T(8,128)(2,1)}, u32[]{:S(2)}, u32[]{:S(2)}) collective-permute-start(bf16[4,176,1408]{2,1,0:T(8,128)(2,1)} %pad_maximum_fusion.rest_0_), channel_id=1, source_target_pairs={{0,268},{16,19},{32,300},{48,51},{64,332},{80,83},{96,364},{112,11... | collective-permute-start | bytes 5947400 | tf_op jit(solution)/shard_map/ppermute | solution.py:46
  39.3 1.9 %collective-permute-start.3 = (bf16[4,176,1408]{2,1,0:T(8,128)(2,1)}, bf16[4,176,1408]{2,1,0:T(8,128)(2,1)}, u32[]{:S(2)}, u32[]{:S(2)}) collective-permute-start(bf16[4,176,1408]{2,1,0:T(8,128)(2,1)} %pad_maximum_fusion.rest_0_), channel_id=1, source_target_pairs={{0,4},{16,17},{32,36},{48,49},{64,68},{80,81},{96,100},{112,113},{... | collective-permute-start | bytes 5947400 | tf_op jit(solution)/shard_map/ppermute | solution.py:46
  42.1 0.4 multiply_reduce_fusion
  42.5 9.3 %collective-permute-start.7 = (bf16[4,176,1408]{2,1,0:T(8,128)(2,1)}, bf16[4,176,1408]{2,1,0:T(8,128)(2,1)}, u32[]{:S(2)}, u32[]{:S(2)}) collective-permute-start(bf16[4,176,1408]{2,1,0:T(8,128)(2,1)} %pad_maximum_fusion.rest_0_), channel_id=1, source_target_pairs={{0,16},{16,0},{32,48},{48,32},{64,80},{80,64},{96,112},{112,96},{1... | collective-permute-start | bytes 5947400 | tf_op jit(solution)/shard_map/ppermute | solution.py:46
  51.8 9.6 %collective-permute-done.4.rest_2_ = bf16[4,176,1408]{2,1,0:T(8,128)(2,1)} collective-permute-done((bf16[4,176,1408]{2,1,0:T(8,128)(2,1)}, bf16[4,176,1408]{2,1,0:T(8,128)(2,1)}, u32[]{:S(2)}, u32[]{:S(2)}) %collective-permute-start.4) | collective-permute-done | bytes 1982496 | tf_op jit(solution)/shard_map/ppermute | solution.py:46
  61.3 2.2 %slice.36 = bf16[2,176,1408]{2,1,0:T(8,128)(2,1)} slice(bf16[4,176,1408]{2,1,0:T(8,128)(2,1)} %collective-permute-done.4.rest_2_), slice={[2:4], [0:176], [0:1408]} | slice | bytes 1982464 | tf_op jit(solution)/shard_map/slice | solution.py:174
  63.6 5.4 %collective-permute-start.6 = (bf16[2,176,1408]{2,1,0:T(8,128)(2,1)}, bf16[2,176,1408]{2,1,0:T(8,128)(2,1)S(1)}, u32[]{:S(2)}, u32[]{:S(2)}) collective-permute-start(bf16[2,176,1408]{2,1,0:T(8,128)(2,1)} %slice.36), channel_id=1, source_target_pairs={{0,268},{16,19},{32,300},{48,51},{64,332},{80,83},{96,364},{112,11... | collective-permute-start | bytes 2973704 | tf_op jit(solution)/shard_map/ppermute | solution.py:46
  69.1 2.3 %slice.35 = bf16[2,176,1408]{2,1,0:T(8,128)(2,1)} slice(bf16[4,176,1408]{2,1,0:T(8,128)(2,1)} %collective-permute-done.3.rest_1_), slice={[0:2], [0:176], [0:1408]} | slice | bytes 1982464 | tf_op jit(solution)/shard_map/slice | solution.py:173
  71.4 1.9 %collective-permute-start.5 = (bf16[2,176,1408]{2,1,0:T(8,128)(2,1)}, bf16[2,176,1408]{2,1,0:T(8,128)(2,1)S(1)}, u32[]{:S(2)}, u32[]{:S(2)}) collective-permute-start(bf16[2,176,1408]{2,1,0:T(8,128)(2,1)} %slice.35), channel_id=1, source_target_pairs={{0,4},{16,17},{32,36},{48,49},{64,68},{80,81},{96,100},{112,113},{... | collective-permute-start | bytes 2973704 | tf_op jit(solution)/shard_map/ppermute | solution.py:46
  73.3 8.9 %collective-permute-start.9 = (bf16[4,176,1408]{2,1,0:T(8,128)(2,1)}, bf16[4,176,1408]{2,1,0:T(8,128)(2,1)}, u32[]{:S(2)}, u32[]{:S(2)}) collective-permute-start(bf16[4,176,1408]{2,1,0:T(8,128)(2,1)} %collective-permute-done.4.rest_2_), channel_id=1, source_target_pairs={{0,16},{16,0},{32,48},{48,32},{64,80},{80,64},{96,112},{112,96},{1... | collective-permute-start | bytes 5947400 | tf_op jit(solution)/shard_map/ppermute | solution.py:46
  82.2 1.9 %collective-permute-start.8 = (bf16[4,176,1408]{2,1,0:T(8,128)(2,1)}, bf16[4,176,1408]{2,1,0:T(8,128)(2,1)}, u32[]{:S(2)}, u32[]{:S(2)}) collective-permute-start(bf16[4,176,1408]{2,1,0:T(8,128)(2,1)} %collective-permute-done.3.rest_1_), channel_id=1, source_target_pairs={{0,16},{16,0},{32,48},{48,32},{64,80},{80,64},{96,112},{112,96},{1... | collective-permute-start | bytes 5947400 | tf_op jit(solution)/shard_map/ppermute | solution.py:46
  84.3 0.2 reshape.75
  84.6 0.3 copy.29
  84.9 0.4 transpose.54
  85.3 1.3 pad.19
  86.6 2.9 %copy.27 = f32[2816,128]{0,1:T(8,128)} copy(f32[2816,128]{1,0:T(8,128)} %bitcast.37) | data formatting | bytes 2883584 | tf_op jit(solution)/shard_map/reshape | solution.py:157
  89.5 2.6 %reshape.73 = f32[16,165,128]{2,1,0:T(8,128)} reshape(f32[2640,128]{1,0:T(8,128)} %bitcast.44) | data formatting | bytes 2703360 | tf_op jit(solution)/shard_map/reshape | solution.py:156
  92.1 2.5 %pad.20 = f32[16,176,128]{2,1,0:T(8,128)} pad(f32[16,165,128]{2,1,0:T(8,128)} %reshape.73, f32[]{:T(128)} %constant.50.clone.1), padding=0_0x0_11x0_0 | pad | bytes 2793476 | tf_op jit(solution)/shard_map/jit(_pad)/pad | solution.py:157
  94.6 3.0 %copy.28 = f32[2816,128]{0,1:T(8,128)} copy(f32[2816,128]{1,0:T(8,128)} %bitcast.38) | data formatting | bytes 2883584 | tf_op jit(solution)/shard_map/reshape | solution.py:157
  97.6 2.9 %copy.26 = f32[2816,128]{0,1:T(8,128)} copy(f32[2816,128]{1,0:T(8,128)} %bitcast.35) | data formatting | bytes 2883584 | tf_op jit(solution)/shard_map/reshape | solution.py:157
  100.5 1.0 fusion
  101.5 1.4 bitcast_convert_fusion.cb_ref
  103.0 2.4 %collective-permute-start.11 = (bf16[2,176,1408]{2,1,0:T(8,128)(2,1)S(1)}, bf16[2,176,1408]{2,1,0:T(8,128)(2,1)S(1)}, u32[]{:S(2)}, u32[]{:S(2)}) collective-permute-start(bf16[2,176,1408]{2,1,0:T(8,128)(2,1)S(1)} %collective-permute-done.6.rest_4_), channel_id=1, source_target_pairs={{0,16},{16,0},{32,48},{48,32},{64,80},{80,64},{96,112},{112,96},{1... | collective-permute-start | bytes 2973704 | tf_op jit(solution)/shard_map/ppermute | solution.py:46
  105.4 1.9 %collective-permute-start.10 = (bf16[2,176,1408]{2,1,0:T(8,128)(2,1)S(1)}, bf16[2,176,1408]{2,1,0:T(8,128)(2,1)S(1)}, u32[]{:S(2)}, u32[]{:S(2)}) collective-permute-start(bf16[2,176,1408]{2,1,0:T(8,128)(2,1)S(1)} %collective-permute-done.5.rest_3_), channel_id=1, source_target_pairs={{0,16},{16,0},{32,48},{48,32},{64,80},{80,64},{96,112},{112,96},{1... | collective-permute-start | bytes 2973704 | tf_op jit(solution)/shard_map/ppermute | solution.py:46
  107.4 1.3 multiply_convert_fusion
  108.7 1.2 collective-permute-done.10.rest_8_
  109.9 0.9 copy-done.8
  110.9 1.2 copy-done.1
  112.1 25.7 %shard_map.85 = (bf16[128,2816]{1,0:T(8,128)(2,1)S(1)}, bf16[128,2816]{1,0:T(8,128)(2,1)S(1)}, f32[1,2816]{1,0:T(1,128)S(1)}) custom-call(s32[4]{0:T(128)S(1)} %pad_add_fusion.place, bf16[128,2816]{1,0:T(8,128)(2,1)S(1)} %get-tuple-element.9.op0_ref, bf16[128,2816]{1,0:T(8,128)(2,1)S(1)} %bitcast_convert_fusion.cb_ref, ...), custom_call_target="tpu_custom_call" | custom-call | flops 8120172544 | bytes 15859712 | tf_op jit(solution)/shard_map/pallas_call | solution.py:133
  137.9 17.5 %all_to_all.12 = f32[16,1,2816]{2,1,0:T(1,128)S(1)} all-to-all(f32[16,1,2816]{2,1,0:T(1,128)S(1)} %broadcast_in_dim.4), channel_id=1, replica_groups={{0,16,32,48,64,80,96,112,128,144,160,176,192,208,224,240},{256,272,288,..., dimensions={0} | all-to-all | bytes 360448 | tf_op jit(solution)/shard_map/all_to_all | solution.py:181
  155.6 0.9 broadcast_in_dim.5
  156.5 5.5 %all-to-all-start.1 = ((f32[32,1,2816]{2,1,0:T(1,128)}), f32[32,1,2816]{2,1,0:T(1,128)}, u32[]{:S(2)}, u32[]{:S(2)}) async-start(f32[32,1,2816]{2,1,0:T(1,128)} %broadcast_in_dim.5), calls=%async_computation.1 | async-start | bytes 720896 | tf_op jit(solution)/shard_map/all_to_all | solution.py:184
  162.1 0.4 copy.30
  162.5 1.1 reshape.80
  163.5 0.4 copy.31
  163.9 1.1 reshape.82
  165.0 11.2 %all-to-all-done.1 = f32[32,1,2816]{2,1,0:T(1,128)} async-done(((f32[32,1,2816]{2,1,0:T(1,128)}), f32[32,1,2816]{2,1,0:T(1,128)}, u32[]{:S(2)}, u32[]{:S(2)}) %all-to-all-start.1) | async-done | bytes 360480 | tf_op jit(solution)/shard_map/all_to_all | solution.py:184
  176.2 1.2 reduce_sum.29
  177.5 0.7 reshape_transpose_reshape.3
  (38 shorter events, 1.0 us)
Async XLA Ops:
  10.3 12.2 %collective-permute-start = (bf16[176,1408]{1,0:T(8,128)(2,1)S(1)}, bf16[176,1408]{1,0:T(8,128)(2,1)S(1)}, u32[]{:S(2)}, u32[]{:S(2)}) collective-permute-start(bf16[176,1408]{1,0:T(8,128)(2,1)S(1)} %slice_select_fusion), channel_id=1, source_target_pairs={{0,1},{16,20},{32,33},{48,52},{64,65},{80,84},{96,97},{112,116},{1... | collective-permute-start | bytes 1486856 | tf_op jit(solution)/shard_map/ppermute | solution.py:46
  14.4 10.1 %collective-permute-start.2 = (bf16[176,1408]{1,0:T(8,128)(2,1)S(1)}, bf16[176,1408]{1,0:T(8,128)(2,1)S(1)}, u32[]{:S(2)}, u32[]{:S(2)}) collective-permute-start(bf16[176,1408]{1,0:T(8,128)(2,1)S(1)} %slice_select_fusion), channel_id=1, source_target_pairs={{0,3},{16,284},{32,35},{48,316},{64,67},{80,348},{96,99},{112,380}... | collective-permute-start | bytes 1486856 | tf_op jit(solution)/shard_map/ppermute | solution.py:46
  22.5 10.8 %collective-permute-start.1 = (bf16[176,1408]{1,0:T(8,128)(2,1)S(1)}, bf16[176,1408]{1,0:T(8,128)(2,1)S(1)}, u32[]{:S(2)}, u32[]{:S(2)}) collective-permute-start(bf16[176,1408]{1,0:T(8,128)(2,1)S(1)} %collective-permute-done), channel_id=1, source_target_pairs={{0,1},{16,20},{32,33},{48,52},{64,65},{80,84},{96,97},{112,116},{1... | collective-permute-start | bytes 1486856 | tf_op jit(solution)/shard_map/ppermute | solution.py:46
  33.3 8.6 %copy-start.4 = (f32[128,2640]{0,1:T(8,128)S(1)}, f32[128,2640]{0,1:T(8,128)}, u32[]{:S(2)}) copy-start(f32[128,2640]{0,1:T(8,128)} %param.6) | copy-start | bytes 4055044
  34.9 26.4 %collective-permute-start.4 = (bf16[4,176,1408]{2,1,0:T(8,128)(2,1)}, bf16[4,176,1408]{2,1,0:T(8,128)(2,1)}, u32[]{:S(2)}, u32[]{:S(2)}) collective-permute-start(bf16[4,176,1408]{2,1,0:T(8,128)(2,1)} %pad_maximum_fusion.rest_0_), channel_id=1, source_target_pairs={{0,268},{16,19},{32,300},{48,51},{64,332},{80,83},{96,364},{112,11... | collective-permute-start | bytes 5947400 | tf_op jit(solution)/shard_map/ppermute | solution.py:46
  39.3 29.8 %collective-permute-start.3 = (bf16[4,176,1408]{2,1,0:T(8,128)(2,1)}, bf16[4,176,1408]{2,1,0:T(8,128)(2,1)}, u32[]{:S(2)}, u32[]{:S(2)}) collective-permute-start(bf16[4,176,1408]{2,1,0:T(8,128)(2,1)} %pad_maximum_fusion.rest_0_), channel_id=1, source_target_pairs={{0,4},{16,17},{32,36},{48,49},{64,68},{80,81},{96,100},{112,113},{... | collective-permute-start | bytes 5947400 | tf_op jit(solution)/shard_map/ppermute | solution.py:46
  42.1 21.5 %copy-start.2 = (f32[16,176,128]{2,1,0:T(8,128)}, f32[16,176,128]{2,1,0:T(8,128)S(1)}, u32[]{:S(2)}) copy-start(f32[16,176,128]{2,1,0:T(8,128)S(1)} %pad.18) | copy-start | bytes 4325380
  42.5 66.2 %collective-permute-start.7 = (bf16[4,176,1408]{2,1,0:T(8,128)(2,1)}, bf16[4,176,1408]{2,1,0:T(8,128)(2,1)}, u32[]{:S(2)}, u32[]{:S(2)}) collective-permute-start(bf16[4,176,1408]{2,1,0:T(8,128)(2,1)} %pad_maximum_fusion.rest_0_), channel_id=1, source_target_pairs={{0,16},{16,0},{32,48},{48,32},{64,80},{80,64},{96,112},{112,96},{1... | collective-permute-start | bytes 5947400 | tf_op jit(solution)/shard_map/ppermute | solution.py:46
  63.6 20.6 %copy-start.6 = (f32[2640]{0:T(1024)S(1)}, f32[2640]{0:T(1024)}, u32[]{:S(2)}) copy-start(f32[2640]{0:T(1024)} %param.9) | copy-start | bytes 31684
  63.6 20.7 %copy-start.5 = (bf16[128,2640]{0,1:T(8,128)(2,1)S(1)}, bf16[128,2640]{0,1:T(8,128)(2,1)}, u32[]{:S(2)}) copy-start(bf16[128,2640]{0,1:T(8,128)(2,1)} %param.7) | copy-start | bytes 2027524
  63.6 39.4 %collective-permute-start.6 = (bf16[2,176,1408]{2,1,0:T(8,128)(2,1)}, bf16[2,176,1408]{2,1,0:T(8,128)(2,1)S(1)}, u32[]{:S(2)}, u32[]{:S(2)}) collective-permute-start(bf16[2,176,1408]{2,1,0:T(8,128)(2,1)} %slice.36), channel_id=1, source_target_pairs={{0,268},{16,19},{32,300},{48,51},{64,332},{80,83},{96,364},{112,11... | collective-permute-start | bytes 2973704 | tf_op jit(solution)/shard_map/ppermute | solution.py:46
  71.4 34.0 %collective-permute-start.5 = (bf16[2,176,1408]{2,1,0:T(8,128)(2,1)}, bf16[2,176,1408]{2,1,0:T(8,128)(2,1)S(1)}, u32[]{:S(2)}, u32[]{:S(2)}) collective-permute-start(bf16[2,176,1408]{2,1,0:T(8,128)(2,1)} %slice.35), channel_id=1, source_target_pairs={{0,4},{16,17},{32,36},{48,49},{64,68},{80,81},{96,100},{112,113},{... | collective-permute-start | bytes 2973704 | tf_op jit(solution)/shard_map/ppermute | solution.py:46
  73.3 35.4 %collective-permute-start.9 = (bf16[4,176,1408]{2,1,0:T(8,128)(2,1)}, bf16[4,176,1408]{2,1,0:T(8,128)(2,1)}, u32[]{:S(2)}, u32[]{:S(2)}) collective-permute-start(bf16[4,176,1408]{2,1,0:T(8,128)(2,1)} %collective-permute-done.4.rest_2_), channel_id=1, source_target_pairs={{0,16},{16,0},{32,48},{48,32},{64,80},{80,64},{96,112},{112,96},{1... | collective-permute-start | bytes 5947400 | tf_op jit(solution)/shard_map/ppermute | solution.py:46
  82.2 27.7 %collective-permute-start.8 = (bf16[4,176,1408]{2,1,0:T(8,128)(2,1)}, bf16[4,176,1408]{2,1,0:T(8,128)(2,1)}, u32[]{:S(2)}, u32[]{:S(2)}) collective-permute-start(bf16[4,176,1408]{2,1,0:T(8,128)(2,1)} %collective-permute-done.3.rest_1_), channel_id=1, source_target_pairs={{0,16},{16,0},{32,48},{48,32},{64,80},{80,64},{96,112},{112,96},{1... | collective-permute-start | bytes 5947400 | tf_op jit(solution)/shard_map/ppermute | solution.py:46
  100.5 6.9 %copy-start.3 = (f32[2816,128]{0,1:T(8,128)S(1)}, f32[2816,128]{0,1:T(8,128)}, u32[]{:S(2)}) copy-start(f32[2816,128]{0,1:T(8,128)} %copy.26) | copy-start | bytes 4325380
  103.0 5.7 %collective-permute-start.11 = (bf16[2,176,1408]{2,1,0:T(8,128)(2,1)S(1)}, bf16[2,176,1408]{2,1,0:T(8,128)(2,1)S(1)}, u32[]{:S(2)}, u32[]{:S(2)}) collective-permute-start(bf16[2,176,1408]{2,1,0:T(8,128)(2,1)S(1)} %collective-permute-done.6.rest_4_), channel_id=1, source_target_pairs={{0,16},{16,0},{32,48},{48,32},{64,80},{80,64},{96,112},{112,96},{1... | collective-permute-start | bytes 2973704 | tf_op jit(solution)/shard_map/ppermute | solution.py:46
  105.4 3.3 %copy-start = (bf16[2,176,1408]{2,1,0:T(8,128)(2,1)}, bf16[2,176,1408]{2,1,0:T(8,128)(2,1)S(1)}, u32[]{:S(2)}) copy-start(bf16[2,176,1408]{2,1,0:T(8,128)(2,1)S(1)} %collective-permute-done.5.rest_3_) | copy-start | bytes 2973700
  105.4 4.5 %collective-permute-start.10 = (bf16[2,176,1408]{2,1,0:T(8,128)(2,1)S(1)}, bf16[2,176,1408]{2,1,0:T(8,128)(2,1)S(1)}, u32[]{:S(2)}, u32[]{:S(2)}) collective-permute-start(bf16[2,176,1408]{2,1,0:T(8,128)(2,1)S(1)} %collective-permute-done.5.rest_3_), channel_id=1, source_target_pairs={{0,16},{16,0},{32,48},{48,32},{64,80},{80,64},{96,112},{112,96},{1... | collective-permute-start | bytes 2973704 | tf_op jit(solution)/shard_map/ppermute | solution.py:46
  108.7 1.2 copy-start.7
  109.9 1.0 copy-start.8
  110.9 1.2 copy-start.1
  156.5 19.7 %all-to-all-start.1 = ((f32[32,1,2816]{2,1,0:T(1,128)}), f32[32,1,2816]{2,1,0:T(1,128)}, u32[]{:S(2)}, u32[]{:S(2)}) async-start(f32[32,1,2816]{2,1,0:T(1,128)} %broadcast_in_dim.5), calls=%async_computation.1 | async-start | bytes 720896 | tf_op jit(solution)/shard_map/all_to_all | solution.py:184

commit v2 on v1

--- a/solution.py
+++ b/solution.py
@@ -50,30 +50,106 @@
     return lax.dot_general(a, b, (((1,), (1,)), ((), ())), preferred_element_type=F32)
 
 
+def spread_kernel(place, w_ref, out_ref, wide_ref):
+    wide_ref[...] = jnp.zeros_like(wide_ref)
+    for t in range(20):
+        wide_ref[0:SH, 128 * t : 128 * t + 128] = w_ref[:, 128 * t : 128 * t + 128].astype(F32)
+    wide_ref[0:SH, 2560:W] = w_ref[:, 2560:W].astype(F32)
+    lane = lax.broadcasted_iota(jnp.int32, (SP, 128), 1)
+    for core in range(2):
+
+        @pl.when(place[2] == core)
+        def _():
+            for t in range(HALF // 128):
+                tile = jnp.zeros((SP, 128), F32)
+                for j in range(8):
+                    low, high = SP * j - 128 * t, SP * j + SH - 128 * t
+                    if high <= 0 or low >= 128:
+                        continue
+                    q = SH * (8 * core + j) - low
+                    base = (q // 128) * 128
+                    win = wide_ref[:, base : base + 256]
+                    moved = pltpu.roll(win, (base - q) % 256, 1)[:, :128]
+                    tile = jnp.where((lane >= low) & (lane < high), moved, tile)
+                out_ref[:, 128 * t : 128 * t + 128] = tile.astype(BF)
+
+def spread(place, w):
+    vm = pl.BlockSpec(memory_space=pltpu.VMEM)
+    return pl.pallas_call(
+        spread_kernel,
+        out_shape=jax.ShapeDtypeStruct((SP, HALF), BF),
+        in_specs=[pl.BlockSpec(memory_space=pltpu.SMEM), vm],
+        out_specs=vm,
+        scratch_shapes=[pltpu.VMEM((SP, 2944), F32)],
+        compiler_params=pltpu.CompilerParams(vmem_limit_bytes=16 * 2**20),
+    )(place, w)
+
+def prepare_kernel(state_ref, inj_ref, cot_ref, gain_ref, n0_ref, op0_ref, injw_ref, cotw_ref, cb_ref, wide_ref, tall_ref):
+    def regroup(src_ref):
+        for s in range(16):
+            wide_ref[SP * s : SP * s + SH, :] = src_ref[SH * s : SH * s + SH, :]
+
+    for s in range(16):
+        wide_ref[SP * s + SH : SP * s + SP, :] = jnp.zeros((SP - SH, TOK), F32)
+    regroup(state_ref)
+    acc = jnp.zeros((TOK, 128), F32)
+    for t in range(WP // 128):
+        cols = slice(128 * t, 128 * t + 128)
+        s = wide_ref[cols, :].T
+        n0_ref[:, cols] = s
+        acc = acc + s * s
+    inv = lax.rsqrt(jnp.sum(acc, axis=1, keepdims=True) / W + EPS)
+    for t in range(WP // 128):
+        cols = slice(128 * t, 128 * t + 128)
+        n0 = n0_ref[:, cols] * inv
+        n0_ref[:, cols] = n0
+        op0_ref[:, cols] = (n0 * gain_ref[:, cols]).astype(BF)
+    regroup(cot_ref)
+    for t in range(WP // 128):
+        cols = slice(128 * t, 128 * t + 128)
+        c = wide_ref[cols, :].T
+        cotw_ref[:, cols] = c
+        cb_ref[:, cols] = c.astype(BF)
+    tall_ref[...] = inj_ref[...].astype(F32)
+    regroup(tall_ref)
+    for t in range(WP // 128):
+        cols = slice(128 * t, 128 * t + 128)
+        injw_ref[:, cols] = wide_ref[cols, :].T.astype(BF)
+
+def prepare(state, inj, cot, gain):
+    vm = pl.BlockSpec(memory_space=pltpu.VMEM)
+    wide = lambda dt: jax.ShapeDtypeStruct((TOK, WP), dt)
+    return pl.pallas_call(
+        prepare_kernel,
+        out_shape=(wide(F32), wide(BF), wide(BF), wide(F32), wide(BF)),
+        in_specs=[vm] * 4,
+        out_specs=(vm,) * 5,
+        scratch_shapes=[pltpu.VMEM((WP, TOK), F32), pltpu.VMEM((W, TOK), F32)],
+        compiler_params=pltpu.CompilerParams(vmem_limit_bytes=24 * 2**20),
+        cost_estimate=pl.CostEstimate(flops=10**6, bytes_accessed=10**7, transcendentals=0),
+    )(state.T, inj.T, cot.T, gain)
+
+
+SINGLE = 2
+SLOT = (0, 1, None, 2)
+
+
 def core_kernel(place, op0_ref, cb_ref, n0_ref, inj_ref, cot_ref, gain_ref, *rest):
-    pieces = rest[:10]
-    final_ref, injg_ref, part_ref = rest[10:13]
-    w_ref, s1_ref, back_ref, op1_ref, db_ref, sems = rest[13:]
+    pieces = rest[:16]
+    final_ref, injg_ref, part_ref = rest[16:19]
+    w_ref, s1_ref, back_ref, op1_ref, db_ref, sems = rest[19:]
     px, py, pc, rounds = place[0], place[1], place[2], place[3]
     copies = []
     for who in range(2):
         core = pc if who == 0 else 1 - pc
-        base = 5 * who
         for k in range(4):
             for j in range(4):
                 sx = jnp.where(core == 0, px + 4 - j, px + 4 - k) % 4
                 sy = jnp.where(core == 0, py + 4 - k, py + 4 - j) % 4
                 row = pl.multiple_of((sy * 4 + sx) * SP, SP)
-                if k == 0:
-                    src = pieces[base].at[j]
-                elif k == 1:
-                    src = pieces[base + 1].at[j]
-                elif k == 3:
-                    src = pieces[base + 2].at[j]
-                elif j < 2:
-                    src = pieces[base + 3].at[j]
-                else:
-                    src = pieces[base + 4].at[j - 2]
+                src = pieces[8 * who + 2 * k + (j == SINGLE)]
+                if j != SINGLE:
+                    src = src.at[SLOT[j]]
                 dst = w_ref.at[pl.ds(row, SP), pl.ds(pl.multiple_of(core * HALF, 128), HALF)]
                 copies.append(pltpu.make_async_copy(src, dst, sems.at[len(copies)]))
     for c in copies:
@@ -83,13 +159,13 @@
     deep = rounds >= 2
 
     def first(t, ssq):
-        cols = pl.ds(pl.multiple_of(t * TILE, TILE), TILE)
+        cols = pl.ds(pl.multiple_of(t * HALF, 128), HALF)
+        back_ref[:, cols] = nt(cb_ref[...], w_ref[cols, :])
         s1 = jnp.dot(op0_ref[...], w_ref[:, cols], preferred_element_type=F32) + inj_ref[:, cols].astype(F32)
         s1_ref[:, cols] = s1
-        back_ref[:, cols] = nt(cb_ref[...], w_ref[cols, :])
         return ssq + jnp.sum(s1 * s1, axis=1, keepdims=True)
 
-    ssq = lax.fori_loop(0, WP // TILE, first, jnp.zeros((TOK, 1), F32))
+    ssq = lax.fori_loop(0, 2, first, jnp.zeros((TOK, 1), F32))
     inv1 = lax.rsqrt(ssq / W + EPS)
 
     def second(t, dots):
@@ -117,7 +193,7 @@
     lax.fori_loop(0, WP // TILE, third, 0)
 
     def fourth(t, carry):
-        cols = pl.ds(pl.multiple_of(t * TILE, TILE), TILE)
+        cols = pl.ds(pl.multiple_of(t * HALF, 128), HALF)
         s2 = jnp.dot(op1_ref[...], w_ref[:, cols], preferred_element_type=F32) + inj_ref[:, cols].astype(F32)
         final_ref[:, cols] = jnp.where(deep, s2, s1_ref[:, cols]).astype(BF)
         back = nt(db_ref[...], w_ref[cols, :])
@@ -125,7 +201,7 @@
         part_ref[:, cols] += jnp.where(deep, part2, jnp.zeros_like(part2))
         return carry
 
-    lax.fori_loop(0, WP // TILE, fourth, 0)
+    lax.fori_loop(0, 2, fourth, 0)
 
 
 def core_call(place, op0, cb, n0, inj, cot, gain, pieces):
@@ -137,7 +213,7 @@
             jax.ShapeDtypeStruct((TOK, WP), BF),
             jax.ShapeDtypeStruct((1, WP), F32),
         ),
-        in_specs=[pl.BlockSpec(memory_space=pltpu.SMEM)] + [vm] * 6 + [pl.BlockSpec(memory_space=pl.ANY)] * 10,
+        in_specs=[pl.BlockSpec(memory_space=pltpu.SMEM)] + [vm] * 6 + [pl.BlockSpec(memory_space=pl.ANY)] * 16,
         out_specs=(vm, vm, vm),
         scratch_shapes=[
             pltpu.VMEM((WP, WP), BF),
@@ -152,28 +228,29 @@
     )(place, op0, cb, n0, inj, cot, gain, *pieces)
 
 
-def widen(array):
-    flipped = array.T.reshape(16, SH, TOK)
-    return jnp.pad(flipped, ((0, 0), (0, SP - SH), (0, 0))).reshape(WP, TOK).T
-
-
 def narrow(array):
     return array.T.reshape(16, SP, -1)[:, :SH].reshape(W, -1).T
 
 
-def gather(weight, pc):
-    wide = jnp.pad(weight.reshape(SH, 16, SH), ((0, SP - SH), (0, 0), (0, SP - SH))).reshape(SP, WP)
-    own = jnp.where(pc == 0, wide[:, :HALF], wide[:, HALF:])
+def gather(own, acts):
     m1 = send(own, along(True, 1))
     m3 = send(own, along(True, -1))
-    m2 = send(m1, along(True, 1))
-    row = jnp.stack([own, m1, m2, m3])
-    n1 = send(row, along(False, 1))
-    n3 = send(row, along(False, -1))
-    n2a = send(n1[:2], along(False, 1))
-    n2b = send(n3[2:], along(False, -1))
-    mine = (row, n1, n3, n2a, n2b)
-    return mine + tuple(send(a, SWAP) for a in mine)
+    m2 = send(own, along(True, 2))
+    three = jnp.stack([own, m1, m3])
+    three1 = send(three, along(False, 1))
+    three3 = send(three, along(False, -1))
+    three1, three3, m2 = lax.optimization_barrier((three1, three3, m2))
+    three2 = send(three1, along(False, 1))
+    one3 = send(m2, along(False, -1))
+    one1 = send(m2, along(False, 1))
+    own4 = lax.optimization_barrier((three, m2, three1, three3, one3))
+    one2 = send(own4[4], along(False, -1))
+    early = tuple(send(a, SWAP) for a in own4)
+    acts, early, (three2, one1, one2) = lax.optimization_barrier((acts, early, (three2, one1, one2)))
+    late = tuple(send(a, SWAP) for a in (three2, one1, one2))
+    mine = (three, m2, three1, one1, three2, one2, three3, one3)
+    theirs = (early[0], early[1], early[2], late[1], late[0], late[2], early[3], early[4])
+    return acts, mine + theirs
 
 
 def total(part):
@@ -189,14 +266,10 @@
     dp, fs = lax.axis_index("dp"), lax.axis_index("fsdp")
     pc = dp % 2
     place = jnp.stack([fs % 4, fs // 4, pc, counts[0]]).astype(jnp.int32)
-    pieces = gather(core_weight, pc)
-    gain_w = widen(jnp.broadcast_to(gain, (TOK, W)))[:1]
-    start = widen(state0)
-    inv = lax.rsqrt(jnp.sum(start * start, axis=-1, keepdims=True) / W + EPS)
-    n0 = start * inv
-    op0 = (n0 * gain_w).astype(BF)
-    cot = widen(cotangent)
-    final, injg, part = core_call(place, op0, cot.astype(BF), n0, widen(injected), cot, gain_w, pieces)
+    gain_w = jnp.pad(gain.reshape(16, SH), ((0, 0), (0, SP - SH))).reshape(1, WP)
+    acts = prepare(state0, injected, cotangent, gain_w)
+    (n0, op0, inj, cot, cb), pieces = gather(spread(place, core_weight), acts)
+    final, injg, part = core_call(place, op0, cb, n0, inj, cot, gain_w, pieces)
     return (narrow(final), narrow(injg), narrow(total(part)).reshape(W))
 
 

time: 179 us -> 177 us (0.989)
  local copies, waits for them, and re-layouts: 38.5 us -> 12.9 us
  waiting for transfers between devices: 35.1 us -> 55.2 us
  other arithmetic: 6.27 us -> 1.77 us
  starting transfers between devices: 53.4 us -> 57.1 us
  blocking collectives: 17.5 us -> 20.3 us
    ppermute x12 -> x17, waiting for transfers between devices: 23.9 us -> 44 us  [send(): return lax.ppermute(array, AXES, pairs)]
    reshape x9 -> x2, local copies, waits for them, and re-layouts: 20 us -> 0.19 us  [the longest x1 0.1 us: shards(): gain.reshape(16, SH)]
    unnamed x18 -> x32, local copies, waits for them, and re-layouts: 2.18 us -> 7.97 us
    slice x3 -> x0, local copies, waits for them, and re-layouts: 5.59 us -> none  [the longest x1 2.3 us: gather(): n2a = send(n1[:2], along(False, 1))]
    pad x5 -> x1, local copies, waits for them, and re-layouts: 5.55 us -> 0.01 us  [shards(): jnp.pad(gain.reshape(16, SH), ((0, 0), (0, SP - SH))).reshape(1, WP)]
    ppermute x12 -> x17, starting transfers between devices: 47.8 us -> 51.9 us  [send(): return lax.ppermute(array, AXES, pairs)]
    convert_element_type x2 -> x0, other arithmetic: 2.74 us -> none  [the longest x1 1.44 us: shards(): cot.astype(BF)]
    all_to_all x1, blocking collectives: 17.5 us -> 20.3 us  [total(): lax.all_to_all(jnp.broadcast_to(part, (16, WP)), 'dp', 0, 0, axis_index_g...]
  transfers between devices with their start and end apart: 13 -> 18, of which waited for: 5 -> 8; matrix products, arithmetic and copies ran while one was open for 16% -> 2% of each run, Pallas kernels for 0% -> 1%
where the time goes in v2:
time: 177 us; the launch traced here: 176 us
  starting transfers between devices  57.1 us (32%)
  waiting for transfers between devices  55.2 us (31%)
  Pallas kernels  27.2 us (15%)
  blocking collectives  20.3 us (11%)
  local copies, waits for them, and re-layouts  12.9 us (7%)
  other arithmetic  1.77 us (1%)
    ppermute x17, starting transfers between devices, send(): return lax.ppermute(array, AXES, pairs)  51.9 us
    ppermute x17, waiting for transfers between devices, send(): return lax.ppermute(array, AXES, pairs)  44 us
    pallas_call x1, Pallas kernels, core_call(): pl.pallas_call(core_kernel, out_shape=(jax.ShapeDtypeStruct((TOK, WP), BF...  24.6 us
    all_to_all x1, blocking collectives, total(): lax.all_to_all(jnp.broadcast_to(part, (16, WP)), 'dp', 0, 0, axis_index_g...  20.3 us
    all_to_all x1, waiting for transfers between devices, total(): lax.all_to_all(jnp.broadcast_to(part, (32, WP)), AXES, 0, 0, axis_index_g...  11.2 us
    unnamed x32, local copies, waits for them, and re-layouts  7.97 us
    all_to_all x1, starting transfers between devices, total(): lax.all_to_all(jnp.broadcast_to(part, (32, WP)), AXES, 0, 0, axis_index_g...  5.26 us
  transfers between devices with their start and end apart: 18, of which 8 were waited for; matrix products, arithmetic and copies ran while one was open for 2% of the time, Pallas kernels for 1%

profile of v2, /device:TPU:1, one launch (start us, length us, event | category | flops | bytes accessed | tf_op | source)
XLA Modules:
  0.0 176.1 jit_solution(10894750052153338047)
XLA Ops:
  1.4 1.2 copy-done.2
  2.6 1.2 shard_map.86
  3.7 5.9 %collective-permute-start.1 = (bf16[176,1408]{1,0:T(8,128)(2,1)S(1)}, bf16[176,1408]{1,0:T(8,128)(2,1)S(1)}, u32[]{:S(2)}, u32[]{:S(2)}) collective-permute-start(bf16[176,1408]{1,0:T(8,128)(2,1)S(1)} %shard_map.86), channel_id=1, source_target_pairs={{0,3},{16,284},{32,35},{48,316},{64,67},{80,348},{96,99},{112,380}... | collective-permute-start | bytes 1486856 | tf_op jit(solution)/shard_map/ppermute | solution.py:46
  9.7 1.9 %collective-permute-start = (bf16[176,1408]{1,0:T(8,128)(2,1)S(1)}, bf16[176,1408]{1,0:T(8,128)(2,1)S(1)}, u32[]{:S(2)}, u32[]{:S(2)}) collective-permute-start(bf16[176,1408]{1,0:T(8,128)(2,1)S(1)} %shard_map.86), channel_id=1, source_target_pairs={{0,1},{16,20},{32,33},{48,52},{64,65},{80,84},{96,97},{112,116},{1... | collective-permute-start | bytes 1486856 | tf_op jit(solution)/shard_map/ppermute | solution.py:46
  11.6 3.9 %collective-permute-done.1 = bf16[176,1408]{1,0:T(8,128)(2,1)S(1)} collective-permute-done((bf16[176,1408]{1,0:T(8,128)(2,1)S(1)}, bf16[176,1408]{1,0:T(8,128)(2,1)S(1)}, u32[]{:S(2)}, u32[]{:S(2)}) %collective-permute-start.1) | collective-permute-done | bytes 495648 | tf_op jit(solution)/shard_map/ppermute | solution.py:46
  15.5 5.3 %collective-permute-done = bf16[176,1408]{1,0:T(8,128)(2,1)S(1)} collective-permute-done((bf16[176,1408]{1,0:T(8,128)(2,1)S(1)}, bf16[176,1408]{1,0:T(8,128)(2,1)S(1)}, u32[]{:S(2)}, u32[]{:S(2)}) %collective-permute-start) | collective-permute-done | bytes 495648 | tf_op jit(solution)/shard_map/ppermute | solution.py:46
  20.8 1.3 pad_maximum_fusion.rest_0_
  22.1 4.2 %collective-permute-start.3 = (bf16[3,176,1408]{2,1,0:T(8,128)(2,1)}, bf16[3,176,1408]{2,1,0:T(8,128)(2,1)}, u32[]{:S(2)}, u32[]{:S(2)}) collective-permute-start(bf16[3,176,1408]{2,1,0:T(8,128)(2,1)} %pad_maximum_fusion.rest_0_), channel_id=1, source_target_pairs={{0,268},{16,19},{32,300},{48,51},{64,332},{80,83},{96,364},{112,11... | collective-permute-start | bytes 4460552 | tf_op jit(solution)/shard_map/ppermute | solution.py:46
  26.3 1.9 %collective-permute-start.2 = (bf16[3,176,1408]{2,1,0:T(8,128)(2,1)}, bf16[3,176,1408]{2,1,0:T(8,128)(2,1)}, u32[]{:S(2)}, u32[]{:S(2)}) collective-permute-start(bf16[3,176,1408]{2,1,0:T(8,128)(2,1)} %pad_maximum_fusion.rest_0_), channel_id=1, source_target_pairs={{0,4},{16,17},{32,36},{48,49},{64,68},{80,81},{96,100},{112,113},{... | collective-permute-start | bytes 4460552 | tf_op jit(solution)/shard_map/ppermute | solution.py:46
  28.3 1.9 %collective-permute-start.4 = (bf16[176,1408]{1,0:T(8,128)(2,1)S(1)}, bf16[176,1408]{1,0:T(8,128)(2,1)S(1)}, u32[]{:S(2)}, u32[]{:S(2)}) collective-permute-start(bf16[176,1408]{1,0:T(8,128)(2,1)S(1)} %shard_map.86), channel_id=1, source_target_pairs={{0,2},{16,24},{32,34},{48,56},{64,66},{80,88},{96,98},{112,120},{1... | collective-permute-start | bytes 1486856 | tf_op jit(solution)/shard_map/ppermute | solution.py:46
  30.2 19.5 %collective-permute-done.4.rest_1_ = bf16[176,1408]{1,0:T(8,128)(2,1)S(1)} collective-permute-done((bf16[176,1408]{1,0:T(8,128)(2,1)S(1)}, bf16[176,1408]{1,0:T(8,128)(2,1)S(1)}, u32[]{:S(2)}, u32[]{:S(2)}) %collective-permute-start.4) | collective-permute-done | bytes 495648 | tf_op jit(solution)/shard_map/ppermute | solution.py:46
  49.7 4.0 %collective-permute-done.2.rest_2_ = bf16[3,176,1408]{2,1,0:T(8,128)(2,1)} collective-permute-done((bf16[3,176,1408]{2,1,0:T(8,128)(2,1)}, bf16[3,176,1408]{2,1,0:T(8,128)(2,1)}, u32[]{:S(2)}, u32[]{:S(2)}) %collective-permute-start.2) | collective-permute-done | bytes 1486880 | tf_op jit(solution)/shard_map/ppermute | solution.py:46
  53.7 1.9 %collective-permute-start.5 = (bf16[176,1408]{1,0:T(8,128)(2,1)S(1)}, bf16[176,1408]{1,0:T(8,128)(2,1)}, u32[]{:S(2)}, u32[]{:S(2)}) collective-permute-start(bf16[176,1408]{1,0:T(8,128)(2,1)S(1)} %collective-permute-done.4.rest_1_), channel_id=1, source_target_pairs={{0,268},{16,19},{32,300},{48,51},{64,332},{80,83},{96,364},{112,11... | collective-permute-start | bytes 1486856 | tf_op jit(solution)/shard_map/ppermute | solution.py:46
  55.6 3.4 %collective-permute-start.12 = (bf16[176,1408]{1,0:T(8,128)(2,1)S(1)}, bf16[176,1408]{1,0:T(8,128)(2,1)S(1)}, u32[]{:S(2)}, u32[]{:S(2)}) collective-permute-start(bf16[176,1408]{1,0:T(8,128)(2,1)S(1)} %collective-permute-done.4.rest_1_), channel_id=1, source_target_pairs={{0,4},{16,17},{32,36},{48,49},{64,68},{80,81},{96,100},{112,113},{... | collective-permute-start | bytes 1486856 | tf_op jit(solution)/shard_map/ppermute | solution.py:46
  59.0 1.9 %collective-permute-start.11 = (bf16[3,176,1408]{2,1,0:T(8,128)(2,1)}, bf16[3,176,1408]{2,1,0:T(8,128)(2,1)}, u32[]{:S(2)}, u32[]{:S(2)}) collective-permute-start(bf16[3,176,1408]{2,1,0:T(8,128)(2,1)} %collective-permute-done.2.rest_2_), channel_id=1, source_target_pairs={{0,4},{16,17},{32,36},{48,49},{64,68},{80,81},{96,100},{112,113},{... | collective-permute-start | bytes 4460552 | tf_op jit(solution)/shard_map/ppermute | solution.py:46
  60.9 2.5 %collective-permute-done.5.rest_7_ = bf16[176,1408]{1,0:T(8,128)(2,1)} collective-permute-done((bf16[176,1408]{1,0:T(8,128)(2,1)S(1)}, bf16[176,1408]{1,0:T(8,128)(2,1)}, u32[]{:S(2)}, u32[]{:S(2)}) %collective-permute-start.5) | collective-permute-done | bytes 495648 | tf_op jit(solution)/shard_map/ppermute | solution.py:46
  63.4 9.3 %collective-permute-start.7 = (bf16[176,1408]{1,0:T(8,128)(2,1)S(1)}, bf16[176,1408]{1,0:T(8,128)(2,1)S(1)}, u32[]{:S(2)}, u32[]{:S(2)}) collective-permute-start(bf16[176,1408]{1,0:T(8,128)(2,1)S(1)} %collective-permute-done.4.rest_1_), channel_id=1, source_target_pairs={{0,16},{16,0},{32,48},{48,32},{64,80},{80,64},{96,112},{112,96},{1... | collective-permute-start | bytes 1486856 | tf_op jit(solution)/shard_map/ppermute | solution.py:46
  72.7 0.8 copy-done.8
  73.5 1.9 %collective-permute-start.6 = (bf16[3,176,1408]{2,1,0:T(8,128)(2,1)}, bf16[3,176,1408]{2,1,0:T(8,128)(2,1)}, u32[]{:S(2)}, u32[]{:S(2)}) collective-permute-start(bf16[3,176,1408]{2,1,0:T(8,128)(2,1)} %pad_maximum_fusion.rest_0_), channel_id=1, source_target_pairs={{0,16},{16,0},{32,48},{48,32},{64,80},{80,64},{96,112},{112,96},{1... | collective-permute-start | bytes 4460552 | tf_op jit(solution)/shard_map/ppermute | solution.py:46
  75.4 2.4 %collective-permute-start.8 = (bf16[3,176,1408]{2,1,0:T(8,128)(2,1)}, bf16[3,176,1408]{2,1,0:T(8,128)(2,1)}, u32[]{:S(2)}, u32[]{:S(2)}) collective-permute-start(bf16[3,176,1408]{2,1,0:T(8,128)(2,1)} %collective-permute-done.2.rest_2_), channel_id=1, source_target_pairs={{0,16},{16,0},{32,48},{48,32},{64,80},{80,64},{96,112},{112,96},{1... | collective-permute-start | bytes 4460552 | tf_op jit(solution)/shard_map/ppermute | solution.py:46
  77.9 1.9 %collective-permute-start.9 = (bf16[3,176,1408]{2,1,0:T(8,128)(2,1)}, bf16[3,176,1408]{2,1,0:T(8,128)(2,1)}, u32[]{:S(2)}, u32[]{:S(2)}) collective-permute-start(bf16[3,176,1408]{2,1,0:T(8,128)(2,1)} %collective-permute-done.3.rest_6_), channel_id=1, source_target_pairs={{0,16},{16,0},{32,48},{48,32},{64,80},{80,64},{96,112},{112,96},{1... | collective-permute-start | bytes 4460552 | tf_op jit(solution)/shard_map/ppermute | solution.py:46
  79.8 0.8 copy-done.12
  80.6 3.5 %collective-permute-start.13 = (bf16[176,1408]{1,0:T(8,128)(2,1)}, bf16[176,1408]{1,0:T(8,128)(2,1)}, u32[]{:S(2)}, u32[]{:S(2)}) collective-permute-start(bf16[176,1408]{1,0:T(8,128)(2,1)} %collective-permute-done.5.rest_7_), channel_id=1, source_target_pairs={{0,268},{16,19},{32,300},{48,51},{64,332},{80,83},{96,364},{112,11... | collective-permute-start | bytes 1486856 | tf_op jit(solution)/shard_map/ppermute | solution.py:46
  84.1 6.7 %collective-permute-done.13.rest_5_ = bf16[176,1408]{1,0:T(8,128)(2,1)} collective-permute-done((bf16[176,1408]{1,0:T(8,128)(2,1)}, bf16[176,1408]{1,0:T(8,128)(2,1)}, u32[]{:S(2)}, u32[]{:S(2)}) %collective-permute-start.13) | collective-permute-done | bytes 495648 | tf_op jit(solution)/shard_map/ppermute | solution.py:46
  90.8 3.5 %collective-permute-start.10 = (bf16[176,1408]{1,0:T(8,128)(2,1)}, bf16[176,1408]{1,0:T(8,128)(2,1)}, u32[]{:S(2)}, u32[]{:S(2)}) collective-permute-start(bf16[176,1408]{1,0:T(8,128)(2,1)} %collective-permute-done.5.rest_7_), channel_id=1, source_target_pairs={{0,16},{16,0},{32,48},{48,32},{64,80},{80,64},{96,112},{112,96},{1... | collective-permute-start | bytes 1486856 | tf_op jit(solution)/shard_map/ppermute | solution.py:46
  94.3 0.1 reshape.36
  94.6 1.4 shard_map.85
  96.1 1.2 copy-done.4
  97.3 1.1 copy-done.5
  98.4 0.9 copy-done.6
  99.3 0.9 copy-done.7
  100.2 1.9 %collective-permute-start.15 = (bf16[3,176,1408]{2,1,0:T(8,128)(2,1)}, bf16[3,176,1408]{2,1,0:T(8,128)(2,1)S(1)}, u32[]{:S(2)}, u32[]{:S(2)}) collective-permute-start(bf16[3,176,1408]{2,1,0:T(8,128)(2,1)} %collective-permute-done.11.rest_4_), channel_id=1, source_target_pairs={{0,16},{16,0},{32,48},{48,32},{64,80},{80,64},{96,112},{112,96},{1... | collective-permute-start | bytes 4460552 | tf_op jit(solution)/shard_map/ppermute | solution.py:46
  102.1 2.4 %collective-permute-start.14 = (bf16[176,1408]{1,0:T(8,128)(2,1)S(1)}, bf16[176,1408]{1,0:T(8,128)(2,1)S(1)}, u32[]{:S(2)}, u32[]{:S(2)}) collective-permute-start(bf16[176,1408]{1,0:T(8,128)(2,1)S(1)} %copy-done.11), channel_id=1, source_target_pairs={{0,16},{16,0},{32,48},{48,32},{64,80},{80,64},{96,112},{112,96},{1... | collective-permute-start | bytes 1486856 | tf_op jit(solution)/shard_map/ppermute | solution.py:46
  104.6 1.9 %collective-permute-start.16 = (bf16[176,1408]{1,0:T(8,128)(2,1)}, bf16[176,1408]{1,0:T(8,128)(2,1)S(1)}, u32[]{:S(2)}, u32[]{:S(2)}) collective-permute-start(bf16[176,1408]{1,0:T(8,128)(2,1)} %collective-permute-done.13.rest_5_), channel_id=1, source_target_pairs={{0,16},{16,0},{32,48},{48,32},{64,80},{80,64},{96,112},{112,96},{1... | collective-permute-start | bytes 1486856 | tf_op jit(solution)/shard_map/ppermute | solution.py:46
  106.5 2.0 %collective-permute-done.16.rest_13_ = bf16[176,1408]{1,0:T(8,128)(2,1)S(1)} collective-permute-done((bf16[176,1408]{1,0:T(8,128)(2,1)}, bf16[176,1408]{1,0:T(8,128)(2,1)S(1)}, u32[]{:S(2)}, u32[]{:S(2)}) %collective-permute-start.16) | collective-permute-done | bytes 495648 | tf_op jit(solution)/shard_map/ppermute | solution.py:46
  108.5 1.1 copy-done.15
  109.6 24.6 %shard_map.87 = (bf16[128,2816]{1,0:T(8,128)(2,1)S(1)}, bf16[128,2816]{1,0:T(8,128)(2,1)S(1)}, f32[1,2816]{1,0:T(1,128)S(1)}) custom-call(s32[4]{0:T(128)S(1)} %pad_add_fusion.place, bf16[128,2816]{1,0:T(8,128)(2,1)S(1)} %get-tuple-element.45.op0_ref, bf16[128,2816]{1,0:T(8,128)(2,1)} %copy-done.7, f32[128,2816]{1,0:T(8,128)} %copy-done.4, ...), custom_call_target="tpu_custom_call" | custom-call | flops 8120172544 | bytes 15859712 | tf_op jit(solution)/shard_map/pallas_call | solution.py:209
  134.4 20.3 %all_to_all.12 = f32[16,1,2816]{2,1,0:T(1,128)S(1)} all-to-all(f32[16,1,2816]{2,1,0:T(1,128)S(1)} %broadcast_in_dim.4), channel_id=1, replica_groups={{0,16,32,48,64,80,96,112,128,144,160,176,192,208,224,240},{256,272,288,..., dimensions={0} | all-to-all | bytes 360448 | tf_op jit(solution)/shard_map/all_to_all | solution.py:258
  154.6 0.1 reduce_sum.18
  154.7 0.9 broadcast_in_dim.5
  155.7 5.3 %all-to-all-start.1 = ((f32[32,1,2816]{2,1,0:T(1,128)}), f32[32,1,2816]{2,1,0:T(1,128)S(1)}, u32[]{:S(2)}, u32[]{:S(2)}) async-start(f32[32,1,2816]{2,1,0:T(1,128)} %broadcast_in_dim.5), calls=%async_computation.1 | async-start | bytes 720896 | tf_op jit(solution)/shard_map/all_to_all | solution.py:261
  160.9 0.3 copy.15
  161.4 1.1 reshape.39
  162.4 0.3 copy.16
  162.8 1.1 reshape.41
  163.9 11.2 %all-to-all-done.1 = f32[32,1,2816]{2,1,0:T(1,128)S(1)} async-done(((f32[32,1,2816]{2,1,0:T(1,128)}), f32[32,1,2816]{2,1,0:T(1,128)S(1)}, u32[]{:S(2)}, u32[]{:S(2)}) %all-to-all-start.1) | async-done | bytes 360480 | tf_op jit(solution)/shard_map/all_to_all | solution.py:261
  175.1 0.2 reduce_sum.19
  175.4 0.7 reshape_transpose_reshape.3
  (42 shorter events, 0.6 us)
Async XLA Ops:
  1.4 1.2 copy-start.2
  2.6 92.0 %copy-start.3 = (bf16[128,2640]{0,1:T(8,128)(2,1)S(1)}, bf16[128,2640]{0,1:T(8,128)(2,1)}, u32[]{:S(2)}) copy-start(bf16[128,2640]{0,1:T(8,128)(2,1)} %param.7) | copy-start | bytes 2027524
  3.7 11.7 %collective-permute-start.1 = (bf16[176,1408]{1,0:T(8,128)(2,1)S(1)}, bf16[176,1408]{1,0:T(8,128)(2,1)S(1)}, u32[]{:S(2)}, u32[]{:S(2)}) collective-permute-start(bf16[176,1408]{1,0:T(8,128)(2,1)S(1)} %shard_map.86), channel_id=1, source_target_pairs={{0,3},{16,284},{32,35},{48,316},{64,67},{80,348},{96,99},{112,380}... | collective-permute-start | bytes 1486856 | tf_op jit(solution)/shard_map/ppermute | solution.py:46
  9.7 11.1 %collective-permute-start = (bf16[176,1408]{1,0:T(8,128)(2,1)S(1)}, bf16[176,1408]{1,0:T(8,128)(2,1)S(1)}, u32[]{:S(2)}, u32[]{:S(2)}) collective-permute-start(bf16[176,1408]{1,0:T(8,128)(2,1)S(1)} %shard_map.86), channel_id=1, source_target_pairs={{0,1},{16,20},{32,33},{48,52},{64,65},{80,84},{96,97},{112,116},{1... | collective-permute-start | bytes 1486856 | tf_op jit(solution)/shard_map/ppermute | solution.py:46
  20.8 73.5 %copy-start.14 = (f32[2640]{0:T(1024)S(1)}, f32[2640]{0:T(1024)}, u32[]{:S(2)}) copy-start(f32[2640]{0:T(1024)} %param.9) | copy-start | bytes 31684
  20.8 73.8 %copy-start = (f32[128,2640]{0,1:T(8,128)S(1)}, f32[128,2640]{0,1:T(8,128)}, u32[]{:S(2)}) copy-start(f32[128,2640]{0,1:T(8,128)} %param.6) | copy-start | bytes 4055044
  20.8 73.8 %copy-start.1 = (f32[128,2640]{0,1:T(8,128)S(1)}, f32[128,2640]{0,1:T(8,128)}, u32[]{:S(2)}) copy-start(f32[128,2640]{0,1:T(8,128)} %param.11) | copy-start | bytes 4055044
  22.1 27.6 %collective-permute-start.3 = (bf16[3,176,1408]{2,1,0:T(8,128)(2,1)}, bf16[3,176,1408]{2,1,0:T(8,128)(2,1)}, u32[]{:S(2)}, u32[]{:S(2)}) collective-permute-start(bf16[3,176,1408]{2,1,0:T(8,128)(2,1)} %pad_maximum_fusion.rest_0_), channel_id=1, source_target_pairs={{0,268},{16,19},{32,300},{48,51},{64,332},{80,83},{96,364},{112,11... | collective-permute-start | bytes 4460552 | tf_op jit(solution)/shard_map/ppermute | solution.py:46
  26.3 27.4 %collective-permute-start.2 = (bf16[3,176,1408]{2,1,0:T(8,128)(2,1)}, bf16[3,176,1408]{2,1,0:T(8,128)(2,1)}, u32[]{:S(2)}, u32[]{:S(2)}) collective-permute-start(bf16[3,176,1408]{2,1,0:T(8,128)(2,1)} %pad_maximum_fusion.rest_0_), channel_id=1, source_target_pairs={{0,4},{16,17},{32,36},{48,49},{64,68},{80,81},{96,100},{112,113},{... | collective-permute-start | bytes 4460552 | tf_op jit(solution)/shard_map/ppermute | solution.py:46
  28.3 21.5 %collective-permute-start.4 = (bf16[176,1408]{1,0:T(8,128)(2,1)S(1)}, bf16[176,1408]{1,0:T(8,128)(2,1)S(1)}, u32[]{:S(2)}, u32[]{:S(2)}) collective-permute-start(bf16[176,1408]{1,0:T(8,128)(2,1)S(1)} %shard_map.86), channel_id=1, source_target_pairs={{0,2},{16,24},{32,34},{48,56},{64,66},{80,88},{96,98},{112,120},{1... | collective-permute-start | bytes 1486856 | tf_op jit(solution)/shard_map/ppermute | solution.py:46
  53.7 9.7 %collective-permute-start.5 = (bf16[176,1408]{1,0:T(8,128)(2,1)S(1)}, bf16[176,1408]{1,0:T(8,128)(2,1)}, u32[]{:S(2)}, u32[]{:S(2)}) collective-permute-start(bf16[176,1408]{1,0:T(8,128)(2,1)S(1)} %collective-permute-done.4.rest_1_), channel_id=1, source_target_pairs={{0,268},{16,19},{32,300},{48,51},{64,332},{80,83},{96,364},{112,11... | collective-permute-start | bytes 1486856 | tf_op jit(solution)/shard_map/ppermute | solution.py:46
  55.6 22.2 %collective-permute-start.12 = (bf16[176,1408]{1,0:T(8,128)(2,1)S(1)}, bf16[176,1408]{1,0:T(8,128)(2,1)S(1)}, u32[]{:S(2)}, u32[]{:S(2)}) collective-permute-start(bf16[176,1408]{1,0:T(8,128)(2,1)S(1)} %collective-permute-done.4.rest_1_), channel_id=1, source_target_pairs={{0,4},{16,17},{32,36},{48,49},{64,68},{80,81},{96,100},{112,113},{... | collective-permute-start | bytes 1486856 | tf_op jit(solution)/shard_map/ppermute | solution.py:46
  59.0 41.2 %collective-permute-start.11 = (bf16[3,176,1408]{2,1,0:T(8,128)(2,1)}, bf16[3,176,1408]{2,1,0:T(8,128)(2,1)}, u32[]{:S(2)}, u32[]{:S(2)}) collective-permute-start(bf16[3,176,1408]{2,1,0:T(8,128)(2,1)} %collective-permute-done.2.rest_2_), channel_id=1, source_target_pairs={{0,4},{16,17},{32,36},{48,49},{64,68},{80,81},{96,100},{112,113},{... | collective-permute-start | bytes 4460552 | tf_op jit(solution)/shard_map/ppermute | solution.py:46
  63.4 16.4 %collective-permute-start.7 = (bf16[176,1408]{1,0:T(8,128)(2,1)S(1)}, bf16[176,1408]{1,0:T(8,128)(2,1)S(1)}, u32[]{:S(2)}, u32[]{:S(2)}) collective-permute-start(bf16[176,1408]{1,0:T(8,128)(2,1)S(1)} %collective-permute-done.4.rest_1_), channel_id=1, source_target_pairs={{0,16},{16,0},{32,48},{48,32},{64,80},{80,64},{96,112},{112,96},{1... | collective-permute-start | bytes 1486856 | tf_op jit(solution)/shard_map/ppermute | solution.py:46
  72.7 0.8 copy-start.8
  73.5 26.7 %collective-permute-start.6 = (bf16[3,176,1408]{2,1,0:T(8,128)(2,1)}, bf16[3,176,1408]{2,1,0:T(8,128)(2,1)}, u32[]{:S(2)}, u32[]{:S(2)}) collective-permute-start(bf16[3,176,1408]{2,1,0:T(8,128)(2,1)} %pad_maximum_fusion.rest_0_), channel_id=1, source_target_pairs={{0,16},{16,0},{32,48},{48,32},{64,80},{80,64},{96,112},{112,96},{1... | collective-permute-start | bytes 4460552 | tf_op jit(solution)/shard_map/ppermute | solution.py:46
  75.4 24.8 %collective-permute-start.8 = (bf16[3,176,1408]{2,1,0:T(8,128)(2,1)}, bf16[3,176,1408]{2,1,0:T(8,128)(2,1)}, u32[]{:S(2)}, u32[]{:S(2)}) collective-permute-start(bf16[3,176,1408]{2,1,0:T(8,128)(2,1)} %collective-permute-done.2.rest_2_), channel_id=1, source_target_pairs={{0,16},{16,0},{32,48},{48,32},{64,80},{80,64},{96,112},{112,96},{1... | collective-permute-start | bytes 4460552 | tf_op jit(solution)/shard_map/ppermute | solution.py:46
  77.8 2.0 %copy-start.10 = (bf16[176,1408]{1,0:T(8,128)(2,1)}, bf16[176,1408]{1,0:T(8,128)(2,1)S(1)}, u32[]{:S(2)}) copy-start(bf16[176,1408]{1,0:T(8,128)(2,1)S(1)} %collective-permute-done.12.rest_3_) | copy-start | bytes 1486852
  77.9 22.3 %collective-permute-start.9 = (bf16[3,176,1408]{2,1,0:T(8,128)(2,1)}, bf16[3,176,1408]{2,1,0:T(8,128)(2,1)}, u32[]{:S(2)}, u32[]{:S(2)}) collective-permute-start(bf16[3,176,1408]{2,1,0:T(8,128)(2,1)} %collective-permute-done.3.rest_6_), channel_id=1, source_target_pairs={{0,16},{16,0},{32,48},{48,32},{64,80},{80,64},{96,112},{112,96},{1... | collective-permute-start | bytes 4460552 | tf_op jit(solution)/shard_map/ppermute | solution.py:46
  79.8 0.8 copy-start.12
  80.6 10.2 %collective-permute-start.13 = (bf16[176,1408]{1,0:T(8,128)(2,1)}, bf16[176,1408]{1,0:T(8,128)(2,1)}, u32[]{:S(2)}, u32[]{:S(2)}) collective-permute-start(bf16[176,1408]{1,0:T(8,128)(2,1)} %collective-permute-done.5.rest_7_), channel_id=1, source_target_pairs={{0,268},{16,19},{32,300},{48,51},{64,332},{80,83},{96,364},{112,11... | collective-permute-start | bytes 1486856 | tf_op jit(solution)/shard_map/ppermute | solution.py:46
  90.8 9.3 %collective-permute-start.10 = (bf16[176,1408]{1,0:T(8,128)(2,1)}, bf16[176,1408]{1,0:T(8,128)(2,1)}, u32[]{:S(2)}, u32[]{:S(2)}) collective-permute-start(bf16[176,1408]{1,0:T(8,128)(2,1)} %collective-permute-done.5.rest_7_), channel_id=1, source_target_pairs={{0,16},{16,0},{32,48},{48,32},{64,80},{80,64},{96,112},{112,96},{1... | collective-permute-start | bytes 1486856 | tf_op jit(solution)/shard_map/ppermute | solution.py:46
  94.6 7.6 %copy-start.11 = (bf16[176,1408]{1,0:T(8,128)(2,1)S(1)}, bf16[176,1408]{1,0:T(8,128)(2,1)}, u32[]{:S(2)}) copy-start(bf16[176,1408]{1,0:T(8,128)(2,1)} %copy-done.10) | copy-start | bytes 1486852
  94.6 15.0 %copy-start.9 = (bf16[176,1408]{1,0:T(8,128)(2,1)S(1)}, bf16[176,1408]{1,0:T(8,128)(2,1)}, u32[]{:S(2)}) copy-start(bf16[176,1408]{1,0:T(8,128)(2,1)} %copy-done.8) | copy-start | bytes 1486852
  94.6 15.0 %copy-start.13 = (bf16[176,1408]{1,0:T(8,128)(2,1)S(1)}, bf16[176,1408]{1,0:T(8,128)(2,1)}, u32[]{:S(2)}) copy-start(bf16[176,1408]{1,0:T(8,128)(2,1)} %copy-done.12) | copy-start | bytes 1486852
  96.1 1.2 copy-start.4
  97.3 1.1 copy-start.5
  98.4 0.9 copy-start.6
  99.3 0.9 copy-start.7
  100.2 8.3 %collective-permute-start.15 = (bf16[3,176,1408]{2,1,0:T(8,128)(2,1)}, bf16[3,176,1408]{2,1,0:T(8,128)(2,1)S(1)}, u32[]{:S(2)}, u32[]{:S(2)}) collective-permute-start(bf16[3,176,1408]{2,1,0:T(8,128)(2,1)} %collective-permute-done.11.rest_4_), channel_id=1, source_target_pairs={{0,16},{16,0},{32,48},{48,32},{64,80},{80,64},{96,112},{112,96},{1... | collective-permute-start | bytes 4460552 | tf_op jit(solution)/shard_map/ppermute | solution.py:46
  102.1 4.3 %collective-permute-start.14 = (bf16[176,1408]{1,0:T(8,128)(2,1)S(1)}, bf16[176,1408]{1,0:T(8,128)(2,1)S(1)}, u32[]{:S(2)}, u32[]{:S(2)}) collective-permute-start(bf16[176,1408]{1,0:T(8,128)(2,1)S(1)} %copy-done.11), channel_id=1, source_target_pairs={{0,16},{16,0},{32,48},{48,32},{64,80},{80,64},{96,112},{112,96},{1... | collective-permute-start | bytes 1486856 | tf_op jit(solution)/shard_map/ppermute | solution.py:46
  104.6 4.0 %collective-permute-start.16 = (bf16[176,1408]{1,0:T(8,128)(2,1)}, bf16[176,1408]{1,0:T(8,128)(2,1)S(1)}, u32[]{:S(2)}, u32[]{:S(2)}) collective-permute-start(bf16[176,1408]{1,0:T(8,128)(2,1)} %collective-permute-done.13.rest_5_), channel_id=1, source_target_pairs={{0,16},{16,0},{32,48},{48,32},{64,80},{80,64},{96,112},{112,96},{1... | collective-permute-start | bytes 1486856 | tf_op jit(solution)/shard_map/ppermute | solution.py:46
  108.5 1.1 copy-start.15
  155.7 19.4 %all-to-all-start.1 = ((f32[32,1,2816]{2,1,0:T(1,128)}), f32[32,1,2816]{2,1,0:T(1,128)S(1)}, u32[]{:S(2)}, u32[]{:S(2)}) async-start(f32[32,1,2816]{2,1,0:T(1,128)} %broadcast_in_dim.5), calls=%async_computation.1 | async-start | bytes 720896 | tf_op jit(solution)/shard_map/all_to_all | solution.py:261

commit v3 on v2

--- a/solution.py
+++ b/solution.py
@@ -130,8 +130,7 @@
     )(state.T, inj.T, cot.T, gain)
 
 
-SINGLE = 2
-SLOT = (0, 1, None, 2)
+PLACE = (0, 2, 6, 4)
 
 
 def core_kernel(place, op0_ref, cb_ref, n0_ref, inj_ref, cot_ref, gain_ref, *rest):
@@ -147,25 +146,26 @@
                 sx = jnp.where(core == 0, px + 4 - j, px + 4 - k) % 4
                 sy = jnp.where(core == 0, py + 4 - k, py + 4 - j) % 4
                 row = pl.multiple_of((sy * 4 + sx) * SP, SP)
-                src = pieces[8 * who + 2 * k + (j == SINGLE)]
-                if j != SINGLE:
-                    src = src.at[SLOT[j]]
+                src = pieces[8 * who + PLACE[k] + j // 2].at[j % 2]
                 dst = w_ref.at[pl.ds(row, SP), pl.ds(pl.multiple_of(core * HALF, 128), HALF)]
                 copies.append(pltpu.make_async_copy(src, dst, sems.at[len(copies)]))
     for c in copies:
         c.start()
-    for c in copies:
-        c.wait()
     deep = rounds >= 2
 
-    def first(t, ssq):
-        cols = pl.ds(pl.multiple_of(t * HALF, 128), HALF)
-        back_ref[:, cols] = nt(cb_ref[...], w_ref[cols, :])
+    ssq = jnp.zeros((TOK, 1), F32)
+    for who in range(2):
+        for c in copies[16 * who : 16 * who + 16]:
+            c.wait()
+        core = pc if who == 0 else 1 - pc
+        cols = pl.ds(pl.multiple_of(core * HALF, 128), HALF)
         s1 = jnp.dot(op0_ref[...], w_ref[:, cols], preferred_element_type=F32) + inj_ref[:, cols].astype(F32)
         s1_ref[:, cols] = s1
-        return ssq + jnp.sum(s1 * s1, axis=1, keepdims=True)
-
-    ssq = lax.fori_loop(0, 2, first, jnp.zeros((TOK, 1), F32))
+        ssq = ssq + jnp.sum(s1 * s1, axis=1, keepdims=True)
+        for t in range(2):
+            rows = slice(t * HALF, t * HALF + HALF)
+            back = nt(cb_ref[:, cols], w_ref[rows, cols])
+            back_ref[:, rows] = back if who == 0 else back_ref[:, rows] + back
     inv1 = lax.rsqrt(ssq / W + EPS)
 
     def second(t, dots):
@@ -233,24 +233,27 @@
 
 
 def gather(own, acts):
-    m1 = send(own, along(True, 1))
-    m3 = send(own, along(True, -1))
-    m2 = send(own, along(True, 2))
-    three = jnp.stack([own, m1, m3])
-    three1 = send(three, along(False, 1))
-    three3 = send(three, along(False, -1))
-    three1, three3, m2 = lax.optimization_barrier((three1, three3, m2))
-    three2 = send(three1, along(False, 1))
-    one3 = send(m2, along(False, -1))
-    one1 = send(m2, along(False, 1))
-    own4 = lax.optimization_barrier((three, m2, three1, three3, one3))
-    one2 = send(own4[4], along(False, -1))
-    early = tuple(send(a, SWAP) for a in own4)
-    acts, early, (three2, one1, one2) = lax.optimization_barrier((acts, early, (three2, one1, one2)))
-    late = tuple(send(a, SWAP) for a in (three2, one1, one2))
-    mine = (three, m2, three1, one1, three2, one2, three3, one3)
-    theirs = (early[0], early[1], early[2], late[1], late[0], late[2], early[3], early[4])
-    return acts, mine + theirs
+    down = send(own, along(True, -1))
+    up = send(own, along(True, 1))
+    far = send(own, along(True, 2))
+    acts, down, up, far = lax.optimization_barrier((acts, down, up, far))
+    low = jnp.stack([own, up])
+    high = jnp.stack([far, down])
+    near = (low, high)
+    swapped = tuple(send(a, SWAP) for a in near)
+    low3 = send(low, along(False, -1))
+    high1 = send(high, along(False, 1))
+    high3 = send(high, along(False, -1))
+    low1 = send(low, along(False, 1))
+    swapped, low3, high1, low1, high3 = lax.optimization_barrier((swapped, low3, high1, low1, high3))
+    middle = (low1, high1, low3, high3)
+    swapped += tuple(send(a, SWAP) for a in middle)
+    high2 = send(high3, along(False, -1))
+    low2 = send(low1, along(False, 1))
+    swapped, low2, high2 = lax.optimization_barrier((swapped, low2, high2))
+    last = (low2, high2)
+    swapped += tuple(send(a, SWAP) for a in last)
+    return acts, near + middle + last + swapped
 
 
 def total(part):

time: 177 us -> 158 us (0.89)
  waiting for transfers between devices: 55.2 us -> 40.1 us
  local copies, waits for them, and re-layouts: 12.9 us -> 10.2 us
  Pallas kernels: 27.2 us -> 24.6 us
  starting transfers between devices: 57.1 us -> 59.4 us
    ppermute x17, waiting for transfers between devices: 44 us -> 28.9 us  [send(): return lax.ppermute(array, AXES, pairs)]
    unnamed x32 -> x38, local copies, waits for them, and re-layouts: 7.97 us -> 4.6 us
    all_to_all x1, starting transfers between devices: 5.26 us -> 7.91 us  [total(): lax.all_to_all(jnp.broadcast_to(part, (32, WP)), AXES, 0, 0, axis_index_g...]
    pallas_call x1, Pallas kernels: 24.6 us -> 22 us  [core_call(): pl.pallas_call(core_kernel, out_shape=(jax.ShapeDtypeStruct((TOK, WP), BF...]
where the time goes in v3:
time: 158 us; the launch traced here: 157 us
  starting transfers between devices  59.4 us (38%)
  waiting for transfers between devices  40.1 us (25%)
  Pallas kernels  24.6 us (16%)
  blocking collectives  20.2 us (13%)
  local copies, waits for them, and re-layouts  10.2 us (6%)
  between operations  1.84 us (1%)
    ppermute x17, starting transfers between devices, send(): return lax.ppermute(array, AXES, pairs)  51.5 us
    ppermute x17, waiting for transfers between devices, send(): return lax.ppermute(array, AXES, pairs)  28.9 us
    pallas_call x1, Pallas kernels, core_call(): pl.pallas_call(core_kernel, out_shape=(jax.ShapeDtypeStruct((TOK, WP), BF...  22 us
    all_to_all x1, blocking collectives, total(): lax.all_to_all(jnp.broadcast_to(part, (16, WP)), 'dp', 0, 0, axis_index_g...  20.2 us
    all_to_all x1, waiting for transfers between devices, total(): lax.all_to_all(jnp.broadcast_to(part, (32, WP)), AXES, 0, 0, axis_index_g...  11.2 us
    all_to_all x1, starting transfers between devices, total(): lax.all_to_all(jnp.broadcast_to(part, (32, WP)), AXES, 0, 0, axis_index_g...  7.91 us
    unnamed x38, local copies, waits for them, and re-layouts  4.6 us
  transfers between devices with their start and end apart: 18, of which 8 were waited for; matrix products, arithmetic and copies ran while one was open for 2% of the time, Pallas kernels for 1%

profile of v3, /device:TPU:1, one launch (start us, length us, event | category | flops | bytes accessed | tf_op | source)
XLA Modules:
  0.0 157.0 jit_solution(3635338708414360676)
XLA Ops:
  1.4 0.1 pad_add_fusion.place
  1.5 1.2 copy-done.2
  2.7 1.2 shard_map.86
  3.8 5.0 %collective-permute-start.2 = (bf16[176,1408]{1,0:T(8,128)(2,1)S(1)}, bf16[176,1408]{1,0:T(8,128)(2,1)S(1)}, u32[]{:S(2)}, u32[]{:S(2)}) collective-permute-start(bf16[176,1408]{1,0:T(8,128)(2,1)S(1)} %shard_map.86), channel_id=1, source_target_pairs={{0,2},{16,24},{32,34},{48,56},{64,66},{80,88},{96,98},{112,120},{1... | collective-permute-start | bytes 1486856 | tf_op jit(solution)/shard_map/ppermute | solution.py:46
  8.9 3.2 %collective-permute-start.1 = (bf16[176,1408]{1,0:T(8,128)(2,1)S(1)}, bf16[176,1408]{1,0:T(8,128)(2,1)S(1)}, u32[]{:S(2)}, u32[]{:S(2)}) collective-permute-start(bf16[176,1408]{1,0:T(8,128)(2,1)S(1)} %shard_map.86), channel_id=1, source_target_pairs={{0,1},{16,20},{32,33},{48,52},{64,65},{80,84},{96,97},{112,116},{1... | collective-permute-start | bytes 1486856 | tf_op jit(solution)/shard_map/ppermute | solution.py:46
  12.1 3.3 %collective-permute-start = (bf16[176,1408]{1,0:T(8,128)(2,1)S(1)}, bf16[176,1408]{1,0:T(8,128)(2,1)S(1)}, u32[]{:S(2)}, u32[]{:S(2)}) collective-permute-start(bf16[176,1408]{1,0:T(8,128)(2,1)S(1)} %shard_map.86), channel_id=1, source_target_pairs={{0,3},{16,284},{32,35},{48,316},{64,67},{80,348},{96,99},{112,380}... | collective-permute-start | bytes 1486856 | tf_op jit(solution)/shard_map/ppermute | solution.py:46
  15.4 0.8 reshape.36
  16.2 0.1 reshape.37.gain_ref
  16.3 1.3 copy-done.1
  17.7 1.1 copy-done.3
  18.8 1.4 shard_map.85
  20.2 7.2 %collective-permute-done.1 = bf16[176,1408]{1,0:T(8,128)(2,1)S(1)} collective-permute-done((bf16[176,1408]{1,0:T(8,128)(2,1)S(1)}, bf16[176,1408]{1,0:T(8,128)(2,1)S(1)}, u32[]{:S(2)}, u32[]{:S(2)}) %collective-permute-start.1) | collective-permute-done | bytes 495648 | tf_op jit(solution)/shard_map/ppermute | solution.py:46
  27.4 0.1 pad_maximum_fusion.1.rest_1_
  27.5 4.1 %collective-permute-start.8 = (bf16[2,176,1408]{2,1,0:T(8,128)(2,1)S(1)}, bf16[2,176,1408]{2,1,0:T(8,128)(2,1)S(1)}, u32[]{:S(2)}, u32[]{:S(2)}) collective-permute-start(bf16[2,176,1408]{2,1,0:T(8,128)(2,1)S(1)} %pad_maximum_fusion.1.rest_1_), channel_id=1, source_target_pairs={{0,268},{16,19},{32,300},{48,51},{64,332},{80,83},{96,364},{112,11... | collective-permute-start | bytes 2973704 | tf_op jit(solution)/shard_map/ppermute | solution.py:46
  31.6 1.9 %collective-permute-start.6 = (bf16[2,176,1408]{2,1,0:T(8,128)(2,1)S(1)}, bf16[2,176,1408]{2,1,0:T(8,128)(2,1)S(1)}, u32[]{:S(2)}, u32[]{:S(2)}) collective-permute-start(bf16[2,176,1408]{2,1,0:T(8,128)(2,1)S(1)} %pad_maximum_fusion.1.rest_1_), channel_id=1, source_target_pairs={{0,4},{16,17},{32,36},{48,49},{64,68},{80,81},{96,100},{112,113},{... | collective-permute-start | bytes 2973704 | tf_op jit(solution)/shard_map/ppermute | solution.py:46
  33.6 2.6 %collective-permute-start.4 = (bf16[2,176,1408]{2,1,0:T(8,128)(2,1)S(1)}, bf16[2,176,1408]{2,1,0:T(8,128)(2,1)S(1)}, u32[]{:S(2)}, u32[]{:S(2)}) collective-permute-start(bf16[2,176,1408]{2,1,0:T(8,128)(2,1)S(1)} %pad_maximum_fusion.1.rest_1_), channel_id=1, source_target_pairs={{0,16},{16,0},{32,48},{48,32},{64,80},{80,64},{96,112},{112,96},{1... | collective-permute-start | bytes 2973704 | tf_op jit(solution)/shard_map/ppermute | solution.py:46
  36.1 0.1 pad_maximum_fusion.rest_0_
  36.3 2.1 %collective-permute-start.7 = (bf16[2,176,1408]{2,1,0:T(8,128)(2,1)S(1)}, bf16[2,176,1408]{2,1,0:T(8,128)(2,1)S(1)}, u32[]{:S(2)}, u32[]{:S(2)}) collective-permute-start(bf16[2,176,1408]{2,1,0:T(8,128)(2,1)S(1)} %pad_maximum_fusion.rest_0_), channel_id=1, source_target_pairs={{0,4},{16,17},{32,36},{48,49},{64,68},{80,81},{96,100},{112,113},{... | collective-permute-start | bytes 2973704 | tf_op jit(solution)/shard_map/ppermute | solution.py:46
  38.4 4.4 %collective-permute-start.5 = (bf16[2,176,1408]{2,1,0:T(8,128)(2,1)S(1)}, bf16[2,176,1408]{2,1,0:T(8,128)(2,1)S(1)}, u32[]{:S(2)}, u32[]{:S(2)}) collective-permute-start(bf16[2,176,1408]{2,1,0:T(8,128)(2,1)S(1)} %pad_maximum_fusion.rest_0_), channel_id=1, source_target_pairs={{0,268},{16,19},{32,300},{48,51},{64,332},{80,83},{96,364},{112,11... | collective-permute-start | bytes 2973704 | tf_op jit(solution)/shard_map/ppermute | solution.py:46
  42.8 3.5 %collective-permute-start.3 = (bf16[2,176,1408]{2,1,0:T(8,128)(2,1)S(1)}, bf16[2,176,1408]{2,1,0:T(8,128)(2,1)S(1)}, u32[]{:S(2)}, u32[]{:S(2)}) collective-permute-start(bf16[2,176,1408]{2,1,0:T(8,128)(2,1)S(1)} %pad_maximum_fusion.rest_0_), channel_id=1, source_target_pairs={{0,16},{16,0},{32,48},{48,32},{64,80},{80,64},{96,112},{112,96},{1... | collective-permute-start | bytes 2973704 | tf_op jit(solution)/shard_map/ppermute | solution.py:46
  46.4 1.7 %collective-permute-done.6.rest_3_ = bf16[2,176,1408]{2,1,0:T(8,128)(2,1)S(1)} collective-permute-done((bf16[2,176,1408]{2,1,0:T(8,128)(2,1)S(1)}, bf16[2,176,1408]{2,1,0:T(8,128)(2,1)S(1)}, u32[]{:S(2)}, u32[]{:S(2)}) %collective-permute-start.6) | collective-permute-done | bytes 991264 | tf_op jit(solution)/shard_map/ppermute | solution.py:46
  48.1 10.3 %collective-permute-done.7.rest_2_ = bf16[2,176,1408]{2,1,0:T(8,128)(2,1)S(1)} collective-permute-done((bf16[2,176,1408]{2,1,0:T(8,128)(2,1)S(1)}, bf16[2,176,1408]{2,1,0:T(8,128)(2,1)S(1)}, u32[]{:S(2)}, u32[]{:S(2)}) %collective-permute-start.7) | collective-permute-done | bytes 991264 | tf_op jit(solution)/shard_map/ppermute | solution.py:46
  58.4 1.9 %collective-permute-start.10 = (bf16[2,176,1408]{2,1,0:T(8,128)(2,1)S(1)}, bf16[2,176,1408]{2,1,0:T(8,128)(2,1)S(1)}, u32[]{:S(2)}, u32[]{:S(2)}) collective-permute-start(bf16[2,176,1408]{2,1,0:T(8,128)(2,1)S(1)} %collective-permute-done.6.rest_3_), channel_id=1, source_target_pairs={{0,16},{16,0},{32,48},{48,32},{64,80},{80,64},{96,112},{112,96},{1... | collective-permute-start | bytes 2973704 | tf_op jit(solution)/shard_map/ppermute | solution.py:46
  60.3 1.9 %collective-permute-start.13 = (bf16[2,176,1408]{2,1,0:T(8,128)(2,1)S(1)}, bf16[2,176,1408]{2,1,0:T(8,128)(2,1)S(1)}, u32[]{:S(2)}, u32[]{:S(2)}) collective-permute-start(bf16[2,176,1408]{2,1,0:T(8,128)(2,1)S(1)} %collective-permute-done.7.rest_2_), channel_id=1, source_target_pairs={{0,4},{16,17},{32,36},{48,49},{64,68},{80,81},{96,100},{112,113},{... | collective-permute-start | bytes 2973704 | tf_op jit(solution)/shard_map/ppermute | solution.py:46
  62.3 2.8 %collective-permute-start.9 = (bf16[2,176,1408]{2,1,0:T(8,128)(2,1)S(1)}, bf16[2,176,1408]{2,1,0:T(8,128)(2,1)S(1)}, u32[]{:S(2)}, u32[]{:S(2)}) collective-permute-start(bf16[2,176,1408]{2,1,0:T(8,128)(2,1)S(1)} %collective-permute-done.7.rest_2_), channel_id=1, source_target_pairs={{0,16},{16,0},{32,48},{48,32},{64,80},{80,64},{96,112},{112,96},{1... | collective-permute-start | bytes 2973704 | tf_op jit(solution)/shard_map/ppermute | solution.py:46
  65.1 1.9 %collective-permute-start.11 = (bf16[2,176,1408]{2,1,0:T(8,128)(2,1)S(1)}, bf16[2,176,1408]{2,1,0:T(8,128)(2,1)S(1)}, u32[]{:S(2)}, u32[]{:S(2)}) collective-permute-start(bf16[2,176,1408]{2,1,0:T(8,128)(2,1)S(1)} %collective-permute-done.5.rest_4_), channel_id=1, source_target_pairs={{0,16},{16,0},{32,48},{48,32},{64,80},{80,64},{96,112},{112,96},{1... | collective-permute-start | bytes 2973704 | tf_op jit(solution)/shard_map/ppermute | solution.py:46
  67.0 4.2 %collective-permute-start.14 = (bf16[2,176,1408]{2,1,0:T(8,128)(2,1)S(1)}, bf16[2,176,1408]{2,1,0:T(8,128)(2,1)S(1)}, u32[]{:S(2)}, u32[]{:S(2)}) collective-permute-start(bf16[2,176,1408]{2,1,0:T(8,128)(2,1)S(1)} %collective-permute-done.8.rest_5_), channel_id=1, source_target_pairs={{0,268},{16,19},{32,300},{48,51},{64,332},{80,83},{96,364},{112,11... | collective-permute-start | bytes 2973704 | tf_op jit(solution)/shard_map/ppermute | solution.py:46
  71.2 3.0 %collective-permute-start.12 = (bf16[2,176,1408]{2,1,0:T(8,128)(2,1)S(1)}, bf16[2,176,1408]{2,1,0:T(8,128)(2,1)S(1)}, u32[]{:S(2)}, u32[]{:S(2)}) collective-permute-start(bf16[2,176,1408]{2,1,0:T(8,128)(2,1)S(1)} %collective-permute-done.8.rest_5_), channel_id=1, source_target_pairs={{0,16},{16,0},{32,48},{48,32},{64,80},{80,64},{96,112},{112,96},{1... | collective-permute-start | bytes 2973704 | tf_op jit(solution)/shard_map/ppermute | solution.py:46
  74.2 2.6 %collective-permute-done.13.rest_6_ = bf16[2,176,1408]{2,1,0:T(8,128)(2,1)S(1)} collective-permute-done((bf16[2,176,1408]{2,1,0:T(8,128)(2,1)S(1)}, bf16[2,176,1408]{2,1,0:T(8,128)(2,1)S(1)}, u32[]{:S(2)}, u32[]{:S(2)}) %collective-permute-start.13) | collective-permute-done | bytes 991264 | tf_op jit(solution)/shard_map/ppermute | solution.py:46
  76.8 5.5 %collective-permute-done.14.rest_7_ = bf16[2,176,1408]{2,1,0:T(8,128)(2,1)S(1)} collective-permute-done((bf16[2,176,1408]{2,1,0:T(8,128)(2,1)S(1)}, bf16[2,176,1408]{2,1,0:T(8,128)(2,1)S(1)}, u32[]{:S(2)}, u32[]{:S(2)}) %collective-permute-start.14) | collective-permute-done | bytes 991264 | tf_op jit(solution)/shard_map/ppermute | solution.py:46
  82.3 3.5 %collective-permute-start.15 = (bf16[2,176,1408]{2,1,0:T(8,128)(2,1)S(1)}, bf16[2,176,1408]{2,1,0:T(8,128)(2,1)S(1)}, u32[]{:S(2)}, u32[]{:S(2)}) collective-permute-start(bf16[2,176,1408]{2,1,0:T(8,128)(2,1)S(1)} %collective-permute-done.13.rest_6_), channel_id=1, source_target_pairs={{0,16},{16,0},{32,48},{48,32},{64,80},{80,64},{96,112},{112,96},{1... | collective-permute-start | bytes 2973704 | tf_op jit(solution)/shard_map/ppermute | solution.py:46
  85.9 2.1 %collective-permute-start.16 = (bf16[2,176,1408]{2,1,0:T(8,128)(2,1)S(1)}, bf16[2,176,1408]{2,1,0:T(8,128)(2,1)}, u32[]{:S(2)}, u32[]{:S(2)}) collective-permute-start(bf16[2,176,1408]{2,1,0:T(8,128)(2,1)S(1)} %collective-permute-done.14.rest_7_), channel_id=1, source_target_pairs={{0,16},{16,0},{32,48},{48,32},{64,80},{80,64},{96,112},{112,96},{1... | collective-permute-start | bytes 2973704 | tf_op jit(solution)/shard_map/ppermute | solution.py:46
  88.1 0.9 copy-done.18
  89.0 1.5 collective-permute-done.16.rest_15_
  90.5 22.0 %shard_map.87 = (bf16[128,2816]{1,0:T(8,128)(2,1)S(1)}, bf16[128,2816]{1,0:T(8,128)(2,1)S(1)}, f32[1,2816]{1,0:T(1,128)S(1)}) custom-call(s32[4]{0:T(128)S(1)} %pad_add_fusion.place, bf16[128,2816]{1,0:T(8,128)(2,1)S(1)} %get-tuple-element.38.op0_ref, bf16[128,2816]{1,0:T(8,128)(2,1)S(1)} %get-tuple-element.39.cb_ref, f32[128,2816]{1,0:T(8,128)} %copy-done.4, ...), custom_call_target="tpu_custom_call" | custom-call | flops 8120172544 | bytes 15859712 | tf_op jit(solution)/shard_map/pallas_call | solution.py:209
  112.6 0.1 broadcast_in_dim.4
  112.7 20.2 %all_to_all.12 = f32[16,1,2816]{2,1,0:T(1,128)S(1)} all-to-all(f32[16,1,2816]{2,1,0:T(1,128)S(1)} %broadcast_in_dim.4), channel_id=1, replica_groups={{0,16,32,48,64,80,96,112,128,144,160,176,192,208,224,240},{256,272,288,..., dimensions={0} | all-to-all | bytes 360448 | tf_op jit(solution)/shard_map/all_to_all | solution.py:261
  132.9 0.1 reduce_sum.18
  133.1 0.9 broadcast_in_dim.5
  134.0 7.9 %all-to-all-start.1 = ((f32[32,1,2816]{2,1,0:T(1,128)}), f32[32,1,2816]{2,1,0:T(1,128)S(1)}, u32[]{:S(2)}, u32[]{:S(2)}) async-start(f32[32,1,2816]{2,1,0:T(1,128)} %broadcast_in_dim.5), calls=%async_computation.1 | async-start | bytes 720896 | tf_op jit(solution)/shard_map/all_to_all | solution.py:264
  141.9 0.3 copy.15
  142.3 1.1 reshape.39
  143.4 0.3 copy.16
  143.8 1.1 reshape.41
  144.8 11.2 %all-to-all-done.1 = f32[32,1,2816]{2,1,0:T(1,128)S(1)} async-done(((f32[32,1,2816]{2,1,0:T(1,128)}), f32[32,1,2816]{2,1,0:T(1,128)S(1)}, u32[]{:S(2)}, u32[]{:S(2)}) %all-to-all-start.1) | async-done | bytes 360480 | tf_op jit(solution)/shard_map/all_to_all | solution.py:264
  156.0 0.2 reduce_sum.19
  156.2 0.1 reshape_transpose_broadcast_in_dim.3
  156.3 0.7 reshape_transpose_reshape.3
  (49 shorter events, 0.3 us)
Async XLA Ops:
  0.6 15.7 %copy-start = (f32[128,2640]{0,1:T(8,128)S(1)}, f32[128,2640]{0,1:T(8,128)}, u32[]{:S(2)}) copy-start(f32[128,2640]{0,1:T(8,128)} %param.6) | copy-start | bytes 4055044
  1.5 1.2 copy-start.2
  3.8 16.4 %collective-permute-start.2 = (bf16[176,1408]{1,0:T(8,128)(2,1)S(1)}, bf16[176,1408]{1,0:T(8,128)(2,1)S(1)}, u32[]{:S(2)}, u32[]{:S(2)}) collective-permute-start(bf16[176,1408]{1,0:T(8,128)(2,1)S(1)} %shard_map.86), channel_id=1, source_target_pairs={{0,2},{16,24},{32,34},{48,56},{64,66},{80,88},{96,98},{112,120},{1... | collective-permute-start | bytes 1486856 | tf_op jit(solution)/shard_map/ppermute | solution.py:46
  8.9 18.5 %collective-permute-start.1 = (bf16[176,1408]{1,0:T(8,128)(2,1)S(1)}, bf16[176,1408]{1,0:T(8,128)(2,1)S(1)}, u32[]{:S(2)}, u32[]{:S(2)}) collective-permute-start(bf16[176,1408]{1,0:T(8,128)(2,1)S(1)} %shard_map.86), channel_id=1, source_target_pairs={{0,1},{16,20},{32,33},{48,52},{64,65},{80,84},{96,97},{112,116},{1... | collective-permute-start | bytes 1486856 | tf_op jit(solution)/shard_map/ppermute | solution.py:46
  12.1 15.3 %collective-permute-start = (bf16[176,1408]{1,0:T(8,128)(2,1)S(1)}, bf16[176,1408]{1,0:T(8,128)(2,1)S(1)}, u32[]{:S(2)}, u32[]{:S(2)}) collective-permute-start(bf16[176,1408]{1,0:T(8,128)(2,1)S(1)} %shard_map.86), channel_id=1, source_target_pairs={{0,3},{16,284},{32,35},{48,316},{64,67},{80,348},{96,99},{112,380}... | collective-permute-start | bytes 1486856 | tf_op jit(solution)/shard_map/ppermute | solution.py:46
  16.3 1.3 copy-start.1
  17.7 1.1 copy-start.3
  20.2 16.1 %copy-start.4 = (f32[128,2816]{1,0:T(8,128)}, f32[128,2816]{1,0:T(8,128)S(1)}, u32[]{:S(2)}) copy-start(f32[128,2816]{1,0:T(8,128)S(1)} %get-tuple-element.40.n0_ref) | copy-start | bytes 4325380
  20.2 16.1 %copy-start.5 = (f32[128,2816]{1,0:T(8,128)}, f32[128,2816]{1,0:T(8,128)S(1)}, u32[]{:S(2)}) copy-start(f32[128,2816]{1,0:T(8,128)S(1)} %get-tuple-element.42.cot_ref) | copy-start | bytes 4325380
  27.5 15.2 %collective-permute-start.8 = (bf16[2,176,1408]{2,1,0:T(8,128)(2,1)S(1)}, bf16[2,176,1408]{2,1,0:T(8,128)(2,1)S(1)}, u32[]{:S(2)}, u32[]{:S(2)}) collective-permute-start(bf16[2,176,1408]{2,1,0:T(8,128)(2,1)S(1)} %pad_maximum_fusion.1.rest_1_), channel_id=1, source_target_pairs={{0,268},{16,19},{32,300},{48,51},{64,332},{80,83},{96,364},{112,11... | collective-permute-start | bytes 2973704 | tf_op jit(solution)/shard_map/ppermute | solution.py:46
  31.6 16.4 %collective-permute-start.6 = (bf16[2,176,1408]{2,1,0:T(8,128)(2,1)S(1)}, bf16[2,176,1408]{2,1,0:T(8,128)(2,1)S(1)}, u32[]{:S(2)}, u32[]{:S(2)}) collective-permute-start(bf16[2,176,1408]{2,1,0:T(8,128)(2,1)S(1)} %pad_maximum_fusion.1.rest_1_), channel_id=1, source_target_pairs={{0,4},{16,17},{32,36},{48,49},{64,68},{80,81},{96,100},{112,113},{... | collective-permute-start | bytes 2973704 | tf_op jit(solution)/shard_map/ppermute | solution.py:46
  33.6 14.5 %collective-permute-start.4 = (bf16[2,176,1408]{2,1,0:T(8,128)(2,1)S(1)}, bf16[2,176,1408]{2,1,0:T(8,128)(2,1)S(1)}, u32[]{:S(2)}, u32[]{:S(2)}) collective-permute-start(bf16[2,176,1408]{2,1,0:T(8,128)(2,1)S(1)} %pad_maximum_fusion.1.rest_1_), channel_id=1, source_target_pairs={{0,16},{16,0},{32,48},{48,32},{64,80},{80,64},{96,112},{112,96},{1... | collective-permute-start | bytes 2973704 | tf_op jit(solution)/shard_map/ppermute | solution.py:46
  36.3 22.1 %collective-permute-start.7 = (bf16[2,176,1408]{2,1,0:T(8,128)(2,1)S(1)}, bf16[2,176,1408]{2,1,0:T(8,128)(2,1)S(1)}, u32[]{:S(2)}, u32[]{:S(2)}) collective-permute-start(bf16[2,176,1408]{2,1,0:T(8,128)(2,1)S(1)} %pad_maximum_fusion.rest_0_), channel_id=1, source_target_pairs={{0,4},{16,17},{32,36},{48,49},{64,68},{80,81},{96,100},{112,113},{... | collective-permute-start | bytes 2973704 | tf_op jit(solution)/shard_map/ppermute | solution.py:46
  38.4 20.0 %collective-permute-start.5 = (bf16[2,176,1408]{2,1,0:T(8,128)(2,1)S(1)}, bf16[2,176,1408]{2,1,0:T(8,128)(2,1)S(1)}, u32[]{:S(2)}, u32[]{:S(2)}) collective-permute-start(bf16[2,176,1408]{2,1,0:T(8,128)(2,1)S(1)} %pad_maximum_fusion.rest_0_), channel_id=1, source_target_pairs={{0,268},{16,19},{32,300},{48,51},{64,332},{80,83},{96,364},{112,11... | collective-permute-start | bytes 2973704 | tf_op jit(solution)/shard_map/ppermute | solution.py:46
  42.8 47.7 %copy-start.6 = (bf16[2,176,1408]{2,1,0:T(8,128)(2,1)}, bf16[2,176,1408]{2,1,0:T(8,128)(2,1)S(1)}, u32[]{:S(2)}) copy-start(bf16[2,176,1408]{2,1,0:T(8,128)(2,1)S(1)} %collective-permute-done.8.rest_5_) | copy-start | bytes 2973700
  42.8 15.6 %collective-permute-start.3 = (bf16[2,176,1408]{2,1,0:T(8,128)(2,1)S(1)}, bf16[2,176,1408]{2,1,0:T(8,128)(2,1)S(1)}, u32[]{:S(2)}, u32[]{:S(2)}) collective-permute-start(bf16[2,176,1408]{2,1,0:T(8,128)(2,1)S(1)} %pad_maximum_fusion.rest_0_), channel_id=1, source_target_pairs={{0,16},{16,0},{32,48},{48,32},{64,80},{80,64},{96,112},{112,96},{1... | collective-permute-start | bytes 2973704 | tf_op jit(solution)/shard_map/ppermute | solution.py:46
  48.1 42.4 %copy-start.7 = (bf16[2,176,1408]{2,1,0:T(8,128)(2,1)}, bf16[2,176,1408]{2,1,0:T(8,128)(2,1)S(1)}, u32[]{:S(2)}) copy-start(bf16[2,176,1408]{2,1,0:T(8,128)(2,1)S(1)} %collective-permute-done.6.rest_3_) | copy-start | bytes 2973700
  48.1 42.4 %copy-start.8 = (bf16[2,176,1408]{2,1,0:T(8,128)(2,1)}, bf16[2,176,1408]{2,1,0:T(8,128)(2,1)S(1)}, u32[]{:S(2)}) copy-start(bf16[2,176,1408]{2,1,0:T(8,128)(2,1)S(1)} %collective-permute-done.4.rest_9_) | copy-start | bytes 2973700
  58.4 32.1 %copy-start.9 = (bf16[2,176,1408]{2,1,0:T(8,128)(2,1)}, bf16[2,176,1408]{2,1,0:T(8,128)(2,1)S(1)}, u32[]{:S(2)}) copy-start(bf16[2,176,1408]{2,1,0:T(8,128)(2,1)S(1)} %collective-permute-done.7.rest_2_) | copy-start | bytes 2973700
  58.4 32.1 %copy-start.10 = (bf16[2,176,1408]{2,1,0:T(8,128)(2,1)}, bf16[2,176,1408]{2,1,0:T(8,128)(2,1)S(1)}, u32[]{:S(2)}) copy-start(bf16[2,176,1408]{2,1,0:T(8,128)(2,1)S(1)} %collective-permute-done.5.rest_4_) | copy-start | bytes 2973700
  58.4 32.1 %copy-start.11 = (bf16[2,176,1408]{2,1,0:T(8,128)(2,1)}, bf16[2,176,1408]{2,1,0:T(8,128)(2,1)S(1)}, u32[]{:S(2)}) copy-start(bf16[2,176,1408]{2,1,0:T(8,128)(2,1)S(1)} %collective-permute-done.3.rest_8_) | copy-start | bytes 2973700
  58.4 12.8 %collective-permute-start.10 = (bf16[2,176,1408]{2,1,0:T(8,128)(2,1)S(1)}, bf16[2,176,1408]{2,1,0:T(8,128)(2,1)S(1)}, u32[]{:S(2)}, u32[]{:S(2)}) collective-permute-start(bf16[2,176,1408]{2,1,0:T(8,128)(2,1)S(1)} %collective-permute-done.6.rest_3_), channel_id=1, source_target_pairs={{0,16},{16,0},{32,48},{48,32},{64,80},{80,64},{96,112},{112,96},{1... | collective-permute-start | bytes 2973704 | tf_op jit(solution)/shard_map/ppermute | solution.py:46
  60.3 16.4 %collective-permute-start.13 = (bf16[2,176,1408]{2,1,0:T(8,128)(2,1)S(1)}, bf16[2,176,1408]{2,1,0:T(8,128)(2,1)S(1)}, u32[]{:S(2)}, u32[]{:S(2)}) collective-permute-start(bf16[2,176,1408]{2,1,0:T(8,128)(2,1)S(1)} %collective-permute-done.7.rest_2_), channel_id=1, source_target_pairs={{0,4},{16,17},{32,36},{48,49},{64,68},{80,81},{96,100},{112,113},{... | collective-permute-start | bytes 2973704 | tf_op jit(solution)/shard_map/ppermute | solution.py:46
  62.3 14.5 %collective-permute-start.9 = (bf16[2,176,1408]{2,1,0:T(8,128)(2,1)S(1)}, bf16[2,176,1408]{2,1,0:T(8,128)(2,1)S(1)}, u32[]{:S(2)}, u32[]{:S(2)}) collective-permute-start(bf16[2,176,1408]{2,1,0:T(8,128)(2,1)S(1)} %collective-permute-done.7.rest_2_), channel_id=1, source_target_pairs={{0,16},{16,0},{32,48},{48,32},{64,80},{80,64},{96,112},{112,96},{1... | collective-permute-start | bytes 2973704 | tf_op jit(solution)/shard_map/ppermute | solution.py:46
  65.1 9.1 %collective-permute-start.11 = (bf16[2,176,1408]{2,1,0:T(8,128)(2,1)S(1)}, bf16[2,176,1408]{2,1,0:T(8,128)(2,1)S(1)}, u32[]{:S(2)}, u32[]{:S(2)}) collective-permute-start(bf16[2,176,1408]{2,1,0:T(8,128)(2,1)S(1)} %collective-permute-done.5.rest_4_), channel_id=1, source_target_pairs={{0,16},{16,0},{32,48},{48,32},{64,80},{80,64},{96,112},{112,96},{1... | collective-permute-start | bytes 2973704 | tf_op jit(solution)/shard_map/ppermute | solution.py:46
  67.0 15.3 %collective-permute-start.14 = (bf16[2,176,1408]{2,1,0:T(8,128)(2,1)S(1)}, bf16[2,176,1408]{2,1,0:T(8,128)(2,1)S(1)}, u32[]{:S(2)}, u32[]{:S(2)}) collective-permute-start(bf16[2,176,1408]{2,1,0:T(8,128)(2,1)S(1)} %collective-permute-done.8.rest_5_), channel_id=1, source_target_pairs={{0,268},{16,19},{32,300},{48,51},{64,332},{80,83},{96,364},{112,11... | collective-permute-start | bytes 2973704 | tf_op jit(solution)/shard_map/ppermute | solution.py:46
  71.2 19.3 %copy-start.12 = (bf16[2,176,1408]{2,1,0:T(8,128)(2,1)}, bf16[2,176,1408]{2,1,0:T(8,128)(2,1)S(1)}, u32[]{:S(2)}) copy-start(bf16[2,176,1408]{2,1,0:T(8,128)(2,1)S(1)} %collective-permute-done.10.rest_11_) | copy-start | bytes 2973700
  71.2 11.1 %collective-permute-start.12 = (bf16[2,176,1408]{2,1,0:T(8,128)(2,1)S(1)}, bf16[2,176,1408]{2,1,0:T(8,128)(2,1)S(1)}, u32[]{:S(2)}, u32[]{:S(2)}) collective-permute-start(bf16[2,176,1408]{2,1,0:T(8,128)(2,1)S(1)} %collective-permute-done.8.rest_5_), channel_id=1, source_target_pairs={{0,16},{16,0},{32,48},{48,32},{64,80},{80,64},{96,112},{112,96},{1... | collective-permute-start | bytes 2973704 | tf_op jit(solution)/shard_map/ppermute | solution.py:46
  74.2 13.8 %copy-start.15 = (bf16[2,176,1408]{2,1,0:T(8,128)(2,1)}, bf16[2,176,1408]{2,1,0:T(8,128)(2,1)S(1)}, u32[]{:S(2)}) copy-start(bf16[2,176,1408]{2,1,0:T(8,128)(2,1)S(1)} %collective-permute-done.11.rest_12_) | copy-start | bytes 2973700
  76.8 13.7 %copy-start.13 = (bf16[2,176,1408]{2,1,0:T(8,128)(2,1)}, bf16[2,176,1408]{2,1,0:T(8,128)(2,1)S(1)}, u32[]{:S(2)}) copy-start(bf16[2,176,1408]{2,1,0:T(8,128)(2,1)S(1)} %collective-permute-done.13.rest_6_) | copy-start | bytes 2973700
  76.8 11.3 %copy-start.14 = (bf16[2,176,1408]{2,1,0:T(8,128)(2,1)}, bf16[2,176,1408]{2,1,0:T(8,128)(2,1)S(1)}, u32[]{:S(2)}) copy-start(bf16[2,176,1408]{2,1,0:T(8,128)(2,1)S(1)} %collective-permute-done.9.rest_10_) | copy-start | bytes 2973700
  82.3 5.7 %copy-start.16 = (bf16[2,176,1408]{2,1,0:T(8,128)(2,1)}, bf16[2,176,1408]{2,1,0:T(8,128)(2,1)S(1)}, u32[]{:S(2)}) copy-start(bf16[2,176,1408]{2,1,0:T(8,128)(2,1)S(1)} %collective-permute-done.14.rest_7_) | copy-start | bytes 2973700
  82.3 5.7 %copy-start.17 = (bf16[2,176,1408]{2,1,0:T(8,128)(2,1)}, bf16[2,176,1408]{2,1,0:T(8,128)(2,1)S(1)}, u32[]{:S(2)}) copy-start(bf16[2,176,1408]{2,1,0:T(8,128)(2,1)S(1)} %collective-permute-done.12.rest_13_) | copy-start | bytes 2973700
  82.3 5.7 %collective-permute-start.15 = (bf16[2,176,1408]{2,1,0:T(8,128)(2,1)S(1)}, bf16[2,176,1408]{2,1,0:T(8,128)(2,1)S(1)}, u32[]{:S(2)}, u32[]{:S(2)}) collective-permute-start(bf16[2,176,1408]{2,1,0:T(8,128)(2,1)S(1)} %collective-permute-done.13.rest_6_), channel_id=1, source_target_pairs={{0,16},{16,0},{32,48},{48,32},{64,80},{80,64},{96,112},{112,96},{1... | collective-permute-start | bytes 2973704 | tf_op jit(solution)/shard_map/ppermute | solution.py:46
  85.9 4.6 %collective-permute-start.16 = (bf16[2,176,1408]{2,1,0:T(8,128)(2,1)S(1)}, bf16[2,176,1408]{2,1,0:T(8,128)(2,1)}, u32[]{:S(2)}, u32[]{:S(2)}) collective-permute-start(bf16[2,176,1408]{2,1,0:T(8,128)(2,1)S(1)} %collective-permute-done.14.rest_7_), channel_id=1, source_target_pairs={{0,16},{16,0},{32,48},{48,32},{64,80},{80,64},{96,112},{112,96},{1... | collective-permute-start | bytes 2973704 | tf_op jit(solution)/shard_map/ppermute | solution.py:46
  88.0 1.0 copy-start.18
  134.0 22.0 %all-to-all-start.1 = ((f32[32,1,2816]{2,1,0:T(1,128)}), f32[32,1,2816]{2,1,0:T(1,128)S(1)}, u32[]{:S(2)}, u32[]{:S(2)}) async-start(f32[32,1,2816]{2,1,0:T(1,128)} %broadcast_in_dim.5), calls=%async_computation.1 | async-start | bytes 720896 | tf_op jit(solution)/shard_map/all_to_all | solution.py:264

commit v4 on v3

v4 whole, which is shorter than its diff:
```python
import itertools

import jax
import jax.numpy as jnp
from jax import lax
from jax.experimental import pallas as pl
from jax.experimental.pallas import tpu as pltpu
from jax.sharding import PartitionSpec as P

AXES = ("dp", "fsdp")
NX, NY, NZ, NC = 4, 8, 8, 2
YL = 4
W = 2640
SH = 165
SP = 176
WP = 16 * SP
HALF = WP // 2
TOK = 128
TILE = 256
EPS = 1e-06
BF = jnp.bfloat16
F32 = jnp.float32


def line(x, y, z, c):
    x, y, z, c = x % NX, y % NY, z % NZ, c % NC
    return ((y // YL) * NZ * NC + z * NC + c) * 16 + (y % YL) * NX + x


def chips():
    return itertools.product(range(NX), range(NY), range(NZ), range(NC))


def along(first, step):
    pairs = []
    for x, y, z, c in chips():
        in_x = (c == 0) == first
        pairs.append((line(x, y, z, c), line(x + step * in_x, y + step * (not in_x), z, c)))
    return pairs


SWAP = [(line(x, y, z, c), line(x, y, z, 1 - c)) for x, y, z, c in chips()]


def send(array, pairs):
    return lax.ppermute(array, AXES, pairs)


def nt(a, b):
    return lax.dot_general(a, b, (((1,), (1,)), ((), ())), preferred_element_type=F32)


def spread_kernel(place, w_ref, out_ref, wide_ref):
    wide_ref[...] = jnp.zeros_like(wide_ref)
    for t in range(20):
        wide_ref[0:SH, 128 * t : 128 * t + 128] = w_ref[:, 128 * t : 128 * t + 128].astype(F32)
    wide_ref[0:SH, 2560:W] = w_ref[:, 2560:W].astype(F32)
    lane = lax.broadcasted_iota(jnp.int32, (SP, 128), 1)
    for core in range(2):

        @pl.when(place[2] == core)
        def _():
            for t in range(HALF // 128):
                tile = jnp.zeros((SP, 128), F32)
                for j in range(8):
                    low, high = SP * j - 128 * t, SP * j + SH - 128 * t
                    if high <= 0 or low >= 128:
                        continue
                    q = SH * (8 * core + j) - low
                    base = (q // 128) * 128
                    win = wide_ref[:, base : base + 256]
                    moved = pltpu.roll(win, (base - q) % 256, 1)[:, :128]
                    tile = jnp.where((lane >= low) & (lane < high), moved, tile)
                out_ref[:, 128 * t : 128 * t + 128] = tile.astype(BF)

def spread(place, w):
    vm = pl.BlockSpec(memory_space=pltpu.VMEM)
    return pl.pallas_call(
        spread_kernel,
        out_shape=jax.ShapeDtypeStruct((SP, HALF), BF),
        in_specs=[pl.BlockSpec(memory_space=pltpu.SMEM), vm],
        out_specs=vm,
        scratch_shapes=[pltpu.VMEM((SP, 2944), F32)],
        compiler_params=pltpu.CompilerParams(vmem_limit_bytes=16 * 2**20),
    )(place, w)

def prepare_kernel(state_ref, inj_ref, cot_ref, gain_ref, n0_ref, acts_ref, injw_ref, cotw_ref, wide_ref, tall_ref):
    def regroup(src_ref):
        for s in range(16):
            wide_ref[SP * s : SP * s + SH, :] = src_ref[SH * s : SH * s + SH, :]

    for s in range(16):
        wide_ref[SP * s + SH : SP * s + SP, :] = jnp.zeros((SP - SH, TOK), F32)
    regroup(state_ref)
    acc = jnp.zeros((TOK, 128), F32)
    for t in range(WP // 128):
        cols = slice(128 * t, 128 * t + 128)
        s = wide_ref[cols, :].T
        n0_ref[:, cols] = s
        acc = acc + s * s
    inv = lax.rsqrt(jnp.sum(acc, axis=1, keepdims=True) / W + EPS)
    for t in range(WP // 128):
        cols = slice(128 * t, 128 * t + 128)
        n0 = n0_ref[:, cols] * inv
        n0_ref[:, cols] = n0
        acts_ref[0, :, cols] = (n0 * gain_ref[:, cols]).astype(BF)
    regroup(cot_ref)
    for t in range(WP // 128):
        cols = slice(128 * t, 128 * t + 128)
        c = wide_ref[cols, :].T
        cotw_ref[:, cols] = c
        acts_ref[1, :, cols] = c.astype(BF)
    tall_ref[...] = inj_ref[...].astype(F32)
    regroup(tall_ref)
    for t in range(WP // 128):
        cols = slice(128 * t, 128 * t + 128)
        injw_ref[:, cols] = wide_ref[cols, :].T.astype(BF)

def prepare(state, inj, cot, gain):
    vm = pl.BlockSpec(memory_space=pltpu.VMEM)
    wide = lambda dt: jax.ShapeDtypeStruct((TOK, WP), dt)
    return pl.pallas_call(
        prepare_kernel,
        out_shape=(wide(F32), jax.ShapeDtypeStruct((2, TOK, WP), BF), wide(BF), wide(F32)),
        in_specs=[vm] * 4,
        out_specs=(vm,) * 4,
        scratch_shapes=[pltpu.VMEM((WP, TOK), F32), pltpu.VMEM((W, TOK), F32)],
        compiler_params=pltpu.CompilerParams(vmem_limit_bytes=24 * 2**20),
        cost_estimate=pl.CostEstimate(flops=10**6, bytes_accessed=10**7, transcendentals=0),
    )(state.T, inj.T, cot.T, gain)


PLACE = (0, 2, 6, 4)
ALL = 2 * TOK


def half_of(core):
    return pl.ds(pl.multiple_of(core * HALF, 128), HALF)


def first_kernel(place, acts_ref, peer_ref, *rest):
    pieces = rest[:8]
    s_ref, back_ref, give_ref, w_ref, both_ref, sems = rest[8:]
    px, py, pc = place[0], place[1], place[2]
    copies = []
    for k in range(4):
        for j in range(4):
            sx = jnp.where(pc == 0, px + 4 - j, px + 4 - k) % 4
            sy = jnp.where(pc == 0, py + 4 - k, py + 4 - j) % 4
            row = pl.multiple_of((sy * 4 + sx) * SP, SP)
            src = pieces[PLACE[k] + j // 2].at[j % 2]
            copies.append(pltpu.make_async_copy(src, w_ref.at[pl.ds(row, SP), :], sems.at[len(copies)]))
    for c in copies:
        c.start()
    both_ref[:TOK] = acts_ref[0]
    both_ref[TOK:] = peer_ref[0]
    grads = jnp.concatenate([acts_ref[1, :, half_of(pc)], peer_ref[1, :, half_of(pc)]], axis=0)
    for c in copies:
        c.wait()
    s1 = jnp.dot(both_ref[...], w_ref[...], preferred_element_type=F32)
    s_ref[...] = s1[:TOK]
    give_ref[:, :HALF] = s1[TOK:]
    for t in range(2):
        rows = slice(t * HALF, t * HALF + HALF)
        back = nt(grads, w_ref[rows, :])
        back_ref[:, rows] = back[:TOK]
        give_ref[:, HALF + t * HALF : 2 * HALF + t * HALF] = back[TOK:]


def middle_kernel(place, s_ref, back_ref, got_ref, n0_ref, inj_ref, cot_ref, gain_ref, next_ref, injg_ref, part_ref, s1_ref):
    pc, deep = place[2], place[3] >= 2
    mine, other = half_of(pc), half_of(1 - pc)
    s1_ref[:, mine] = s_ref[...] + inj_ref[:, mine].astype(F32)
    s1_ref[:, other] = got_ref[:, :HALF] + inj_ref[:, other].astype(F32)
    acc = jnp.zeros((TOK, 128), F32)
    for t in range(WP // 128):
        s1 = s1_ref[:, 128 * t : 128 * t + 128]
        acc = acc + s1 * s1
    inv1 = lax.rsqrt(jnp.sum(acc, axis=1, keepdims=True) / W + EPS)

    def second(t, acc):
        cols = pl.ds(pl.multiple_of(t * TILE, TILE), TILE)
        n1 = s1_ref[:, cols] * inv1
        back = back_ref[:, cols] + got_ref[:, pl.ds(pl.multiple_of(HALF + t * TILE, 128), TILE)]
        gain = gain_ref[:, cols]
        next_ref[0, :, cols] = (n1 * gain).astype(BF)
        part_ref[:, cols] = jnp.sum(back * jnp.where(deep, n1, n0_ref[:, cols]), axis=0, keepdims=True)
        return acc + back * gain * n1

    acc = lax.fori_loop(0, WP // TILE, second, jnp.zeros((TOK, TILE), F32))
    mean1 = jnp.sum(acc, axis=1, keepdims=True) / W

    def third(t, carry):
        cols = pl.ds(pl.multiple_of(t * TILE, TILE), TILE)
        n1 = s1_ref[:, cols] * inv1
        back = back_ref[:, cols] + got_ref[:, pl.ds(pl.multiple_of(HALF + t * TILE, 128), TILE)]
        d1 = jnp.where(deep, inv1 * (back * gain_ref[:, cols] - n1 * mean1), 0.0)
        next_ref[1, :, cols] = d1.astype(BF)
        injg_ref[:, cols] = (cot_ref[:, cols] + d1).astype(BF)
        return carry

    lax.fori_loop(0, WP // TILE, third, 0)


def last_kernel(place, next_ref, peer_ref, n0_ref, n0_peer_ref, part1_ref, w_ref, s_ref, give_ref, part_ref, both_ref):
    pc = place[2]
    grads = jnp.concatenate([next_ref[1, :, half_of(pc)], peer_ref[1, :, half_of(pc)]], axis=0)
    for t in range(2):
        rows = slice(t * HALF, t * HALF + HALF)
        back = nt(grads, w_ref[rows, :])
        sums = jnp.sum(back[:TOK] * n0_ref[:, rows] + back[TOK:] * n0_peer_ref[:, rows], axis=0, keepdims=True)
        part_ref[:, rows] = part1_ref[:, rows] + sums
    both_ref[:TOK] = next_ref[0]
    both_ref[TOK:] = peer_ref[0]
    s2 = jnp.dot(both_ref[...], w_ref[...], preferred_element_type=F32)
    s_ref[...] = s2[:TOK]
    give_ref[...] = s2[TOK:]


VM = pl.BlockSpec(memory_space=pltpu.VMEM)
SM = pl.BlockSpec(memory_space=pltpu.SMEM)
HB = pl.BlockSpec(memory_space=pl.ANY)


def shape(*dims, dtype=F32):
    return jax.ShapeDtypeStruct(dims, dtype)


def first_call(place, acts, peer, pieces):
    return pl.pallas_call(
        first_kernel,
        out_shape=(shape(TOK, HALF), shape(TOK, WP), shape(TOK, HALF + WP), shape(WP, HALF, dtype=BF)),
        in_specs=[SM, VM, VM] + [HB] * 8,
        out_specs=(VM,) * 4,
        scratch_shapes=[pltpu.VMEM((ALL, WP), BF), pltpu.SemaphoreType.DMA((16,))],
        compiler_params=pltpu.CompilerParams(vmem_limit_bytes=24 * 2**20),
        cost_estimate=pl.CostEstimate(flops=8 * TOK * WP * HALF, bytes_accessed=2 * WP * HALF, transcendentals=0),
    )(place, acts, peer, *pieces)


def middle_call(place, s_own, back, got, n0, inj, cot, gain):
    return pl.pallas_call(
        middle_kernel,
        out_shape=(shape(2, TOK, WP, dtype=BF), shape(TOK, WP, dtype=BF), shape(1, WP), shape(TOK, WP)),
        in_specs=[SM] + [VM] * 7,
        out_specs=(VM,) * 4,
        compiler_params=pltpu.CompilerParams(vmem_limit_bytes=20 * 2**20),
        cost_estimate=pl.CostEstimate(flops=20 * TOK * WP, bytes_accessed=10**7, transcendentals=0),
    )(place, s_own, back, got, n0, inj, cot, gain)


def last_call(place, nexts, peer, n0, n0_peer, part1, w):
    return pl.pallas_call(
        last_kernel,
        out_shape=(shape(TOK, HALF), shape(TOK, HALF), shape(1, WP)),
        in_specs=[SM] + [VM] * 6,
        out_specs=(VM,) * 3,
        scratch_shapes=[pltpu.VMEM((ALL, WP), BF)],
        compiler_params=pltpu.CompilerParams(vmem_limit_bytes=24 * 2**20),
        cost_estimate=pl.CostEstimate(flops=8 * TOK * WP * HALF, bytes_accessed=2 * WP * HALF, transcendentals=0),
    )(place, nexts, peer, n0, n0_peer, part1, w)


def narrow(array):
    return array.T.reshape(16, SP, -1)[:, :SH].reshape(W, -1).T


def gather(own, acts):
    down = send(own, along(True, -1))
    up = send(own, along(True, 1))
    far = send(own, along(True, 2))
    acts, down, up, far = lax.optimization_barrier((acts, down, up, far))
    low = jnp.stack([own, up])
    high = jnp.stack([far, down])
    low3 = send(low, along(False, -1))
    high1 = send(high, along(False, 1))
    high3 = send(high, along(False, -1))
    low1 = send(low, along(False, 1))
    high2 = send(high3, along(False, -1))
    low2 = send(low1, along(False, 1))
    return acts, (low, high, low1, high1, low3, high3, low2, high2)


def total(part):
    dp_groups = [[yh * 16 + z * 2 + c for z in range(8) for c in range(2)] for yh in range(2)]
    got = lax.all_to_all(jnp.broadcast_to(part, (16, WP)), "dp", 0, 0, axis_index_groups=dp_groups)
    part = jnp.sum(got.reshape(16, WP), axis=0, keepdims=True)
    planes = [[line(x, y, z, c) for y in range(NY) for x in range(NX)] for z in range(NZ) for c in range(NC)]
    got = lax.all_to_all(jnp.broadcast_to(part, (32, WP)), AXES, 0, 0, axis_index_groups=planes)
    return jnp.sum(got.reshape(32, WP), axis=0, keepdims=True)


def shards(state0, injected, core_weight, gain, counts, cotangent):
    dp, fs = lax.axis_index("dp"), lax.axis_index("fsdp")
    pc = dp % 2
    place = jnp.stack([fs % 4, fs // 4, pc, counts[0]]).astype(jnp.int32)
    gain_w = jnp.pad(gain.reshape(16, SH), ((0, 0), (0, SP - SH))).reshape(1, WP)
    acts = prepare(state0, injected, cotangent, gain_w)
    (n0, acts, inj, cot), pieces = gather(spread(place, core_weight), acts)
    peer, n0_peer = lax.optimization_barrier((send(acts, SWAP), send(n0, SWAP)))
    s_own, back, give, half = first_call(place, acts, peer, pieces)
    nexts, injg, part1, s1 = middle_call(place, s_own, back, send(give, SWAP), n0, inj, cot, gain_w)
    s_own, give, part = last_call(place, nexts, send(nexts, SWAP), n0, n0_peer, part1, half)
    got = send(give, SWAP)
    s2 = jnp.where(pc == 0, jnp.concatenate([s_own, got], axis=1), jnp.concatenate([got, s_own], axis=1))
    final = jnp.where(counts[0] >= 2, s2 + inj.astype(F32), s1).astype(BF)
    return (narrow(final), narrow(injg), narrow(total(part)).reshape(W))


def solution(mesh):
    rows = P(AXES, None)
    return jax.shard_map(
        shards,
        mesh=mesh,
        in_specs=(rows, rows, P("fsdp", None), P(), P(AXES), rows),
        out_specs=(rows, rows, P()),
        check_vma=False,
    )
```

time: 158 us -> 156 us (0.987)
  blocking collectives: 20.2 us -> 0 us
  waiting for transfers between devices: 40.1 us -> 47.4 us
  local copies, waits for them, and re-layouts: 10.2 us -> 16.8 us
  other arithmetic: 0.65 us -> 4.49 us
  starting transfers between devices: 59.4 us -> 61.8 us
    all_to_all x1 -> x0, blocking collectives: 20.2 us -> none  [total(): lax.all_to_all(jnp.broadcast_to(part, (16, WP)), 'dp', 0, 0, axis_index_g...]
    all_to_all x0 -> x1, starting transfers between devices: none -> 9.85 us  [total(): lax.all_to_all(jnp.broadcast_to(part, (16, WP)), 'dp', 0, 0, axis_index_g...]
    ppermute x17 -> x14, starting transfers between devices: 51.5 us -> 42.2 us  [send(): return lax.ppermute(array, AXES, pairs)]
    ppermute x17 -> x14, waiting for transfers between devices: 28.9 us -> 35 us  [send(): return lax.ppermute(array, AXES, pairs)]
    all_to_all x0 -> x1, waiting for transfers between devices: none -> 3.55 us  [total(): lax.all_to_all(jnp.broadcast_to(part, (16, WP)), 'dp', 0, 0, axis_index_g...]
    transpose x2, local copies, waits for them, and re-layouts: 0.7 us -> 3.71 us  [narrow(): return array.T.reshape(16, SP, -1)[:, :SH].reshape(W, -1).T]
    transpose x0 -> x1, other arithmetic: none -> 2.66 us  [narrow(): return array.T.reshape(16, SP, -1)[:, :SH].reshape(W, -1).T]
    all_to_all x1, waiting for transfers between devices: 11.2 us -> 8.87 us  [total(): lax.all_to_all(jnp.broadcast_to(part, (32, WP)), AXES, 0, 0, axis_index_g...]
  transfers between devices with their start and end apart: 18 -> 16, of which waited for: 8 -> 10; matrix products, arithmetic and copies ran while one was open for 2% -> 10% of each run, Pallas kernels for 1% -> 1%
where the time goes in v4:
time: 156 us; the launch traced here: 155 us
  starting transfers between devices  61.8 us (40%)
  waiting for transfers between devices  47.4 us (30%)
  Pallas kernels  23.1 us (15%)
  local copies, waits for them, and re-layouts  16.8 us (11%)
  other arithmetic  4.49 us (3%)
  between operations  1.68 us (1%)
    ppermute x14, starting transfers between devices, send(): return lax.ppermute(array, AXES, pairs)  42.2 us
    ppermute x14, waiting for transfers between devices, send(): return lax.ppermute(array, AXES, pairs)  35 us
    pallas_call x1, Pallas kernels, first_call(): pl.pallas_call(first_kernel, out_shape=(shape(TOK, HALF), shape(TOK, WP),...  11.8 us
    all_to_all x1, starting transfers between devices, total(): lax.all_to_all(jnp.broadcast_to(part, (16, WP)), 'dp', 0, 0, axis_index_g...  9.85 us
    all_to_all x1, starting transfers between devices, total(): lax.all_to_all(jnp.broadcast_to(part, (32, WP)), AXES, 0, 0, axis_index_g...  9.72 us
    all_to_all x1, waiting for transfers between devices, total(): lax.all_to_all(jnp.broadcast_to(part, (32, WP)), AXES, 0, 0, axis_index_g...  8.87 us
    pallas_call x1, Pallas kernels, last_call(): pl.pallas_call(last_kernel, out_shape=(shape(TOK, HALF), shape(TOK, HALF)...  6.45 us
    unnamed x10, local copies, waits for them, and re-layouts  4.46 us
  transfers between devices with their start and end apart: 16, of which 10 were waited for; matrix products, arithmetic and copies ran while one was open for 10% of the time, Pallas kernels for 1%

profile of v4, /device:TPU:1, one launch (start us, length us, event | category | flops | bytes accessed | tf_op | source)
XLA Modules:
  0.0 155.3 jit_solution(10383644405671085389)
XLA Ops:
  1.5 1.2 copy-done.2
  2.7 1.2 shard_map.86
  3.8 5.0 %collective-permute-start.2 = (bf16[176,1408]{1,0:T(8,128)(2,1)S(1)}, bf16[176,1408]{1,0:T(8,128)(2,1)}, u32[]{:S(2)}, u32[]{:S(2)}) collective-permute-start(bf16[176,1408]{1,0:T(8,128)(2,1)S(1)} %shard_map.86), channel_id=1, source_target_pairs={{0,2},{16,24},{32,34},{48,56},{64,66},{80,88},{96,98},{112,120},{1... | collective-permute-start | bytes 1486856 | tf_op jit(solution)/shard_map/ppermute | solution.py:46
  8.9 3.2 %collective-permute-start.1 = (bf16[176,1408]{1,0:T(8,128)(2,1)S(1)}, bf16[176,1408]{1,0:T(8,128)(2,1)S(1)}, u32[]{:S(2)}, u32[]{:S(2)}) collective-permute-start(bf16[176,1408]{1,0:T(8,128)(2,1)S(1)} %shard_map.86), channel_id=1, source_target_pairs={{0,1},{16,20},{32,33},{48,52},{64,65},{80,84},{96,97},{112,116},{1... | collective-permute-start | bytes 1486856 | tf_op jit(solution)/shard_map/ppermute | solution.py:46
  12.1 3.3 %collective-permute-start = (bf16[176,1408]{1,0:T(8,128)(2,1)S(1)}, bf16[176,1408]{1,0:T(8,128)(2,1)}, u32[]{:S(2)}, u32[]{:S(2)}) collective-permute-start(bf16[176,1408]{1,0:T(8,128)(2,1)S(1)} %shard_map.86), channel_id=1, source_target_pairs={{0,3},{16,284},{32,35},{48,316},{64,67},{80,348},{96,99},{112,380}... | collective-permute-start | bytes 1486856 | tf_op jit(solution)/shard_map/ppermute | solution.py:46
  15.4 0.8 reshape.38
  16.3 1.3 copy-done.1
  17.7 1.1 copy-done.4
  18.8 1.4 shard_map.85
  20.2 7.2 %collective-permute-done.1 = bf16[176,1408]{1,0:T(8,128)(2,1)S(1)} collective-permute-done((bf16[176,1408]{1,0:T(8,128)(2,1)S(1)}, bf16[176,1408]{1,0:T(8,128)(2,1)S(1)}, u32[]{:S(2)}, u32[]{:S(2)}) %collective-permute-start.1) | collective-permute-done | bytes 495648 | tf_op jit(solution)/shard_map/ppermute | solution.py:46
  27.4 2.7 %collective-permute-start.3 = (bf16[2,128,2816]{2,1,0:T(8,128)(2,1)S(1)}, bf16[2,128,2816]{2,1,0:T(8,128)(2,1)S(1)}, u32[]{:S(2)}, u32[]{:S(2)}) collective-permute-start(bf16[2,128,2816]{2,1,0:T(8,128)(2,1)S(1)} %get-tuple-element.31.acts_ref), channel_id=1, source_target_pairs={{0,16},{16,0},{32,48},{48,32},{64,80},{80,64},{96,112},{112,96},{1... | collective-permute-start | bytes 4325384 | tf_op jit(solution)/shard_map/ppermute | solution.py:46
  30.2 1.3 pad_maximum_fusion.1.rest_1_
  31.5 3.3 %collective-permute-start.8 = (bf16[2,176,1408]{2,1,0:T(8,128)(2,1)S(1)}, bf16[2,176,1408]{2,1,0:T(8,128)(2,1)S(1)}, u32[]{:S(2)}, u32[]{:S(2)}) collective-permute-start(bf16[2,176,1408]{2,1,0:T(8,128)(2,1)S(1)} %pad_maximum_fusion.1.rest_1_), channel_id=1, source_target_pairs={{0,268},{16,19},{32,300},{48,51},{64,332},{80,83},{96,364},{112,11... | collective-permute-start | bytes 2973704 | tf_op jit(solution)/shard_map/ppermute | solution.py:46
  34.9 2.0 %collective-permute-start.5 = (bf16[2,176,1408]{2,1,0:T(8,128)(2,1)S(1)}, bf16[2,176,1408]{2,1,0:T(8,128)(2,1)S(1)}, u32[]{:S(2)}, u32[]{:S(2)}) collective-permute-start(bf16[2,176,1408]{2,1,0:T(8,128)(2,1)S(1)} %pad_maximum_fusion.rest_0_), channel_id=1, source_target_pairs={{0,4},{16,17},{32,36},{48,49},{64,68},{80,81},{96,100},{112,113},{... | collective-permute-start | bytes 2973704 | tf_op jit(solution)/shard_map/ppermute | solution.py:46
  36.9 2.5 %collective-permute-start.4 = (f32[128,2816]{1,0:T(8,128)S(1)}, f32[128,2816]{1,0:T(8,128)S(1)}, u32[]{:S(2)}, u32[]{:S(2)}) collective-permute-start(f32[128,2816]{1,0:T(8,128)S(1)} %get-tuple-element.32.n0_ref), channel_id=1, source_target_pairs={{0,16},{16,0},{32,48},{48,32},{64,80},{80,64},{96,112},{112,96},{1... | collective-permute-start | bytes 4325384 | tf_op jit(solution)/shard_map/ppermute | solution.py:46
  39.4 2.5 %collective-permute-start.6 = (bf16[2,176,1408]{2,1,0:T(8,128)(2,1)S(1)}, bf16[2,176,1408]{2,1,0:T(8,128)(2,1)S(1)}, u32[]{:S(2)}, u32[]{:S(2)}) collective-permute-start(bf16[2,176,1408]{2,1,0:T(8,128)(2,1)S(1)} %pad_maximum_fusion.1.rest_1_), channel_id=1, source_target_pairs={{0,4},{16,17},{32,36},{48,49},{64,68},{80,81},{96,100},{112,113},{... | collective-permute-start | bytes 2973704 | tf_op jit(solution)/shard_map/ppermute | solution.py:46
  41.9 4.8 %collective-permute-done.8.rest_5_ = bf16[2,176,1408]{2,1,0:T(8,128)(2,1)S(1)} collective-permute-done((bf16[2,176,1408]{2,1,0:T(8,128)(2,1)S(1)}, bf16[2,176,1408]{2,1,0:T(8,128)(2,1)S(1)}, u32[]{:S(2)}, u32[]{:S(2)}) %collective-permute-start.8) | collective-permute-done | bytes 991264 | tf_op jit(solution)/shard_map/ppermute | solution.py:46
  46.7 4.5 %collective-permute-start.7 = (bf16[2,176,1408]{2,1,0:T(8,128)(2,1)S(1)}, bf16[2,176,1408]{2,1,0:T(8,128)(2,1)S(1)}, u32[]{:S(2)}, u32[]{:S(2)}) collective-permute-start(bf16[2,176,1408]{2,1,0:T(8,128)(2,1)S(1)} %pad_maximum_fusion.rest_0_), channel_id=1, source_target_pairs={{0,268},{16,19},{32,300},{48,51},{64,332},{80,83},{96,364},{112,11... | collective-permute-start | bytes 2973704 | tf_op jit(solution)/shard_map/ppermute | solution.py:46
  51.2 0.1 collective-permute-done.5.rest_2_
  51.3 1.9 %collective-permute-start.10 = (bf16[2,176,1408]{2,1,0:T(8,128)(2,1)S(1)}, bf16[2,176,1408]{2,1,0:T(8,128)(2,1)S(1)}, u32[]{:S(2)}, u32[]{:S(2)}) collective-permute-start(bf16[2,176,1408]{2,1,0:T(8,128)(2,1)S(1)} %collective-permute-done.8.rest_5_), channel_id=1, source_target_pairs={{0,268},{16,19},{32,300},{48,51},{64,332},{80,83},{96,364},{112,11... | collective-permute-start | bytes 2973704 | tf_op jit(solution)/shard_map/ppermute | solution.py:46
  53.2 3.4 %collective-permute-start.9 = (bf16[2,176,1408]{2,1,0:T(8,128)(2,1)S(1)}, bf16[2,176,1408]{2,1,0:T(8,128)(2,1)S(1)}, u32[]{:S(2)}, u32[]{:S(2)}) collective-permute-start(bf16[2,176,1408]{2,1,0:T(8,128)(2,1)S(1)} %collective-permute-done.5.rest_2_), channel_id=1, source_target_pairs={{0,4},{16,17},{32,36},{48,49},{64,68},{80,81},{96,100},{112,113},{... | collective-permute-start | bytes 2973704 | tf_op jit(solution)/shard_map/ppermute | solution.py:46
  56.6 5.3 %collective-permute-done.6.rest_3_ = bf16[2,176,1408]{2,1,0:T(8,128)(2,1)S(1)} collective-permute-done((bf16[2,176,1408]{2,1,0:T(8,128)(2,1)S(1)}, bf16[2,176,1408]{2,1,0:T(8,128)(2,1)S(1)}, u32[]{:S(2)}, u32[]{:S(2)}) %collective-permute-start.6) | collective-permute-done | bytes 991264 | tf_op jit(solution)/shard_map/ppermute | solution.py:46
  61.9 0.4 collective-permute-done.7.rest_4_
  62.3 10.6 %collective-permute-done.10.rest_7_ = bf16[2,176,1408]{2,1,0:T(8,128)(2,1)S(1)} collective-permute-done((bf16[2,176,1408]{2,1,0:T(8,128)(2,1)S(1)}, bf16[2,176,1408]{2,1,0:T(8,128)(2,1)S(1)}, u32[]{:S(2)}, u32[]{:S(2)}) %collective-permute-start.10) | collective-permute-done | bytes 991264 | tf_op jit(solution)/shard_map/ppermute | solution.py:46
  72.9 11.8 %shard_map.87 = (f32[128,1408]{1,0:T(8,128)S(1)}, f32[128,2816]{1,0:T(8,128)S(1)}, f32[128,4224]{1,0:T(8,128)S(1)}, bf16[2816,1408]{1,0:T(8,128)(2,1)S(1)}) custom-call(s32[4]{0:T(128)S(1)} %pad_add_fusion.place, bf16[2,128,2816]{2,1,0:T(8,128)(2,1)S(1)} %get-tuple-element.31.acts_ref, bf16[2,128,2816]{2,1,0:T(8,128)(2,1)S(1)} %collective-permute-done.3.peer_ref, ...), custom_call_target="tpu_custom_call" | custom-call | flops 4060086272 | bytes 7929856 | tf_op jit(solution)/shard_map/pallas_call | solution.py:230
  84.7 3.3 %collective-permute-start.11 = (f32[128,4224]{1,0:T(8,128)S(1)}, f32[128,4224]{1,0:T(8,128)S(1)}, u32[]{:S(2)}, u32[]{:S(2)}) collective-permute-start(f32[128,4224]{1,0:T(8,128)S(1)} %get-tuple-element.39), channel_id=1, source_target_pairs={{0,16},{16,0},{32,48},{48,32},{64,80},{80,64},{96,112},{112,96},{1... | collective-permute-start | bytes 6488072 | tf_op jit(solution)/shard_map/ppermute | solution.py:46
  88.0 3.9 %collective-permute-done.11.got_ref = f32[128,4224]{1,0:T(8,128)S(1)} collective-permute-done((f32[128,4224]{1,0:T(8,128)S(1)}, f32[128,4224]{1,0:T(8,128)S(1)}, u32[]{:S(2)}, u32[]{:S(2)}) %collective-permute-start.11) | collective-permute-done | bytes 2162720 | tf_op jit(solution)/shard_map/ppermute | solution.py:46
  91.8 2.3 %shard_map.88 = (bf16[2,128,2816]{2,1,0:T(8,128)(2,1)S(1)}, bf16[128,2816]{1,0:T(8,128)(2,1)S(1)}, f32[1,2816]{1,0:T(1,128)S(1)}, f32[128,2816]{1,0:T(8,128)S(1)}) custom-call(s32[4]{0:T(128)S(1)} %pad_add_fusion.place, f32[128,1408]{1,0:T(8,128)S(1)} %get-tuple-element.37.s_ref, f32[128,2816]{1,0:T(8,128)S(1)} %get-tuple-element.38.back_ref, ...), custom_call_target="tpu_custom_call" | custom-call | flops 7208960 | bytes 10000000 | tf_op jit(solution)/shard_map/pallas_call | solution.py:242
  94.1 0.9 copy-done.3
  95.0 2.5 %collective-permute-start.12 = (bf16[2,128,2816]{2,1,0:T(8,128)(2,1)S(1)}, bf16[2,128,2816]{2,1,0:T(8,128)(2,1)S(1)}, u32[]{:S(2)}, u32[]{:S(2)}) collective-permute-start(bf16[2,128,2816]{2,1,0:T(8,128)(2,1)S(1)} %get-tuple-element.42.next_ref), channel_id=1, source_target_pairs={{0,16},{16,0},{32,48},{48,32},{64,80},{80,64},{96,112},{112,96},{1... | collective-permute-start | bytes 4325384 | tf_op jit(solution)/shard_map/ppermute | solution.py:46
  97.4 2.6 %collective-permute-done.12.peer_ref = bf16[2,128,2816]{2,1,0:T(8,128)(2,1)S(1)} collective-permute-done((bf16[2,128,2816]{2,1,0:T(8,128)(2,1)S(1)}, bf16[2,128,2816]{2,1,0:T(8,128)(2,1)S(1)}, u32[]{:S(2)}, u32[]{:S(2)}) %collective-permute-start.12) | collective-permute-done | bytes 1441824 | tf_op jit(solution)/shard_map/ppermute | solution.py:46
  100.1 6.5 %shard_map.89 = (f32[128,1408]{1,0:T(8,128)S(1)}, f32[128,1408]{1,0:T(8,128)}, f32[1,2816]{1,0:T(1,128)S(1)}) custom-call(s32[4]{0:T(128)S(1)} %pad_add_fusion.place, bf16[2,128,2816]{2,1,0:T(8,128)(2,1)S(1)} %get-tuple-element.42.next_ref, bf16[2,128,2816]{2,1,0:T(8,128)(2,1)S(1)} %collective-permute-done.12.peer_ref, ...), custom_call_target="tpu_custom_call" | custom-call | flops 4060086272 | bytes 7929856 | tf_op jit(solution)/shard_map/pallas_call | solution.py:253
  106.5 2.3 %collective-permute-start.13 = (f32[128,1408]{1,0:T(8,128)}, f32[128,1408]{1,0:T(8,128)}, u32[]{:S(2)}, u32[]{:S(2)}) collective-permute-start(f32[128,1408]{1,0:T(8,128)} %get-tuple-element.47), channel_id=1, source_target_pairs={{0,16},{16,0},{32,48},{48,32},{64,80},{80,64},{96,112},{112,96},{1... | collective-permute-start | bytes 2162696 | tf_op jit(solution)/shard_map/ppermute | solution.py:46
  108.8 0.8 broadcast_in_dim.4
  109.6 9.9 %all-to-all-start = ((f32[16,1,2816]{2,1,0:T(1,128)}), f32[16,1,2816]{2,1,0:T(1,128)S(1)}, u32[]{:S(2)}, u32[]{:S(2)}) async-start(f32[16,1,2816]{2,1,0:T(1,128)} %broadcast_in_dim.4), calls=%async_computation | async-start | bytes 360448 | tf_op jit(solution)/shard_map/all_to_all | solution.py:286
  119.4 2.3 %copy.16 = bf16[2816,128]{1,0:T(8,128)(2,1)} copy(bf16[2816,128]{0,1:T(8,128)(2,1)} %bitcast.24) | data formatting | bytes 1441792 | tf_op jit(solution)/shard_map/transpose | solution.py:265
  121.7 2.0 %slice.13 = bf16[16,165,128]{2,1,0:T(8,128)(2,1)} slice(bf16[16,176,128]{2,1,0:T(8,128)(2,1)} %bitcast.26), slice={[0:16], [0:165], [0:128]} | slice | bytes 1351680 | tf_op jit(solution)/shard_map/slice | solution.py:265
  123.7 2.1 %reshape.43 = bf16[2640,128]{1,0:T(8,128)(2,1)} reshape(bf16[16,165,128]{2,1,0:T(8,128)(2,1)} %slice.13) | data formatting | bytes 1351680 | tf_op jit(solution)/shard_map/reshape | solution.py:265
  125.9 3.6 %all-to-all-done = f32[16,1,2816]{2,1,0:T(1,128)S(1)} async-done(((f32[16,1,2816]{2,1,0:T(1,128)}), f32[16,1,2816]{2,1,0:T(1,128)S(1)}, u32[]{:S(2)}, u32[]{:S(2)}) %all-to-all-start) | async-done | bytes 180256 | tf_op jit(solution)/shard_map/all_to_all | solution.py:286
  129.4 0.1 reduce_sum.18
  129.5 0.9 broadcast_in_dim.5
  130.5 9.7 %all-to-all-start.1 = ((f32[32,1,2816]{2,1,0:T(1,128)}), f32[32,1,2816]{2,1,0:T(1,128)S(1)}, u32[]{:S(2)}, u32[]{:S(2)}) async-start(f32[32,1,2816]{2,1,0:T(1,128)} %broadcast_in_dim.5), calls=%async_computation.1 | async-start | bytes 720896 | tf_op jit(solution)/shard_map/all_to_all | solution.py:289
  140.2 2.7 %fusion.3 = bf16[2816,128]{0,1:T(8,128)(2,1)} fusion(f32[128,2816]{1,0:T(8,128)S(1)} %get-tuple-element.48, bf16[128,2816]{1,0:T(8,128)(2,1)S(1)} %get-tuple-element.40.inj_ref, f32[128,1408]{1,0:T(8,128)S(1)} %get-tuple-element.46, f32[128,1408]{1,0:T(8,128)} %collective-permute-done.13, pred[]{:T(512)S(6)} %eq.6, pred[]{:T(512)} %bitcast), kind=kLoop, calls=%fused_computation.6 | loop fusion | flops 2162688 | bytes 4325378 | tf_op jit(solution)/shard_map/transpose | solution.py:265
  142.9 1.5 copy.15
  144.4 1.1 reshape.41
  145.4 8.9 %all-to-all-done.1 = f32[32,1,2816]{2,1,0:T(1,128)S(1)} async-done(((f32[32,1,2816]{2,1,0:T(1,128)}), f32[32,1,2816]{2,1,0:T(1,128)S(1)}, u32[]{:S(2)}, u32[]{:S(2)}) %all-to-all-start.1) | async-done | bytes 360480 | tf_op jit(solution)/shard_map/all_to_all | solution.py:289
  154.3 0.2 reduce_sum.19
  154.6 0.7 reshape_transpose_reshape.3
  (19 shorter events, 0.5 us)
Async XLA Ops:
  0.6 15.7 %copy-start = (f32[128,2640]{0,1:T(8,128)S(1)}, f32[128,2640]{0,1:T(8,128)}, u32[]{:S(2)}) copy-start(f32[128,2640]{0,1:T(8,128)} %param.6) | copy-start | bytes 4055044
  1.5 1.2 copy-start.2
  3.8 16.4 %collective-permute-start.2 = (bf16[176,1408]{1,0:T(8,128)(2,1)S(1)}, bf16[176,1408]{1,0:T(8,128)(2,1)}, u32[]{:S(2)}, u32[]{:S(2)}) collective-permute-start(bf16[176,1408]{1,0:T(8,128)(2,1)S(1)} %shard_map.86), channel_id=1, source_target_pairs={{0,2},{16,24},{32,34},{48,56},{64,66},{80,88},{96,98},{112,120},{1... | collective-permute-start | bytes 1486856 | tf_op jit(solution)/shard_map/ppermute | solution.py:46
  8.9 18.5 %collective-permute-start.1 = (bf16[176,1408]{1,0:T(8,128)(2,1)S(1)}, bf16[176,1408]{1,0:T(8,128)(2,1)S(1)}, u32[]{:S(2)}, u32[]{:S(2)}) collective-permute-start(bf16[176,1408]{1,0:T(8,128)(2,1)S(1)} %shard_map.86), channel_id=1, source_target_pairs={{0,1},{16,20},{32,33},{48,52},{64,65},{80,84},{96,97},{112,116},{1... | collective-permute-start | bytes 1486856 | tf_op jit(solution)/shard_map/ppermute | solution.py:46
  12.1 15.3 %collective-permute-start = (bf16[176,1408]{1,0:T(8,128)(2,1)S(1)}, bf16[176,1408]{1,0:T(8,128)(2,1)}, u32[]{:S(2)}, u32[]{:S(2)}) collective-permute-start(bf16[176,1408]{1,0:T(8,128)(2,1)S(1)} %shard_map.86), channel_id=1, source_target_pairs={{0,3},{16,284},{32,35},{48,316},{64,67},{80,348},{96,99},{112,380}... | collective-permute-start | bytes 1486856 | tf_op jit(solution)/shard_map/ppermute | solution.py:46
  16.3 1.3 copy-start.1
  17.7 1.1 copy-start.4
  27.4 25.8 %collective-permute-start.3 = (bf16[2,128,2816]{2,1,0:T(8,128)(2,1)S(1)}, bf16[2,128,2816]{2,1,0:T(8,128)(2,1)S(1)}, u32[]{:S(2)}, u32[]{:S(2)}) collective-permute-start(bf16[2,128,2816]{2,1,0:T(8,128)(2,1)S(1)} %get-tuple-element.31.acts_ref), channel_id=1, source_target_pairs={{0,16},{16,0},{32,48},{48,32},{64,80},{80,64},{96,112},{112,96},{1... | collective-permute-start | bytes 4325384 | tf_op jit(solution)/shard_map/ppermute | solution.py:46
  31.5 15.2 %collective-permute-start.8 = (bf16[2,176,1408]{2,1,0:T(8,128)(2,1)S(1)}, bf16[2,176,1408]{2,1,0:T(8,128)(2,1)S(1)}, u32[]{:S(2)}, u32[]{:S(2)}) collective-permute-start(bf16[2,176,1408]{2,1,0:T(8,128)(2,1)S(1)} %pad_maximum_fusion.1.rest_1_), channel_id=1, source_target_pairs={{0,268},{16,19},{32,300},{48,51},{64,332},{80,83},{96,364},{112,11... | collective-permute-start | bytes 2973704 | tf_op jit(solution)/shard_map/ppermute | solution.py:46
  34.9 16.4 %collective-permute-start.5 = (bf16[2,176,1408]{2,1,0:T(8,128)(2,1)S(1)}, bf16[2,176,1408]{2,1,0:T(8,128)(2,1)S(1)}, u32[]{:S(2)}, u32[]{:S(2)}) collective-permute-start(bf16[2,176,1408]{2,1,0:T(8,128)(2,1)S(1)} %pad_maximum_fusion.rest_0_), channel_id=1, source_target_pairs={{0,4},{16,17},{32,36},{48,49},{64,68},{80,81},{96,100},{112,113},{... | collective-permute-start | bytes 2973704 | tf_op jit(solution)/shard_map/ppermute | solution.py:46
  36.9 19.7 %collective-permute-start.4 = (f32[128,2816]{1,0:T(8,128)S(1)}, f32[128,2816]{1,0:T(8,128)S(1)}, u32[]{:S(2)}, u32[]{:S(2)}) collective-permute-start(f32[128,2816]{1,0:T(8,128)S(1)} %get-tuple-element.32.n0_ref), channel_id=1, source_target_pairs={{0,16},{16,0},{32,48},{48,32},{64,80},{80,64},{96,112},{112,96},{1... | collective-permute-start | bytes 4325384 | tf_op jit(solution)/shard_map/ppermute | solution.py:46
  39.4 22.5 %collective-permute-start.6 = (bf16[2,176,1408]{2,1,0:T(8,128)(2,1)S(1)}, bf16[2,176,1408]{2,1,0:T(8,128)(2,1)S(1)}, u32[]{:S(2)}, u32[]{:S(2)}) collective-permute-start(bf16[2,176,1408]{2,1,0:T(8,128)(2,1)S(1)} %pad_maximum_fusion.1.rest_1_), channel_id=1, source_target_pairs={{0,4},{16,17},{32,36},{48,49},{64,68},{80,81},{96,100},{112,113},{... | collective-permute-start | bytes 2973704 | tf_op jit(solution)/shard_map/ppermute | solution.py:46
  46.7 15.6 %collective-permute-start.7 = (bf16[2,176,1408]{2,1,0:T(8,128)(2,1)S(1)}, bf16[2,176,1408]{2,1,0:T(8,128)(2,1)S(1)}, u32[]{:S(2)}, u32[]{:S(2)}) collective-permute-start(bf16[2,176,1408]{2,1,0:T(8,128)(2,1)S(1)} %pad_maximum_fusion.rest_0_), channel_id=1, source_target_pairs={{0,268},{16,19},{32,300},{48,51},{64,332},{80,83},{96,364},{112,11... | collective-permute-start | bytes 2973704 | tf_op jit(solution)/shard_map/ppermute | solution.py:46
  51.3 21.6 %collective-permute-start.10 = (bf16[2,176,1408]{2,1,0:T(8,128)(2,1)S(1)}, bf16[2,176,1408]{2,1,0:T(8,128)(2,1)S(1)}, u32[]{:S(2)}, u32[]{:S(2)}) collective-permute-start(bf16[2,176,1408]{2,1,0:T(8,128)(2,1)S(1)} %collective-permute-done.8.rest_5_), channel_id=1, source_target_pairs={{0,268},{16,19},{32,300},{48,51},{64,332},{80,83},{96,364},{112,11... | collective-permute-start | bytes 2973704 | tf_op jit(solution)/shard_map/ppermute | solution.py:46
  53.2 19.7 %collective-permute-start.9 = (bf16[2,176,1408]{2,1,0:T(8,128)(2,1)S(1)}, bf16[2,176,1408]{2,1,0:T(8,128)(2,1)S(1)}, u32[]{:S(2)}, u32[]{:S(2)}) collective-permute-start(bf16[2,176,1408]{2,1,0:T(8,128)(2,1)S(1)} %collective-permute-done.5.rest_2_), channel_id=1, source_target_pairs={{0,4},{16,17},{32,36},{48,49},{64,68},{80,81},{96,100},{112,113},{... | collective-permute-start | bytes 2973704 | tf_op jit(solution)/shard_map/ppermute | solution.py:46
  84.7 7.1 %collective-permute-start.11 = (f32[128,4224]{1,0:T(8,128)S(1)}, f32[128,4224]{1,0:T(8,128)S(1)}, u32[]{:S(2)}, u32[]{:S(2)}) collective-permute-start(f32[128,4224]{1,0:T(8,128)S(1)} %get-tuple-element.39), channel_id=1, source_target_pairs={{0,16},{16,0},{32,48},{48,32},{64,80},{80,64},{96,112},{112,96},{1... | collective-permute-start | bytes 6488072 | tf_op jit(solution)/shard_map/ppermute | solution.py:46
  94.1 0.9 copy-start.3
  95.0 5.1 %collective-permute-start.12 = (bf16[2,128,2816]{2,1,0:T(8,128)(2,1)S(1)}, bf16[2,128,2816]{2,1,0:T(8,128)(2,1)S(1)}, u32[]{:S(2)}, u32[]{:S(2)}) collective-permute-start(bf16[2,128,2816]{2,1,0:T(8,128)(2,1)S(1)} %get-tuple-element.42.next_ref), channel_id=1, source_target_pairs={{0,16},{16,0},{32,48},{48,32},{64,80},{80,64},{96,112},{112,96},{1... | collective-permute-start | bytes 4325384 | tf_op jit(solution)/shard_map/ppermute | solution.py:46
  106.5 33.7 %collective-permute-start.13 = (f32[128,1408]{1,0:T(8,128)}, f32[128,1408]{1,0:T(8,128)}, u32[]{:S(2)}, u32[]{:S(2)}) collective-permute-start(f32[128,1408]{1,0:T(8,128)} %get-tuple-element.47), channel_id=1, source_target_pairs={{0,16},{16,0},{32,48},{48,32},{64,80},{80,64},{96,112},{112,96},{1... | collective-permute-start | bytes 2162696 | tf_op jit(solution)/shard_map/ppermute | solution.py:46
  109.6 19.8 %all-to-all-start = ((f32[16,1,2816]{2,1,0:T(1,128)}), f32[16,1,2816]{2,1,0:T(1,128)S(1)}, u32[]{:S(2)}, u32[]{:S(2)}) async-start(f32[16,1,2816]{2,1,0:T(1,128)} %broadcast_in_dim.4), calls=%async_computation | async-start | bytes 360448 | tf_op jit(solution)/shard_map/all_to_all | solution.py:286
  130.5 23.8 %all-to-all-start.1 = ((f32[32,1,2816]{2,1,0:T(1,128)}), f32[32,1,2816]{2,1,0:T(1,128)S(1)}, u32[]{:S(2)}, u32[]{:S(2)}) async-start(f32[32,1,2816]{2,1,0:T(1,128)} %broadcast_in_dim.5), calls=%async_computation.1 | async-start | bytes 720896 | tf_op jit(solution)/shard_map/all_to_all | solution.py:289

commit v5 on v4

--- a/solution.py
+++ b/solution.py
@@ -202,7 +202,7 @@
     lax.fori_loop(0, WP // TILE, third, 0)
 
 
-def last_kernel(place, next_ref, peer_ref, n0_ref, n0_peer_ref, part1_ref, w_ref, s_ref, give_ref, part_ref, both_ref):
+def grads_kernel(place, next_ref, peer_ref, n0_ref, n0_peer_ref, part1_ref, w_ref, part_ref):
     pc = place[2]
     grads = jnp.concatenate([next_ref[1, :, half_of(pc)], peer_ref[1, :, half_of(pc)]], axis=0)
     for t in range(2):
@@ -210,6 +210,9 @@
         back = nt(grads, w_ref[rows, :])
         sums = jnp.sum(back[:TOK] * n0_ref[:, rows] + back[TOK:] * n0_peer_ref[:, rows], axis=0, keepdims=True)
         part_ref[:, rows] = part1_ref[:, rows] + sums
+
+
+def state_kernel(next_ref, peer_ref, w_ref, s_ref, give_ref, both_ref):
     both_ref[:TOK] = next_ref[0]
     both_ref[TOK:] = peer_ref[0]
     s2 = jnp.dot(both_ref[...], w_ref[...], preferred_element_type=F32)
@@ -249,16 +252,27 @@
     )(place, s_own, back, got, n0, inj, cot, gain)
 
 
-def last_call(place, nexts, peer, n0, n0_peer, part1, w):
-    return pl.pallas_call(
-        last_kernel,
-        out_shape=(shape(TOK, HALF), shape(TOK, HALF), shape(1, WP)),
+def grads_call(place, nexts, peer, n0, n0_peer, part1, w):
+    return pl.pallas_call(
+        grads_kernel,
+        out_shape=shape(1, WP),
         in_specs=[SM] + [VM] * 6,
-        out_specs=(VM,) * 3,
+        out_specs=VM,
+        compiler_params=pltpu.CompilerParams(vmem_limit_bytes=24 * 2**20),
+        cost_estimate=pl.CostEstimate(flops=4 * TOK * WP * HALF, bytes_accessed=2 * WP * HALF, transcendentals=0),
+    )(place, nexts, peer, n0, n0_peer, part1, w)
+
+
+def state_call(nexts, peer, w):
+    return pl.pallas_call(
+        state_kernel,
+        out_shape=(shape(TOK, HALF), shape(TOK, HALF)),
+        in_specs=[VM] * 3,
+        out_specs=(VM,) * 2,
         scratch_shapes=[pltpu.VMEM((ALL, WP), BF)],
         compiler_params=pltpu.CompilerParams(vmem_limit_bytes=24 * 2**20),
-        cost_estimate=pl.CostEstimate(flops=8 * TOK * WP * HALF, bytes_accessed=2 * WP * HALF, transcendentals=0),
-    )(place, nexts, peer, n0, n0_peer, part1, w)
+        cost_estimate=pl.CostEstimate(flops=4 * TOK * WP * HALF, bytes_accessed=2 * WP * HALF, transcendentals=0),
+    )(nexts, peer, w)
 
 
 def narrow(array):
@@ -278,16 +292,21 @@
     low1 = send(low, along(False, 1))
     high2 = send(high3, along(False, -1))
     low2 = send(low1, along(False, 1))
+    high1, low3, acts = lax.optimization_barrier((high1, low3, acts))
     return acts, (low, high, low1, high1, low3, high3, low2, high2)
 
 
-def total(part):
-    dp_groups = [[yh * 16 + z * 2 + c for z in range(8) for c in range(2)] for yh in range(2)]
-    got = lax.all_to_all(jnp.broadcast_to(part, (16, WP)), "dp", 0, 0, axis_index_groups=dp_groups)
-    part = jnp.sum(got.reshape(16, WP), axis=0, keepdims=True)
-    planes = [[line(x, y, z, c) for y in range(NY) for x in range(NX)] for z in range(NZ) for c in range(NC)]
-    got = lax.all_to_all(jnp.broadcast_to(part, (32, WP)), AXES, 0, 0, axis_index_groups=planes)
-    return jnp.sum(got.reshape(32, WP), axis=0, keepdims=True)
+def groups(axis):
+    found = {}
+    for x, y, z, c in chips():
+        key = {"z": (x, y, c), "y": (x, z, c), "xc": (y, z)}[axis]
+        found.setdefault(key, []).append(line(x, y, z, c))
+    return list(found.values())
+
+
+def total(part, axis):
+    got = lax.all_to_all(jnp.broadcast_to(part, (8, WP)), AXES, 0, 0, axis_index_groups=groups(axis))
+    return jnp.sum(got.reshape(8, WP), axis=0, keepdims=True)
 
 
 def shards(state0, injected, core_weight, gain, counts, cotangent):
@@ -300,11 +319,17 @@
     peer, n0_peer = lax.optimization_barrier((send(acts, SWAP), send(n0, SWAP)))
     s_own, back, give, half = first_call(place, acts, peer, pieces)
     nexts, injg, part1, s1 = middle_call(place, s_own, back, send(give, SWAP), n0, inj, cot, gain_w)
-    s_own, give, part = last_call(place, nexts, send(nexts, SWAP), n0, n0_peer, part1, half)
-    got = send(give, SWAP)
+    peer = send(nexts, SWAP)
+    part = grads_call(place, nexts, peer, n0, n0_peer, part1, half)
+    part = total(part, "z")
+    s_own, give = state_call(nexts, peer, half)
+    got, s_own, part = lax.optimization_barrier((send(give, SWAP), s_own, part))
+    part = total(part, "y")
+    injg, part = lax.optimization_barrier((narrow(injg), part))
+    part = total(part, "xc")
     s2 = jnp.where(pc == 0, jnp.concatenate([s_own, got], axis=1), jnp.concatenate([got, s_own], axis=1))
     final = jnp.where(counts[0] >= 2, s2 + inj.astype(F32), s1).astype(BF)
-    return (narrow(final), narrow(injg), narrow(total(part)).reshape(W))
+    return (narrow(final), injg, narrow(part).reshape(W))
 
 
 def solution(mesh):

time: 156 us -> 161 us (1.032)
  blocking collectives: 0 us -> 16.4 us
  waiting for transfers between devices: 47.4 us -> 40.3 us
  starting transfers between devices: 61.8 us -> 56.3 us
    all_to_all x0 -> x1, blocking collectives: none -> 16.4 us  [total(): lax.all_to_all(jnp.broadcast_to(part, (8, WP)), AXES, 0, 0, axis_index_gr...]
    all_to_all x2, waiting for transfers between devices: 12.4 us -> 1.18 us  [total(): lax.all_to_all(jnp.broadcast_to(part, (8, WP)), AXES, 0, 0, axis_index_gr...]
    all_to_all x2, starting transfers between devices: 19.6 us -> 13.9 us  [total(): lax.all_to_all(jnp.broadcast_to(part, (8, WP)), AXES, 0, 0, axis_index_gr...]
    ppermute x14, waiting for transfers between devices: 35 us -> 39.1 us  [send(): return lax.ppermute(array, AXES, pairs)]
    pallas_call x1 -> x2, Pallas kernels: 6.45 us -> 6.51 us  [the longest x1 3.26 us: state_call(): pl.pallas_call(state_kernel, out_shape=(shape(TOK, HALF), shape(TOK, HALF...]
  transfers between devices with their start and end apart: 16 -> 16, of which waited for: 10 -> 9; matrix products, arithmetic and copies ran while one was open for 10% -> 9% of each run, Pallas kernels for 1% -> 3%
where the time goes in v5:
time: 161 us; the launch traced here: 160 us
  starting transfers between devices  56.3 us (35%)
  waiting for transfers between devices  40.3 us (25%)
  Pallas kernels  23.2 us (14%)
  local copies, waits for them, and re-layouts  16.6 us (10%)
  blocking collectives  16.4 us (10%)
  other arithmetic  5.21 us (3%)
  between operations  1.73 us (1%)
    ppermute x14, starting transfers between devices, send(): return lax.ppermute(array, AXES, pairs)  42.5 us
    ppermute x14, waiting for transfers between devices, send(): return lax.ppermute(array, AXES, pairs)  39.1 us
    all_to_all x1, blocking collectives, total(): lax.all_to_all(jnp.broadcast_to(part, (8, WP)), AXES, 0, 0, axis_index_gr...  16.4 us
    all_to_all x2, starting transfers between devices, total(): lax.all_to_all(jnp.broadcast_to(part, (8, WP)), AXES, 0, 0, axis_index_gr...  13.9 us
    pallas_call x1, Pallas kernels, first_call(): pl.pallas_call(first_kernel, out_shape=(shape(TOK, HALF), shape(TOK, WP),...  11.7 us
    unnamed x10, local copies, waits for them, and re-layouts  4.47 us
    transpose x2, local copies, waits for them, and re-layouts, narrow(): return array.T.reshape(16, SP, -1)[:, :SH].reshape(W, -1).T  3.7 us
    pallas_call x1, Pallas kernels, state_call(): pl.pallas_call(state_kernel, out_shape=(shape(TOK, HALF), shape(TOK, HALF...  3.26 us
  transfers between devices with their start and end apart: 16, of which 9 were waited for; matrix products, arithmetic and copies ran while one was open for 9% of the time, Pallas kernels for 3%

profile of v5, /device:TPU:1, one launch (start us, length us, event | category | flops | bytes accessed | tf_op | source)
XLA Modules:
  0.0 159.6 jit_solution(8858541595924139762)
XLA Ops:
  1.5 1.2 copy-done.2
  2.7 1.2 shard_map.86
  3.8 5.0 %collective-permute-start.2 = (bf16[176,1408]{1,0:T(8,128)(2,1)S(1)}, bf16[176,1408]{1,0:T(8,128)(2,1)S(1)}, u32[]{:S(2)}, u32[]{:S(2)}) collective-permute-start(bf16[176,1408]{1,0:T(8,128)(2,1)S(1)} %shard_map.86), channel_id=1, source_target_pairs={{0,2},{16,24},{32,34},{48,56},{64,66},{80,88},{96,98},{112,120},{1... | collective-permute-start | bytes 1486856 | tf_op jit(solution)/shard_map/ppermute | solution.py:46
  8.9 3.2 %collective-permute-start.1 = (bf16[176,1408]{1,0:T(8,128)(2,1)S(1)}, bf16[176,1408]{1,0:T(8,128)(2,1)}, u32[]{:S(2)}, u32[]{:S(2)}) collective-permute-start(bf16[176,1408]{1,0:T(8,128)(2,1)S(1)} %shard_map.86), channel_id=1, source_target_pairs={{0,1},{16,20},{32,33},{48,52},{64,65},{80,84},{96,97},{112,116},{1... | collective-permute-start | bytes 1486856 | tf_op jit(solution)/shard_map/ppermute | solution.py:46
  12.1 3.3 %collective-permute-start = (bf16[176,1408]{1,0:T(8,128)(2,1)S(1)}, bf16[176,1408]{1,0:T(8,128)(2,1)}, u32[]{:S(2)}, u32[]{:S(2)}) collective-permute-start(bf16[176,1408]{1,0:T(8,128)(2,1)S(1)} %shard_map.86), channel_id=1, source_target_pairs={{0,3},{16,284},{32,35},{48,316},{64,67},{80,348},{96,99},{112,380}... | collective-permute-start | bytes 1486856 | tf_op jit(solution)/shard_map/ppermute | solution.py:46
  15.4 0.8 reshape.44
  16.3 1.3 copy-done.1
  17.7 1.1 copy-done.4
  18.8 1.4 shard_map.85
  20.2 7.3 %collective-permute-done.1 = bf16[176,1408]{1,0:T(8,128)(2,1)} collective-permute-done((bf16[176,1408]{1,0:T(8,128)(2,1)S(1)}, bf16[176,1408]{1,0:T(8,128)(2,1)}, u32[]{:S(2)}, u32[]{:S(2)}) %collective-permute-start.1) | collective-permute-done | bytes 495648 | tf_op jit(solution)/shard_map/ppermute | solution.py:46
  27.5 1.1 pad_maximum_fusion.1.rest_0_
  28.7 4.1 %collective-permute-start.4 = (bf16[2,176,1408]{2,1,0:T(8,128)(2,1)S(1)}, bf16[2,176,1408]{2,1,0:T(8,128)(2,1)S(1)}, u32[]{:S(2)}, u32[]{:S(2)}) collective-permute-start(bf16[2,176,1408]{2,1,0:T(8,128)(2,1)S(1)} %pad_maximum_fusion.1.rest_0_), channel_id=1, source_target_pairs={{0,268},{16,19},{32,300},{48,51},{64,332},{80,83},{96,364},{112,11... | collective-permute-start | bytes 2973704 | tf_op jit(solution)/shard_map/ppermute | solution.py:46
  32.8 1.1 pad_maximum_fusion.rest_1_
  33.9 1.9 %collective-permute-start.3 = (bf16[2,176,1408]{2,1,0:T(8,128)(2,1)S(1)}, bf16[2,176,1408]{2,1,0:T(8,128)(2,1)S(1)}, u32[]{:S(2)}, u32[]{:S(2)}) collective-permute-start(bf16[2,176,1408]{2,1,0:T(8,128)(2,1)S(1)} %pad_maximum_fusion.rest_1_), channel_id=1, source_target_pairs={{0,4},{16,17},{32,36},{48,49},{64,68},{80,81},{96,100},{112,113},{... | collective-permute-start | bytes 2973704 | tf_op jit(solution)/shard_map/ppermute | solution.py:46
  35.8 2.1 %collective-permute-start.7 = (bf16[2,176,1408]{2,1,0:T(8,128)(2,1)S(1)}, bf16[2,176,1408]{2,1,0:T(8,128)(2,1)S(1)}, u32[]{:S(2)}, u32[]{:S(2)}) collective-permute-start(bf16[2,176,1408]{2,1,0:T(8,128)(2,1)S(1)} %pad_maximum_fusion.1.rest_0_), channel_id=1, source_target_pairs={{0,4},{16,17},{32,36},{48,49},{64,68},{80,81},{96,100},{112,113},{... | collective-permute-start | bytes 2973704 | tf_op jit(solution)/shard_map/ppermute | solution.py:46
  37.9 4.4 %collective-permute-start.8 = (bf16[2,176,1408]{2,1,0:T(8,128)(2,1)S(1)}, bf16[2,176,1408]{2,1,0:T(8,128)(2,1)S(1)}, u32[]{:S(2)}, u32[]{:S(2)}) collective-permute-start(bf16[2,176,1408]{2,1,0:T(8,128)(2,1)S(1)} %pad_maximum_fusion.rest_1_), channel_id=1, source_target_pairs={{0,268},{16,19},{32,300},{48,51},{64,332},{80,83},{96,364},{112,11... | collective-permute-start | bytes 2973704 | tf_op jit(solution)/shard_map/ppermute | solution.py:46
  42.4 1.5 collective-permute-done.4.rest_4_
  43.9 6.4 %collective-permute-done.3.rest_3_ = bf16[2,176,1408]{2,1,0:T(8,128)(2,1)S(1)} collective-permute-done((bf16[2,176,1408]{2,1,0:T(8,128)(2,1)S(1)}, bf16[2,176,1408]{2,1,0:T(8,128)(2,1)S(1)}, u32[]{:S(2)}, u32[]{:S(2)}) %collective-permute-start.3) | collective-permute-done | bytes 991264 | tf_op jit(solution)/shard_map/ppermute | solution.py:46
  50.3 1.9 %collective-permute-start.5 = (bf16[2,128,2816]{2,1,0:T(8,128)(2,1)S(1)}, bf16[2,128,2816]{2,1,0:T(8,128)(2,1)S(1)}, u32[]{:S(2)}, u32[]{:S(2)}) collective-permute-start(bf16[2,128,2816]{2,1,0:T(8,128)(2,1)S(1)} %get-tuple-element.48.acts_ref), channel_id=1, source_target_pairs={{0,16},{16,0},{32,48},{48,32},{64,80},{80,64},{96,112},{112,96},{1... | collective-permute-start | bytes 4325384 | tf_op jit(solution)/shard_map/ppermute | solution.py:46
  52.3 2.4 %collective-permute-start.6 = (f32[128,2816]{1,0:T(8,128)S(1)}, f32[128,2816]{1,0:T(8,128)S(1)}, u32[]{:S(2)}, u32[]{:S(2)}) collective-permute-start(f32[128,2816]{1,0:T(8,128)S(1)} %get-tuple-element.49.n0_ref), channel_id=1, source_target_pairs={{0,16},{16,0},{32,48},{48,32},{64,80},{80,64},{96,112},{112,96},{1... | collective-permute-start | bytes 4325384 | tf_op jit(solution)/shard_map/ppermute | solution.py:46
  54.7 6.0 %collective-permute-done.7.rest_2_ = bf16[2,176,1408]{2,1,0:T(8,128)(2,1)S(1)} collective-permute-done((bf16[2,176,1408]{2,1,0:T(8,128)(2,1)S(1)}, bf16[2,176,1408]{2,1,0:T(8,128)(2,1)S(1)}, u32[]{:S(2)}, u32[]{:S(2)}) %collective-permute-start.7) | collective-permute-done | bytes 991264 | tf_op jit(solution)/shard_map/ppermute | solution.py:46
  60.7 1.9 %collective-permute-start.9 = (bf16[2,176,1408]{2,1,0:T(8,128)(2,1)S(1)}, bf16[2,176,1408]{2,1,0:T(8,128)(2,1)S(1)}, u32[]{:S(2)}, u32[]{:S(2)}) collective-permute-start(bf16[2,176,1408]{2,1,0:T(8,128)(2,1)S(1)} %collective-permute-done.7.rest_2_), channel_id=1, source_target_pairs={{0,4},{16,17},{32,36},{48,49},{64,68},{80,81},{96,100},{112,113},{... | collective-permute-start | bytes 2973704 | tf_op jit(solution)/shard_map/ppermute | solution.py:46
  62.6 4.6 %collective-permute-start.10 = (bf16[2,176,1408]{2,1,0:T(8,128)(2,1)S(1)}, bf16[2,176,1408]{2,1,0:T(8,128)(2,1)S(1)}, u32[]{:S(2)}, u32[]{:S(2)}) collective-permute-start(bf16[2,176,1408]{2,1,0:T(8,128)(2,1)S(1)} %collective-permute-done.8.rest_5_), channel_id=1, source_target_pairs={{0,268},{16,19},{32,300},{48,51},{64,332},{80,83},{96,364},{112,11... | collective-permute-start | bytes 2973704 | tf_op jit(solution)/shard_map/ppermute | solution.py:46
  67.2 9.9 %collective-permute-done.9.rest_6_ = bf16[2,176,1408]{2,1,0:T(8,128)(2,1)S(1)} collective-permute-done((bf16[2,176,1408]{2,1,0:T(8,128)(2,1)S(1)}, bf16[2,176,1408]{2,1,0:T(8,128)(2,1)S(1)}, u32[]{:S(2)}, u32[]{:S(2)}) %collective-permute-start.9) | collective-permute-done | bytes 991264 | tf_op jit(solution)/shard_map/ppermute | solution.py:46
  77.1 1.2 collective-permute-done.10.rest_7_
  78.3 11.7 %shard_map.87 = (f32[128,1408]{1,0:T(8,128)S(1)}, f32[128,2816]{1,0:T(8,128)S(1)}, f32[128,4224]{1,0:T(8,128)S(1)}, bf16[2816,1408]{1,0:T(8,128)(2,1)S(1)}) custom-call(s32[4]{0:T(128)S(1)} %pad_add_fusion.place, bf16[2,128,2816]{2,1,0:T(8,128)(2,1)S(1)} %get-tuple-element.48.acts_ref, bf16[2,128,2816]{2,1,0:T(8,128)(2,1)S(1)} %collective-permute-done.5.peer_ref, ...), custom_call_target="tpu_custom_call" | custom-call | flops 4060086272 | bytes 7929856 | tf_op jit(solution)/shard_map/pallas_call | solution.py:233
  90.0 2.9 %collective-permute-start.11 = (f32[128,4224]{1,0:T(8,128)S(1)}, f32[128,4224]{1,0:T(8,128)S(1)}, u32[]{:S(2)}, u32[]{:S(2)}) collective-permute-start(f32[128,4224]{1,0:T(8,128)S(1)} %get-tuple-element.55), channel_id=1, source_target_pairs={{0,16},{16,0},{32,48},{48,32},{64,80},{80,64},{96,112},{112,96},{1... | collective-permute-start | bytes 6488072 | tf_op jit(solution)/shard_map/ppermute | solution.py:46
  93.0 3.9 %collective-permute-done.11.got_ref = f32[128,4224]{1,0:T(8,128)S(1)} collective-permute-done((f32[128,4224]{1,0:T(8,128)S(1)}, f32[128,4224]{1,0:T(8,128)S(1)}, u32[]{:S(2)}, u32[]{:S(2)}) %collective-permute-start.11) | collective-permute-done | bytes 2162720 | tf_op jit(solution)/shard_map/ppermute | solution.py:46
  96.8 2.3 %shard_map.88 = (bf16[2,128,2816]{2,1,0:T(8,128)(2,1)S(1)}, bf16[128,2816]{1,0:T(8,128)(2,1)S(1)}, f32[1,2816]{1,0:T(1,128)S(1)}, f32[128,2816]{1,0:T(8,128)S(1)}) custom-call(s32[4]{0:T(128)S(1)} %pad_add_fusion.place, f32[128,1408]{1,0:T(8,128)S(1)} %get-tuple-element.53.s_ref, f32[128,2816]{1,0:T(8,128)S(1)} %get-tuple-element.54.back_ref, ...), custom_call_target="tpu_custom_call" | custom-call | flops 7208960 | bytes 10000000 | tf_op jit(solution)/shard_map/pallas_call | solution.py:245
  99.1 0.9 copy-done.3
  100.0 2.3 %collective-permute-start.12 = (bf16[2,128,2816]{2,1,0:T(8,128)(2,1)S(1)}, bf16[2,128,2816]{2,1,0:T(8,128)(2,1)S(1)}, u32[]{:S(2)}, u32[]{:S(2)}) collective-permute-start(bf16[2,128,2816]{2,1,0:T(8,128)(2,1)S(1)} %get-tuple-element.58.next_ref), channel_id=1, source_target_pairs={{0,16},{16,0},{32,48},{48,32},{64,80},{80,64},{96,112},{112,96},{1... | collective-permute-start | bytes 4325384 | tf_op jit(solution)/shard_map/ppermute | solution.py:46
  102.3 2.8 %collective-permute-done.12.peer_ref = bf16[2,128,2816]{2,1,0:T(8,128)(2,1)S(1)} collective-permute-done((bf16[2,128,2816]{2,1,0:T(8,128)(2,1)S(1)}, bf16[2,128,2816]{2,1,0:T(8,128)(2,1)S(1)}, u32[]{:S(2)}, u32[]{:S(2)}) %collective-permute-start.12) | collective-permute-done | bytes 1441824 | tf_op jit(solution)/shard_map/ppermute | solution.py:46
  105.1 3.3 %shard_map.89 = (f32[128,1408]{1,0:T(8,128)S(1)}, f32[128,1408]{1,0:T(8,128)}) custom-call(bf16[2,128,2816]{2,1,0:T(8,128)(2,1)S(1)} %get-tuple-element.58.next_ref, bf16[2,128,2816]{2,1,0:T(8,128)(2,1)S(1)} %collective-permute-done.12.peer_ref, bf16[2816,1408]{1,0:T(8,128)(2,1)S(1)} %get-tuple-element.59.w_ref), custom_call_target="tpu_custom_call" | custom-call | flops 2030043136 | bytes 7929856 | tf_op jit(solution)/shard_map/pallas_call | solution.py:267
  108.4 2.5 %collective-permute-start.13 = (f32[128,1408]{1,0:T(8,128)}, f32[128,1408]{1,0:T(8,128)}, u32[]{:S(2)}, u32[]{:S(2)}) collective-permute-start(f32[128,1408]{1,0:T(8,128)} %get-tuple-element.60), channel_id=1, source_target_pairs={{0,16},{16,0},{32,48},{48,32},{64,80},{80,64},{96,112},{112,96},{1... | collective-permute-start | bytes 2162696 | tf_op jit(solution)/shard_map/ppermute | solution.py:46
  110.8 3.2 %shard_map.90 = f32[1,2816]{1,0:T(1,128)S(1)} custom-call(s32[4]{0:T(128)S(1)} %pad_add_fusion.place, bf16[2,128,2816]{2,1,0:T(8,128)(2,1)S(1)} %get-tuple-element.58.next_ref, bf16[2,128,2816]{2,1,0:T(8,128)(2,1)S(1)} %collective-permute-done.12.peer_ref, f32[128,2816]{1,0:T(8,128)S(1)} %get-tuple-element.49.n0_ref, ...), custom_call_target="tpu_custom_call" | custom-call | flops 2030043136 | bytes 7929856 | tf_op jit(solution)/shard_map/pallas_call | solution.py:256
  114.2 16.4 %all_to_all.18 = f32[8,1,2816]{2,1,0:T(1,128)S(1)} all-to-all(f32[8,1,2816]{2,1,0:T(1,128)S(1)} %broadcast_in_dim.10), channel_id=1, replica_groups={{0,32,64,96,128,160,192,224},{16,48,80,112,144,176,208,240},{4,36,68,10..., dimensions={0} | all-to-all | bytes 180224 | tf_op jit(solution)/shard_map/all_to_all | solution.py:308
  130.7 0.7 broadcast_in_dim.23
  131.4 6.0 %all-to-all-start.1 = ((f32[8,1,2816]{2,1,0:T(1,128)}), f32[8,1,2816]{2,1,0:T(1,128)S(1)}, u32[]{:S(2)}, u32[]{:S(2)}) async-start(f32[8,1,2816]{2,1,0:T(1,128)} %broadcast_in_dim.23), calls=%async_computation.1 | async-start | bytes 180224 | tf_op jit(solution)/shard_map/all_to_all | solution.py:308
  137.3 2.2 %copy.17 = bf16[2816,128]{1,0:T(8,128)(2,1)} copy(bf16[2816,128]{0,1:T(8,128)(2,1)} %bitcast.24) | data formatting | bytes 1441792 | tf_op jit(solution)/shard_map/transpose | solution.py:279
  139.6 2.0 %slice.13 = bf16[16,165,128]{2,1,0:T(8,128)(2,1)} slice(bf16[16,176,128]{2,1,0:T(8,128)(2,1)} %bitcast.26), slice={[0:16], [0:165], [0:128]} | slice | bytes 1351680 | tf_op jit(solution)/shard_map/slice | solution.py:279
  141.6 2.1 %reshape.49 = bf16[2640,128]{1,0:T(8,128)(2,1)} reshape(bf16[16,165,128]{2,1,0:T(8,128)(2,1)} %slice.13) | data formatting | bytes 1351680 | tf_op jit(solution)/shard_map/reshape | solution.py:279
  143.7 1.2 all-to-all-done.1
  145.1 0.7 broadcast_in_dim.25
  145.7 7.9 %all-to-all-start.2 = ((f32[8,1,2816]{2,1,0:T(1,128)}), f32[8,1,2816]{2,1,0:T(1,128)S(1)}, u32[]{:S(2)}, u32[]{:S(2)}) async-start(f32[8,1,2816]{2,1,0:T(1,128)} %broadcast_in_dim.25), calls=%async_computation.2 | async-start | bytes 180224 | tf_op jit(solution)/shard_map/all_to_all | solution.py:308
  153.6 2.6 %fusion.3 = bf16[2816,128]{0,1:T(8,128)(2,1)} fusion(f32[128,2816]{1,0:T(8,128)S(1)} %get-tuple-element.66, bf16[128,2816]{1,0:T(8,128)(2,1)S(1)} %get-tuple-element.56.inj_ref, f32[128,1408]{1,0:T(8,128)S(1)} %get-tuple-element.64, f32[128,1408]{1,0:T(8,128)} %collective-permute-done.13, pred[]{:T(512)S(6)} %eq.6, pred[]{:T(512)} %bitcast), kind=kLoop, calls=%fused_computation.6 | loop fusion | flops 2162688 | bytes 4325378 | tf_op jit(solution)/shard_map/transpose | solution.py:279
  156.2 1.5 copy.16
  157.7 1.1 reshape.47
  158.9 0.7 reshape_transpose_reshape.3
  (27 shorter events, 0.7 us)
Async XLA Ops:
  0.6 15.7 %copy-start = (f32[128,2640]{0,1:T(8,128)S(1)}, f32[128,2640]{0,1:T(8,128)}, u32[]{:S(2)}) copy-start(f32[128,2640]{0,1:T(8,128)} %param.6) | copy-start | bytes 4055044
  1.5 1.2 copy-start.2
  3.8 16.4 %collective-permute-start.2 = (bf16[176,1408]{1,0:T(8,128)(2,1)S(1)}, bf16[176,1408]{1,0:T(8,128)(2,1)S(1)}, u32[]{:S(2)}, u32[]{:S(2)}) collective-permute-start(bf16[176,1408]{1,0:T(8,128)(2,1)S(1)} %shard_map.86), channel_id=1, source_target_pairs={{0,2},{16,24},{32,34},{48,56},{64,66},{80,88},{96,98},{112,120},{1... | collective-permute-start | bytes 1486856 | tf_op jit(solution)/shard_map/ppermute | solution.py:46
  8.9 18.6 %collective-permute-start.1 = (bf16[176,1408]{1,0:T(8,128)(2,1)S(1)}, bf16[176,1408]{1,0:T(8,128)(2,1)}, u32[]{:S(2)}, u32[]{:S(2)}) collective-permute-start(bf16[176,1408]{1,0:T(8,128)(2,1)S(1)} %shard_map.86), channel_id=1, source_target_pairs={{0,1},{16,20},{32,33},{48,52},{64,65},{80,84},{96,97},{112,116},{1... | collective-permute-start | bytes 1486856 | tf_op jit(solution)/shard_map/ppermute | solution.py:46
  12.1 15.4 %collective-permute-start = (bf16[176,1408]{1,0:T(8,128)(2,1)S(1)}, bf16[176,1408]{1,0:T(8,128)(2,1)}, u32[]{:S(2)}, u32[]{:S(2)}) collective-permute-start(bf16[176,1408]{1,0:T(8,128)(2,1)S(1)} %shard_map.86), channel_id=1, source_target_pairs={{0,3},{16,284},{32,35},{48,316},{64,67},{80,348},{96,99},{112,380}... | collective-permute-start | bytes 1486856 | tf_op jit(solution)/shard_map/ppermute | solution.py:46
  16.3 1.3 copy-start.1
  17.7 1.1 copy-start.4
  28.7 15.2 %collective-permute-start.4 = (bf16[2,176,1408]{2,1,0:T(8,128)(2,1)S(1)}, bf16[2,176,1408]{2,1,0:T(8,128)(2,1)S(1)}, u32[]{:S(2)}, u32[]{:S(2)}) collective-permute-start(bf16[2,176,1408]{2,1,0:T(8,128)(2,1)S(1)} %pad_maximum_fusion.1.rest_0_), channel_id=1, source_target_pairs={{0,268},{16,19},{32,300},{48,51},{64,332},{80,83},{96,364},{112,11... | collective-permute-start | bytes 2973704 | tf_op jit(solution)/shard_map/ppermute | solution.py:46
  33.9 16.4 %collective-permute-start.3 = (bf16[2,176,1408]{2,1,0:T(8,128)(2,1)S(1)}, bf16[2,176,1408]{2,1,0:T(8,128)(2,1)S(1)}, u32[]{:S(2)}, u32[]{:S(2)}) collective-permute-start(bf16[2,176,1408]{2,1,0:T(8,128)(2,1)S(1)} %pad_maximum_fusion.rest_1_), channel_id=1, source_target_pairs={{0,4},{16,17},{32,36},{48,49},{64,68},{80,81},{96,100},{112,113},{... | collective-permute-start | bytes 2973704 | tf_op jit(solution)/shard_map/ppermute | solution.py:46
  35.8 24.8 %collective-permute-start.7 = (bf16[2,176,1408]{2,1,0:T(8,128)(2,1)S(1)}, bf16[2,176,1408]{2,1,0:T(8,128)(2,1)S(1)}, u32[]{:S(2)}, u32[]{:S(2)}) collective-permute-start(bf16[2,176,1408]{2,1,0:T(8,128)(2,1)S(1)} %pad_maximum_fusion.1.rest_0_), channel_id=1, source_target_pairs={{0,4},{16,17},{32,36},{48,49},{64,68},{80,81},{96,100},{112,113},{... | collective-permute-start | bytes 2973704 | tf_op jit(solution)/shard_map/ppermute | solution.py:46
  37.9 24.6 %collective-permute-start.8 = (bf16[2,176,1408]{2,1,0:T(8,128)(2,1)S(1)}, bf16[2,176,1408]{2,1,0:T(8,128)(2,1)S(1)}, u32[]{:S(2)}, u32[]{:S(2)}) collective-permute-start(bf16[2,176,1408]{2,1,0:T(8,128)(2,1)S(1)} %pad_maximum_fusion.rest_1_), channel_id=1, source_target_pairs={{0,268},{16,19},{32,300},{48,51},{64,332},{80,83},{96,364},{112,11... | collective-permute-start | bytes 2973704 | tf_op jit(solution)/shard_map/ppermute | solution.py:46
  50.3 16.8 %collective-permute-start.5 = (bf16[2,128,2816]{2,1,0:T(8,128)(2,1)S(1)}, bf16[2,128,2816]{2,1,0:T(8,128)(2,1)S(1)}, u32[]{:S(2)}, u32[]{:S(2)}) collective-permute-start(bf16[2,128,2816]{2,1,0:T(8,128)(2,1)S(1)} %get-tuple-element.48.acts_ref), channel_id=1, source_target_pairs={{0,16},{16,0},{32,48},{48,32},{64,80},{80,64},{96,112},{112,96},{1... | collective-permute-start | bytes 4325384 | tf_op jit(solution)/shard_map/ppermute | solution.py:46
  52.3 14.9 %collective-permute-start.6 = (f32[128,2816]{1,0:T(8,128)S(1)}, f32[128,2816]{1,0:T(8,128)S(1)}, u32[]{:S(2)}, u32[]{:S(2)}) collective-permute-start(f32[128,2816]{1,0:T(8,128)S(1)} %get-tuple-element.49.n0_ref), channel_id=1, source_target_pairs={{0,16},{16,0},{32,48},{48,32},{64,80},{80,64},{96,112},{112,96},{1... | collective-permute-start | bytes 4325384 | tf_op jit(solution)/shard_map/ppermute | solution.py:46
  60.7 16.4 %collective-permute-start.9 = (bf16[2,176,1408]{2,1,0:T(8,128)(2,1)S(1)}, bf16[2,176,1408]{2,1,0:T(8,128)(2,1)S(1)}, u32[]{:S(2)}, u32[]{:S(2)}) collective-permute-start(bf16[2,176,1408]{2,1,0:T(8,128)(2,1)S(1)} %collective-permute-done.7.rest_2_), channel_id=1, source_target_pairs={{0,4},{16,17},{32,36},{48,49},{64,68},{80,81},{96,100},{112,113},{... | collective-permute-start | bytes 2973704 | tf_op jit(solution)/shard_map/ppermute | solution.py:46
  62.6 15.7 %collective-permute-start.10 = (bf16[2,176,1408]{2,1,0:T(8,128)(2,1)S(1)}, bf16[2,176,1408]{2,1,0:T(8,128)(2,1)S(1)}, u32[]{:S(2)}, u32[]{:S(2)}) collective-permute-start(bf16[2,176,1408]{2,1,0:T(8,128)(2,1)S(1)} %collective-permute-done.8.rest_5_), channel_id=1, source_target_pairs={{0,268},{16,19},{32,300},{48,51},{64,332},{80,83},{96,364},{112,11... | collective-permute-start | bytes 2973704 | tf_op jit(solution)/shard_map/ppermute | solution.py:46
  90.0 6.8 %collective-permute-start.11 = (f32[128,4224]{1,0:T(8,128)S(1)}, f32[128,4224]{1,0:T(8,128)S(1)}, u32[]{:S(2)}, u32[]{:S(2)}) collective-permute-start(f32[128,4224]{1,0:T(8,128)S(1)} %get-tuple-element.55), channel_id=1, source_target_pairs={{0,16},{16,0},{32,48},{48,32},{64,80},{80,64},{96,112},{112,96},{1... | collective-permute-start | bytes 6488072 | tf_op jit(solution)/shard_map/ppermute | solution.py:46
  99.1 0.9 copy-start.3
  100.0 5.1 %collective-permute-start.12 = (bf16[2,128,2816]{2,1,0:T(8,128)(2,1)S(1)}, bf16[2,128,2816]{2,1,0:T(8,128)(2,1)S(1)}, u32[]{:S(2)}, u32[]{:S(2)}) collective-permute-start(bf16[2,128,2816]{2,1,0:T(8,128)(2,1)S(1)} %get-tuple-element.58.next_ref), channel_id=1, source_target_pairs={{0,16},{16,0},{32,48},{48,32},{64,80},{80,64},{96,112},{112,96},{1... | collective-permute-start | bytes 4325384 | tf_op jit(solution)/shard_map/ppermute | solution.py:46
  108.4 22.2 %collective-permute-start.13 = (f32[128,1408]{1,0:T(8,128)}, f32[128,1408]{1,0:T(8,128)}, u32[]{:S(2)}, u32[]{:S(2)}) collective-permute-start(f32[128,1408]{1,0:T(8,128)} %get-tuple-element.60), channel_id=1, source_target_pairs={{0,16},{16,0},{32,48},{48,32},{64,80},{80,64},{96,112},{112,96},{1... | collective-permute-start | bytes 2162696 | tf_op jit(solution)/shard_map/ppermute | solution.py:46
  131.4 13.6 %all-to-all-start.1 = ((f32[8,1,2816]{2,1,0:T(1,128)}), f32[8,1,2816]{2,1,0:T(1,128)S(1)}, u32[]{:S(2)}, u32[]{:S(2)}) async-start(f32[8,1,2816]{2,1,0:T(1,128)} %broadcast_in_dim.23), calls=%async_computation.1 | async-start | bytes 180224 | tf_op jit(solution)/shard_map/all_to_all | solution.py:308
  145.7 13.0 %all-to-all-start.2 = ((f32[8,1,2816]{2,1,0:T(1,128)}), f32[8,1,2816]{2,1,0:T(1,128)S(1)}, u32[]{:S(2)}, u32[]{:S(2)}) async-start(f32[8,1,2816]{2,1,0:T(1,128)} %broadcast_in_dim.25), calls=%async_computation.2 | async-start | bytes 180224 | tf_op jit(solution)/shard_map/all_to_all | solution.py:308

commit v6 on v5

--- a/solution.py
+++ b/solution.py
@@ -275,8 +275,55 @@
     )(nexts, peer, w)
 
 
-def narrow(array):
-    return array.T.reshape(16, SP, -1)[:, :SH].reshape(W, -1).T
+def tighten(wide_ref, tall_ref, out_ref):
+    for s in range(16):
+        tall_ref[SH * s : SH * s + SH, :] = wide_ref[SP * s : SP * s + SH, :]
+    out_ref[...] = tall_ref[...].astype(BF)
+
+
+def flip_kernel(rows_ref, out_ref, wide_ref, tall_ref):
+    for t in range(WP // 128):
+        cols = slice(128 * t, 128 * t + 128)
+        wide_ref[cols, :] = rows_ref[:, cols].astype(F32).T
+    tighten(wide_ref, tall_ref, out_ref)
+
+
+def final_kernel(place, s_ref, got_ref, inj_ref, s1_ref, out_ref, s2_ref, wide_ref, tall_ref):
+    pc, deep = place[2], place[3] >= 2
+    s2_ref[:, half_of(pc)] = s_ref[...]
+    s2_ref[:, half_of(1 - pc)] = got_ref[...]
+    for t in range(WP // 128):
+        cols = slice(128 * t, 128 * t + 128)
+        s2 = s2_ref[:, cols] + inj_ref[:, cols].astype(F32)
+        wide_ref[cols, :] = jnp.where(deep, s2, s1_ref[:, cols]).T
+    tighten(wide_ref, tall_ref, out_ref)
+
+
+FLIPPED = [pltpu.VMEM((WP, TOK), F32), pltpu.VMEM((W, TOK), F32)]
+
+
+def flip_call(rows):
+    return pl.pallas_call(
+        flip_kernel,
+        out_shape=shape(W, TOK, dtype=BF),
+        in_specs=[VM],
+        out_specs=VM,
+        scratch_shapes=FLIPPED,
+        compiler_params=pltpu.CompilerParams(vmem_limit_bytes=16 * 2**20),
+        cost_estimate=pl.CostEstimate(flops=10**6, bytes_accessed=3 * 10**6, transcendentals=0),
+    )(rows).T
+
+
+def final_call(place, s_own, got, inj, s1):
+    return pl.pallas_call(
+        final_kernel,
+        out_shape=shape(W, TOK, dtype=BF),
+        in_specs=[SM] + [VM] * 4,
+        out_specs=VM,
+        scratch_shapes=[pltpu.VMEM((TOK, WP), F32)] + FLIPPED,
+        compiler_params=pltpu.CompilerParams(vmem_limit_bytes=16 * 2**20),
+        cost_estimate=pl.CostEstimate(flops=10**6, bytes_accessed=5 * 10**6, transcendentals=0),
+    )(place, s_own, got, inj, s1).T
 
 
 def gather(own, acts):
@@ -292,7 +339,6 @@
     low1 = send(low, along(False, 1))
     high2 = send(high3, along(False, -1))
     low2 = send(low1, along(False, 1))
-    high1, low3, acts = lax.optimization_barrier((high1, low3, acts))
     return acts, (low, high, low1, high1, low3, high3, low2, high2)
 
 
@@ -316,7 +362,8 @@
     gain_w = jnp.pad(gain.reshape(16, SH), ((0, 0), (0, SP - SH))).reshape(1, WP)
     acts = prepare(state0, injected, cotangent, gain_w)
     (n0, acts, inj, cot), pieces = gather(spread(place, core_weight), acts)
-    peer, n0_peer = lax.optimization_barrier((send(acts, SWAP), send(n0, SWAP)))
+    peer, n0 = lax.optimization_barrier((send(acts, SWAP), n0))
+    peer, n0_peer = lax.optimization_barrier((peer, send(n0, SWAP)))
     s_own, back, give, half = first_call(place, acts, peer, pieces)
     nexts, injg, part1, s1 = middle_call(place, s_own, back, send(give, SWAP), n0, inj, cot, gain_w)
     peer = send(nexts, SWAP)
@@ -325,11 +372,10 @@
     s_own, give = state_call(nexts, peer, half)
     got, s_own, part = lax.optimization_barrier((send(give, SWAP), s_own, part))
     part = total(part, "y")
-    injg, part = lax.optimization_barrier((narrow(injg), part))
+    injg, part = lax.optimization_barrier((flip_call(injg), part))
     part = total(part, "xc")
-    s2 = jnp.where(pc == 0, jnp.concatenate([s_own, got], axis=1), jnp.concatenate([got, s_own], axis=1))
-    final = jnp.where(counts[0] >= 2, s2 + inj.astype(F32), s1).astype(BF)
-    return (narrow(final), injg, narrow(part).reshape(W))
+    final = final_call(place, s_own, got, inj, s1)
+    return (final, injg, part.reshape(16, SP)[:, :SH].reshape(W))
 
 
 def solution(mesh):

time: 161 us -> 154 us (0.957)
  local copies, waits for them, and re-layouts: 16.6 us -> 8.7 us
  Pallas kernels: 23.2 us -> 27.2 us
  other arithmetic: 5.21 us -> 1.77 us
    all_to_all x2, waiting for transfers between devices: 1.18 us -> 7.57 us  [total(): lax.all_to_all(jnp.broadcast_to(part, (8, WP)), AXES, 0, 0, axis_index_gr...]
    ppermute x14, waiting for transfers between devices: 39.1 us -> 34.4 us  [send(): return lax.ppermute(array, AXES, pairs)]
    pallas_call x0 -> x2, Pallas kernels: none -> 3.86 us  [the longest x1 2.65 us: final_call(): pl.pallas_call(final_kernel, out_shape=shape(W, TOK, dtype=BF), in_specs=...]
    transpose x2 -> x0, local copies, waits for them, and re-layouts: 3.7 us -> none  [narrow(): return array.T.reshape(16, SP, -1)[:, :SH].reshape(W, -1).T]
    transpose x1 -> x0, other arithmetic: 2.56 us -> none  [narrow(): return array.T.reshape(16, SP, -1)[:, :SH].reshape(W, -1).T]
    reshape x2 -> x1, local copies, waits for them, and re-layouts: 3.2 us -> 0.7 us  [shards(): return (final, injg, part.reshape(16, SP)[:, :SH].reshape(W))]
    slice x2 -> x0, local copies, waits for them, and re-layouts: 2.07 us -> none  [narrow(): return array.T.reshape(16, SP, -1)[:, :SH].reshape(W, -1).T]
    unnamed x10 -> x12, local copies, waits for them, and re-layouts: 4.47 us -> 5.57 us
  transfers between devices with their start and end apart: 16 -> 16, of which waited for: 9 -> 10; matrix products, arithmetic and copies ran while one was open for 9% -> 2% of each run, Pallas kernels for 3% -> 6%
where the time goes in v6:
time: 154 us; the launch traced here: 153 us
  starting transfers between devices  54.8 us (36%)
  waiting for transfers between devices  41.9 us (27%)
  Pallas kernels  27.2 us (18%)
  blocking collectives  17.2 us (11%)
  local copies, waits for them, and re-layouts  8.7 us (6%)
  other arithmetic  1.77 us (1%)
  between operations  1.7 us (1%)
    ppermute x14, starting transfers between devices, send(): return lax.ppermute(array, AXES, pairs)  41.2 us
    ppermute x14, waiting for transfers between devices, send(): return lax.ppermute(array, AXES, pairs)  34.4 us
    all_to_all x1, blocking collectives, total(): lax.all_to_all(jnp.broadcast_to(part, (8, WP)), AXES, 0, 0, axis_index_gr...  17.2 us
    all_to_all x2, starting transfers between devices, total(): lax.all_to_all(jnp.broadcast_to(part, (8, WP)), AXES, 0, 0, axis_index_gr...  13.6 us
    pallas_call x1, Pallas kernels, first_call(): pl.pallas_call(first_kernel, out_shape=(shape(TOK, HALF), shape(TOK, WP),...  11.8 us
    all_to_all x2, waiting for transfers between devices, total(): lax.all_to_all(jnp.broadcast_to(part, (8, WP)), AXES, 0, 0, axis_index_gr...  7.57 us
    unnamed x12, local copies, waits for them, and re-layouts  5.57 us
    pallas_call x1, Pallas kernels, grads_call(): pl.pallas_call(grads_kernel, out_shape=shape(1, WP), in_specs=[SM] + [VM]...  3.3 us
  transfers between devices with their start and end apart: 16, of which 10 were waited for; matrix products, arithmetic and copies ran while one was open for 2% of the time, Pallas kernels for 6%

profile of v6, /device:TPU:1, one launch (start us, length us, event | category | flops | bytes accessed | tf_op | source)
XLA Modules:
  0.0 153.3 jit_solution(709072089414391198)
XLA Ops:
  1.5 1.2 copy-done.2
  2.7 1.2 shard_map.86
  3.8 5.0 %collective-permute-start.2 = (bf16[176,1408]{1,0:T(8,128)(2,1)S(1)}, bf16[176,1408]{1,0:T(8,128)(2,1)}, u32[]{:S(2)}, u32[]{:S(2)}) collective-permute-start(bf16[176,1408]{1,0:T(8,128)(2,1)S(1)} %shard_map.86), channel_id=1, source_target_pairs={{0,2},{16,24},{32,34},{48,56},{64,66},{80,88},{96,98},{112,120},{1... | collective-permute-start | bytes 1486856 | tf_op jit(solution)/shard_map/ppermute | solution.py:46
  8.9 3.2 %collective-permute-start.1 = (bf16[176,1408]{1,0:T(8,128)(2,1)S(1)}, bf16[176,1408]{1,0:T(8,128)(2,1)S(1)}, u32[]{:S(2)}, u32[]{:S(2)}) collective-permute-start(bf16[176,1408]{1,0:T(8,128)(2,1)S(1)} %shard_map.86), channel_id=1, source_target_pairs={{0,1},{16,20},{32,33},{48,52},{64,65},{80,84},{96,97},{112,116},{1... | collective-permute-start | bytes 1486856 | tf_op jit(solution)/shard_map/ppermute | solution.py:46
  12.1 3.3 %collective-permute-start = (bf16[176,1408]{1,0:T(8,128)(2,1)S(1)}, bf16[176,1408]{1,0:T(8,128)(2,1)}, u32[]{:S(2)}, u32[]{:S(2)}) collective-permute-start(bf16[176,1408]{1,0:T(8,128)(2,1)S(1)} %shard_map.86), channel_id=1, source_target_pairs={{0,3},{16,284},{32,35},{48,316},{64,67},{80,348},{96,99},{112,380}... | collective-permute-start | bytes 1486856 | tf_op jit(solution)/shard_map/ppermute | solution.py:46
  15.4 0.8 reshape.33
  16.2 0.1 reshape.34.gain_ref
  16.3 1.3 copy-done.1
  17.7 1.1 copy-done.5
  18.8 1.4 shard_map.85
  20.2 7.2 %collective-permute-done.1 = bf16[176,1408]{1,0:T(8,128)(2,1)S(1)} collective-permute-done((bf16[176,1408]{1,0:T(8,128)(2,1)S(1)}, bf16[176,1408]{1,0:T(8,128)(2,1)S(1)}, u32[]{:S(2)}, u32[]{:S(2)}) %collective-permute-start.1) | collective-permute-done | bytes 495648 | tf_op jit(solution)/shard_map/ppermute | solution.py:46
  27.4 2.7 %collective-permute-start.3 = (bf16[2,128,2816]{2,1,0:T(8,128)(2,1)S(1)}, bf16[2,128,2816]{2,1,0:T(8,128)(2,1)S(1)}, u32[]{:S(2)}, u32[]{:S(2)}) collective-permute-start(bf16[2,128,2816]{2,1,0:T(8,128)(2,1)S(1)} %get-tuple-element.37.acts_ref), channel_id=1, source_target_pairs={{0,16},{16,0},{32,48},{48,32},{64,80},{80,64},{96,112},{112,96},{1... | collective-permute-start | bytes 4325384 | tf_op jit(solution)/shard_map/ppermute | solution.py:46
  30.2 1.3 pad_maximum_fusion.1.rest_1_
  31.5 3.3 %collective-permute-start.8 = (bf16[2,176,1408]{2,1,0:T(8,128)(2,1)S(1)}, bf16[2,176,1408]{2,1,0:T(8,128)(2,1)S(1)}, u32[]{:S(2)}, u32[]{:S(2)}) collective-permute-start(bf16[2,176,1408]{2,1,0:T(8,128)(2,1)S(1)} %pad_maximum_fusion.1.rest_1_), channel_id=1, source_target_pairs={{0,268},{16,19},{32,300},{48,51},{64,332},{80,83},{96,364},{112,11... | collective-permute-start | bytes 2973704 | tf_op jit(solution)/shard_map/ppermute | solution.py:46
  34.7 0.1 pad_maximum_fusion.rest_0_
  34.8 2.0 %collective-permute-start.5 = (bf16[2,176,1408]{2,1,0:T(8,128)(2,1)S(1)}, bf16[2,176,1408]{2,1,0:T(8,128)(2,1)S(1)}, u32[]{:S(2)}, u32[]{:S(2)}) collective-permute-start(bf16[2,176,1408]{2,1,0:T(8,128)(2,1)S(1)} %pad_maximum_fusion.rest_0_), channel_id=1, source_target_pairs={{0,4},{16,17},{32,36},{48,49},{64,68},{80,81},{96,100},{112,113},{... | collective-permute-start | bytes 2973704 | tf_op jit(solution)/shard_map/ppermute | solution.py:46
  36.9 2.5 %collective-permute-start.4 = (f32[128,2816]{1,0:T(8,128)S(1)}, f32[128,2816]{1,0:T(8,128)S(1)}, u32[]{:S(2)}, u32[]{:S(2)}) collective-permute-start(f32[128,2816]{1,0:T(8,128)S(1)} %get-tuple-element.40.n0_ref), channel_id=1, source_target_pairs={{0,16},{16,0},{32,48},{48,32},{64,80},{80,64},{96,112},{112,96},{1... | collective-permute-start | bytes 4325384 | tf_op jit(solution)/shard_map/ppermute | solution.py:46
  39.4 2.5 %collective-permute-start.6 = (bf16[2,176,1408]{2,1,0:T(8,128)(2,1)S(1)}, bf16[2,176,1408]{2,1,0:T(8,128)(2,1)S(1)}, u32[]{:S(2)}, u32[]{:S(2)}) collective-permute-start(bf16[2,176,1408]{2,1,0:T(8,128)(2,1)S(1)} %pad_maximum_fusion.1.rest_1_), channel_id=1, source_target_pairs={{0,4},{16,17},{32,36},{48,49},{64,68},{80,81},{96,100},{112,113},{... | collective-permute-start | bytes 2973704 | tf_op jit(solution)/shard_map/ppermute | solution.py:46
  41.9 4.0 %collective-permute-start.7 = (bf16[2,176,1408]{2,1,0:T(8,128)(2,1)S(1)}, bf16[2,176,1408]{2,1,0:T(8,128)(2,1)S(1)}, u32[]{:S(2)}, u32[]{:S(2)}) collective-permute-start(bf16[2,176,1408]{2,1,0:T(8,128)(2,1)S(1)} %pad_maximum_fusion.rest_0_), channel_id=1, source_target_pairs={{0,268},{16,19},{32,300},{48,51},{64,332},{80,83},{96,364},{112,11... | collective-permute-start | bytes 2973704 | tf_op jit(solution)/shard_map/ppermute | solution.py:46
  45.9 0.8 collective-permute-done.8.rest_5_
  46.7 4.5 %collective-permute-start.10 = (bf16[2,176,1408]{2,1,0:T(8,128)(2,1)S(1)}, bf16[2,176,1408]{2,1,0:T(8,128)(2,1)S(1)}, u32[]{:S(2)}, u32[]{:S(2)}) collective-permute-start(bf16[2,176,1408]{2,1,0:T(8,128)(2,1)S(1)} %collective-permute-done.8.rest_5_), channel_id=1, source_target_pairs={{0,268},{16,19},{32,300},{48,51},{64,332},{80,83},{96,364},{112,11... | collective-permute-start | bytes 2973704 | tf_op jit(solution)/shard_map/ppermute | solution.py:46
  51.2 0.1 collective-permute-done.5.rest_2_
  51.3 1.9 %collective-permute-start.9 = (bf16[2,176,1408]{2,1,0:T(8,128)(2,1)S(1)}, bf16[2,176,1408]{2,1,0:T(8,128)(2,1)S(1)}, u32[]{:S(2)}, u32[]{:S(2)}) collective-permute-start(bf16[2,176,1408]{2,1,0:T(8,128)(2,1)S(1)} %collective-permute-done.5.rest_2_), channel_id=1, source_target_pairs={{0,4},{16,17},{32,36},{48,49},{64,68},{80,81},{96,100},{112,113},{... | collective-permute-start | bytes 2973704 | tf_op jit(solution)/shard_map/ppermute | solution.py:46
  53.2 8.7 %collective-permute-done.6.rest_3_ = bf16[2,176,1408]{2,1,0:T(8,128)(2,1)S(1)} collective-permute-done((bf16[2,176,1408]{2,1,0:T(8,128)(2,1)S(1)}, bf16[2,176,1408]{2,1,0:T(8,128)(2,1)S(1)}, u32[]{:S(2)}, u32[]{:S(2)}) %collective-permute-start.6) | collective-permute-done | bytes 991264 | tf_op jit(solution)/shard_map/ppermute | solution.py:46
  61.9 6.0 %collective-permute-done.10.rest_7_ = bf16[2,176,1408]{2,1,0:T(8,128)(2,1)S(1)} collective-permute-done((bf16[2,176,1408]{2,1,0:T(8,128)(2,1)S(1)}, bf16[2,176,1408]{2,1,0:T(8,128)(2,1)S(1)}, u32[]{:S(2)}, u32[]{:S(2)}) %collective-permute-start.10) | collective-permute-done | bytes 991264 | tf_op jit(solution)/shard_map/ppermute | solution.py:46
  67.9 4.3 %collective-permute-done.9.rest_6_ = bf16[2,176,1408]{2,1,0:T(8,128)(2,1)S(1)} collective-permute-done((bf16[2,176,1408]{2,1,0:T(8,128)(2,1)S(1)}, bf16[2,176,1408]{2,1,0:T(8,128)(2,1)S(1)}, u32[]{:S(2)}, u32[]{:S(2)}) %collective-permute-start.9) | collective-permute-done | bytes 991264 | tf_op jit(solution)/shard_map/ppermute | solution.py:46
  72.2 11.8 %shard_map.87 = (f32[128,1408]{1,0:T(8,128)S(1)}, f32[128,2816]{1,0:T(8,128)S(1)}, f32[128,4224]{1,0:T(8,128)S(1)}, bf16[2816,1408]{1,0:T(8,128)(2,1)S(1)}) custom-call(s32[4]{0:T(128)S(1)} %pad_add_fusion.place, bf16[2,128,2816]{2,1,0:T(8,128)(2,1)S(1)} %get-tuple-element.37.acts_ref, bf16[2,128,2816]{2,1,0:T(8,128)(2,1)S(1)} %collective-permute-done.3.peer_ref, ...), custom_call_target="tpu_custom_call" | custom-call | flops 4060086272 | bytes 7929856 | tf_op jit(solution)/shard_map/pallas_call | solution.py:233
  84.1 2.0 %collective-permute-start.11 = (f32[128,4224]{1,0:T(8,128)S(1)}, f32[128,4224]{1,0:T(8,128)S(1)}, u32[]{:S(2)}, u32[]{:S(2)}) collective-permute-start(f32[128,4224]{1,0:T(8,128)S(1)} %get-tuple-element.47), channel_id=1, source_target_pairs={{0,16},{16,0},{32,48},{48,32},{64,80},{80,64},{96,112},{112,96},{1... | collective-permute-start | bytes 6488072 | tf_op jit(solution)/shard_map/ppermute | solution.py:46
  86.1 4.1 %collective-permute-done.11.got_ref = f32[128,4224]{1,0:T(8,128)S(1)} collective-permute-done((f32[128,4224]{1,0:T(8,128)S(1)}, f32[128,4224]{1,0:T(8,128)S(1)}, u32[]{:S(2)}, u32[]{:S(2)}) %collective-permute-start.11) | collective-permute-done | bytes 2162720 | tf_op jit(solution)/shard_map/ppermute | solution.py:46
  90.2 2.3 %shard_map.88 = (bf16[2,128,2816]{2,1,0:T(8,128)(2,1)S(1)}, bf16[128,2816]{1,0:T(8,128)(2,1)S(1)}, f32[1,2816]{1,0:T(1,128)S(1)}, f32[128,2816]{1,0:T(8,128)S(1)}) custom-call(s32[4]{0:T(128)S(1)} %pad_add_fusion.place, f32[128,1408]{1,0:T(8,128)S(1)} %get-tuple-element.45.s_ref, f32[128,2816]{1,0:T(8,128)S(1)} %get-tuple-element.46.back_ref, ...), custom_call_target="tpu_custom_call" | custom-call | flops 7208960 | bytes 10000000 | tf_op jit(solution)/shard_map/pallas_call | solution.py:245
  92.5 2.0 %collective-permute-start.12 = (bf16[2,128,2816]{2,1,0:T(8,128)(2,1)S(1)}, bf16[2,128,2816]{2,1,0:T(8,128)(2,1)S(1)}, u32[]{:S(2)}, u32[]{:S(2)}) collective-permute-start(bf16[2,128,2816]{2,1,0:T(8,128)(2,1)S(1)} %get-tuple-element.50.next_ref), channel_id=1, source_target_pairs={{0,16},{16,0},{32,48},{48,32},{64,80},{80,64},{96,112},{112,96},{1... | collective-permute-start | bytes 4325384 | tf_op jit(solution)/shard_map/ppermute | solution.py:46
  94.6 3.1 %collective-permute-done.12.peer_ref = bf16[2,128,2816]{2,1,0:T(8,128)(2,1)S(1)} collective-permute-done((bf16[2,128,2816]{2,1,0:T(8,128)(2,1)S(1)}, bf16[2,128,2816]{2,1,0:T(8,128)(2,1)S(1)}, u32[]{:S(2)}, u32[]{:S(2)}) %collective-permute-start.12) | collective-permute-done | bytes 1441824 | tf_op jit(solution)/shard_map/ppermute | solution.py:46
  97.6 3.3 %shard_map.89 = (f32[128,1408]{1,0:T(8,128)S(1)}, f32[128,1408]{1,0:T(8,128)}) custom-call(bf16[2,128,2816]{2,1,0:T(8,128)(2,1)S(1)} %get-tuple-element.50.next_ref, bf16[2,128,2816]{2,1,0:T(8,128)(2,1)S(1)} %collective-permute-done.12.peer_ref, bf16[2816,1408]{1,0:T(8,128)(2,1)S(1)} %get-tuple-element.51.w_ref), custom_call_target="tpu_custom_call" | custom-call | flops 2030043136 | bytes 7929856 | tf_op jit(solution)/shard_map/pallas_call | solution.py:267
  100.9 0.9 copy-done.3
  101.8 2.2 %collective-permute-start.13 = (f32[128,1408]{1,0:T(8,128)}, f32[128,1408]{1,0:T(8,128)}, u32[]{:S(2)}, u32[]{:S(2)}) collective-permute-start(f32[128,1408]{1,0:T(8,128)} %get-tuple-element.52), channel_id=1, source_target_pairs={{0,16},{16,0},{32,48},{48,32},{64,80},{80,64},{96,112},{112,96},{1... | collective-permute-start | bytes 2162696 | tf_op jit(solution)/shard_map/ppermute | solution.py:46
  104.0 3.3 %shard_map.90 = f32[1,2816]{1,0:T(1,128)S(1)} custom-call(s32[4]{0:T(128)S(1)} %pad_add_fusion.place, bf16[2,128,2816]{2,1,0:T(8,128)(2,1)S(1)} %get-tuple-element.50.next_ref, bf16[2,128,2816]{2,1,0:T(8,128)(2,1)S(1)} %collective-permute-done.12.peer_ref, f32[128,2816]{1,0:T(8,128)S(1)} %get-tuple-element.40.n0_ref, ...), custom_call_target="tpu_custom_call" | custom-call | flops 2030043136 | bytes 7929856 | tf_op jit(solution)/shard_map/pallas_call | solution.py:256
  107.4 17.2 %all_to_all.18 = f32[8,1,2816]{2,1,0:T(1,128)S(1)} all-to-all(f32[8,1,2816]{2,1,0:T(1,128)S(1)} %broadcast_in_dim.10), channel_id=1, replica_groups={{0,32,64,96,128,160,192,224},{16,48,80,112,144,176,208,240},{4,36,68,10..., dimensions={0} | all-to-all | bytes 180224 | tf_op jit(solution)/shard_map/all_to_all | solution.py:354
  124.8 0.7 broadcast_in_dim.23
  125.5 6.2 %all-to-all-start.1 = ((f32[8,1,2816]{2,1,0:T(1,128)}), f32[8,1,2816]{2,1,0:T(1,128)S(1)}, u32[]{:S(2)}, u32[]{:S(2)}) async-start(f32[8,1,2816]{2,1,0:T(1,128)} %broadcast_in_dim.23), calls=%async_computation.1 | async-start | bytes 180224 | tf_op jit(solution)/shard_map/all_to_all | solution.py:354
  131.6 1.2 shard_map.92
  132.8 6.4 %all-to-all-done.1 = f32[8,1,2816]{2,1,0:T(1,128)S(1)} async-done(((f32[8,1,2816]{2,1,0:T(1,128)}), f32[8,1,2816]{2,1,0:T(1,128)S(1)}, u32[]{:S(2)}, u32[]{:S(2)}) %all-to-all-start.1) | async-done | bytes 90144 | tf_op jit(solution)/shard_map/all_to_all | solution.py:354
  139.3 0.7 broadcast_in_dim.25
  140.0 7.4 %all-to-all-start.2 = ((f32[8,1,2816]{2,1,0:T(1,128)}), f32[8,1,2816]{2,1,0:T(1,128)S(1)}, u32[]{:S(2)}, u32[]{:S(2)}) async-start(f32[8,1,2816]{2,1,0:T(1,128)} %broadcast_in_dim.25), calls=%async_computation.2 | async-start | bytes 180224 | tf_op jit(solution)/shard_map/all_to_all | solution.py:354
  147.5 1.1 copy-done.4
  148.6 2.7 %shard_map.91 = bf16[2640,128]{1,0:T(8,128)(2,1)} custom-call(s32[4]{0:T(128)S(1)} %pad_add_fusion.place, f32[128,1408]{1,0:T(8,128)S(1)} %copy-done.4, f32[128,1408]{1,0:T(8,128)} %collective-permute-done.13.got_ref, bf16[128,2816]{1,0:T(8,128)(2,1)S(1)} %get-tuple-element.48.inj_ref, f32[128,2816]{1,0:T(8,128)S(1)} %get-tuple-element.58.s1_ref), custom_call_target="tpu_custom_call" | custom-call | flops 1000000 | bytes 5000000 | tf_op jit(solution)/shard_map/pallas_call | solution.py:318
  151.2 1.2 all-to-all-done.2
  152.5 0.1 reshape_broadcast_in_dim.3
  152.6 0.7 reshape.35
  (24 shorter events, 0.5 us)
Async XLA Ops:
  0.6 15.7 %copy-start = (f32[128,2640]{0,1:T(8,128)S(1)}, f32[128,2640]{0,1:T(8,128)}, u32[]{:S(2)}) copy-start(f32[128,2640]{0,1:T(8,128)} %param.6) | copy-start | bytes 4055044
  1.5 1.2 copy-start.2
  3.8 16.4 %collective-permute-start.2 = (bf16[176,1408]{1,0:T(8,128)(2,1)S(1)}, bf16[176,1408]{1,0:T(8,128)(2,1)}, u32[]{:S(2)}, u32[]{:S(2)}) collective-permute-start(bf16[176,1408]{1,0:T(8,128)(2,1)S(1)} %shard_map.86), channel_id=1, source_target_pairs={{0,2},{16,24},{32,34},{48,56},{64,66},{80,88},{96,98},{112,120},{1... | collective-permute-start | bytes 1486856 | tf_op jit(solution)/shard_map/ppermute | solution.py:46
  8.9 18.5 %collective-permute-start.1 = (bf16[176,1408]{1,0:T(8,128)(2,1)S(1)}, bf16[176,1408]{1,0:T(8,128)(2,1)S(1)}, u32[]{:S(2)}, u32[]{:S(2)}) collective-permute-start(bf16[176,1408]{1,0:T(8,128)(2,1)S(1)} %shard_map.86), channel_id=1, source_target_pairs={{0,1},{16,20},{32,33},{48,52},{64,65},{80,84},{96,97},{112,116},{1... | collective-permute-start | bytes 1486856 | tf_op jit(solution)/shard_map/ppermute | solution.py:46
  12.1 15.3 %collective-permute-start = (bf16[176,1408]{1,0:T(8,128)(2,1)S(1)}, bf16[176,1408]{1,0:T(8,128)(2,1)}, u32[]{:S(2)}, u32[]{:S(2)}) collective-permute-start(bf16[176,1408]{1,0:T(8,128)(2,1)S(1)} %shard_map.86), channel_id=1, source_target_pairs={{0,3},{16,284},{32,35},{48,316},{64,67},{80,348},{96,99},{112,380}... | collective-permute-start | bytes 1486856 | tf_op jit(solution)/shard_map/ppermute | solution.py:46
  16.3 1.3 copy-start.1
  17.7 1.1 copy-start.5
  27.4 9.4 %collective-permute-start.3 = (bf16[2,128,2816]{2,1,0:T(8,128)(2,1)S(1)}, bf16[2,128,2816]{2,1,0:T(8,128)(2,1)S(1)}, u32[]{:S(2)}, u32[]{:S(2)}) collective-permute-start(bf16[2,128,2816]{2,1,0:T(8,128)(2,1)S(1)} %get-tuple-element.37.acts_ref), channel_id=1, source_target_pairs={{0,16},{16,0},{32,48},{48,32},{64,80},{80,64},{96,112},{112,96},{1... | collective-permute-start | bytes 4325384 | tf_op jit(solution)/shard_map/ppermute | solution.py:46
  31.5 15.2 %collective-permute-start.8 = (bf16[2,176,1408]{2,1,0:T(8,128)(2,1)S(1)}, bf16[2,176,1408]{2,1,0:T(8,128)(2,1)S(1)}, u32[]{:S(2)}, u32[]{:S(2)}) collective-permute-start(bf16[2,176,1408]{2,1,0:T(8,128)(2,1)S(1)} %pad_maximum_fusion.1.rest_1_), channel_id=1, source_target_pairs={{0,268},{16,19},{32,300},{48,51},{64,332},{80,83},{96,364},{112,11... | collective-permute-start | bytes 2973704 | tf_op jit(solution)/shard_map/ppermute | solution.py:46
  34.8 16.4 %collective-permute-start.5 = (bf16[2,176,1408]{2,1,0:T(8,128)(2,1)S(1)}, bf16[2,176,1408]{2,1,0:T(8,128)(2,1)S(1)}, u32[]{:S(2)}, u32[]{:S(2)}) collective-permute-start(bf16[2,176,1408]{2,1,0:T(8,128)(2,1)S(1)} %pad_maximum_fusion.rest_0_), channel_id=1, source_target_pairs={{0,4},{16,17},{32,36},{48,49},{64,68},{80,81},{96,100},{112,113},{... | collective-permute-start | bytes 2973704 | tf_op jit(solution)/shard_map/ppermute | solution.py:46
  36.9 16.3 %collective-permute-start.4 = (f32[128,2816]{1,0:T(8,128)S(1)}, f32[128,2816]{1,0:T(8,128)S(1)}, u32[]{:S(2)}, u32[]{:S(2)}) collective-permute-start(f32[128,2816]{1,0:T(8,128)S(1)} %get-tuple-element.40.n0_ref), channel_id=1, source_target_pairs={{0,16},{16,0},{32,48},{48,32},{64,80},{80,64},{96,112},{112,96},{1... | collective-permute-start | bytes 4325384 | tf_op jit(solution)/shard_map/ppermute | solution.py:46
  39.4 22.5 %collective-permute-start.6 = (bf16[2,176,1408]{2,1,0:T(8,128)(2,1)S(1)}, bf16[2,176,1408]{2,1,0:T(8,128)(2,1)S(1)}, u32[]{:S(2)}, u32[]{:S(2)}) collective-permute-start(bf16[2,176,1408]{2,1,0:T(8,128)(2,1)S(1)} %pad_maximum_fusion.1.rest_1_), channel_id=1, source_target_pairs={{0,4},{16,17},{32,36},{48,49},{64,68},{80,81},{96,100},{112,113},{... | collective-permute-start | bytes 2973704 | tf_op jit(solution)/shard_map/ppermute | solution.py:46
  41.9 20.0 %collective-permute-start.7 = (bf16[2,176,1408]{2,1,0:T(8,128)(2,1)S(1)}, bf16[2,176,1408]{2,1,0:T(8,128)(2,1)S(1)}, u32[]{:S(2)}, u32[]{:S(2)}) collective-permute-start(bf16[2,176,1408]{2,1,0:T(8,128)(2,1)S(1)} %pad_maximum_fusion.rest_0_), channel_id=1, source_target_pairs={{0,268},{16,19},{32,300},{48,51},{64,332},{80,83},{96,364},{112,11... | collective-permute-start | bytes 2973704 | tf_op jit(solution)/shard_map/ppermute | solution.py:46
  46.7 21.2 %collective-permute-start.10 = (bf16[2,176,1408]{2,1,0:T(8,128)(2,1)S(1)}, bf16[2,176,1408]{2,1,0:T(8,128)(2,1)S(1)}, u32[]{:S(2)}, u32[]{:S(2)}) collective-permute-start(bf16[2,176,1408]{2,1,0:T(8,128)(2,1)S(1)} %collective-permute-done.8.rest_5_), channel_id=1, source_target_pairs={{0,268},{16,19},{32,300},{48,51},{64,332},{80,83},{96,364},{112,11... | collective-permute-start | bytes 2973704 | tf_op jit(solution)/shard_map/ppermute | solution.py:46
  51.3 20.9 %collective-permute-start.9 = (bf16[2,176,1408]{2,1,0:T(8,128)(2,1)S(1)}, bf16[2,176,1408]{2,1,0:T(8,128)(2,1)S(1)}, u32[]{:S(2)}, u32[]{:S(2)}) collective-permute-start(bf16[2,176,1408]{2,1,0:T(8,128)(2,1)S(1)} %collective-permute-done.5.rest_2_), channel_id=1, source_target_pairs={{0,4},{16,17},{32,36},{48,49},{64,68},{80,81},{96,100},{112,113},{... | collective-permute-start | bytes 2973704 | tf_op jit(solution)/shard_map/ppermute | solution.py:46
  84.1 6.1 %collective-permute-start.11 = (f32[128,4224]{1,0:T(8,128)S(1)}, f32[128,4224]{1,0:T(8,128)S(1)}, u32[]{:S(2)}, u32[]{:S(2)}) collective-permute-start(f32[128,4224]{1,0:T(8,128)S(1)} %get-tuple-element.47), channel_id=1, source_target_pairs={{0,16},{16,0},{32,48},{48,32},{64,80},{80,64},{96,112},{112,96},{1... | collective-permute-start | bytes 6488072 | tf_op jit(solution)/shard_map/ppermute | solution.py:46
  92.5 5.1 %collective-permute-start.12 = (bf16[2,128,2816]{2,1,0:T(8,128)(2,1)S(1)}, bf16[2,128,2816]{2,1,0:T(8,128)(2,1)S(1)}, u32[]{:S(2)}, u32[]{:S(2)}) collective-permute-start(bf16[2,128,2816]{2,1,0:T(8,128)(2,1)S(1)} %get-tuple-element.50.next_ref), channel_id=1, source_target_pairs={{0,16},{16,0},{32,48},{48,32},{64,80},{80,64},{96,112},{112,96},{1... | collective-permute-start | bytes 4325384 | tf_op jit(solution)/shard_map/ppermute | solution.py:46
  100.9 0.9 copy-start.3
  101.8 22.9 %collective-permute-start.13 = (f32[128,1408]{1,0:T(8,128)}, f32[128,1408]{1,0:T(8,128)}, u32[]{:S(2)}, u32[]{:S(2)}) collective-permute-start(f32[128,1408]{1,0:T(8,128)} %get-tuple-element.52), channel_id=1, source_target_pairs={{0,16},{16,0},{32,48},{48,32},{64,80},{80,64},{96,112},{112,96},{1... | collective-permute-start | bytes 2162696 | tf_op jit(solution)/shard_map/ppermute | solution.py:46
  125.5 13.7 %all-to-all-start.1 = ((f32[8,1,2816]{2,1,0:T(1,128)}), f32[8,1,2816]{2,1,0:T(1,128)S(1)}, u32[]{:S(2)}, u32[]{:S(2)}) async-start(f32[8,1,2816]{2,1,0:T(1,128)} %broadcast_in_dim.23), calls=%async_computation.1 | async-start | bytes 180224 | tf_op jit(solution)/shard_map/all_to_all | solution.py:354
  140.0 12.4 %all-to-all-start.2 = ((f32[8,1,2816]{2,1,0:T(1,128)}), f32[8,1,2816]{2,1,0:T(1,128)S(1)}, u32[]{:S(2)}, u32[]{:S(2)}) async-start(f32[8,1,2816]{2,1,0:T(1,128)} %broadcast_in_dim.25), calls=%async_computation.2 | async-start | bytes 180224 | tf_op jit(solution)/shard_map/all_to_all | solution.py:354
  147.5 1.1 copy-start.4

commit v7 on v6

--- a/solution.py
+++ b/solution.py
@@ -350,9 +350,12 @@
     return list(found.values())
 
 
-def total(part, axis):
-    got = lax.all_to_all(jnp.broadcast_to(part, (8, WP)), AXES, 0, 0, axis_index_groups=groups(axis))
-    return jnp.sum(got.reshape(8, WP), axis=0, keepdims=True)
+def spreads(part, axis):
+    return lax.all_to_all(jnp.broadcast_to(part, (8, WP)), AXES, 0, 0, axis_index_groups=groups(axis))
+
+
+def gathered(every):
+    return jnp.sum(every.reshape(8, WP), axis=0, keepdims=True)
 
 
 def shards(state0, injected, core_weight, gain, counts, cotangent):
@@ -368,14 +371,16 @@
     nexts, injg, part1, s1 = middle_call(place, s_own, back, send(give, SWAP), n0, inj, cot, gain_w)
     peer = send(nexts, SWAP)
     part = grads_call(place, nexts, peer, n0, n0_peer, part1, half)
-    part = total(part, "z")
+    nexts, peer, part = lax.optimization_barrier((nexts, peer, part))
+    every = spreads(part, "z")
     s_own, give = state_call(nexts, peer, half)
-    got, s_own, part = lax.optimization_barrier((send(give, SWAP), s_own, part))
-    part = total(part, "y")
-    injg, part = lax.optimization_barrier((flip_call(injg), part))
-    part = total(part, "xc")
+    s_own, give, every = lax.optimization_barrier((s_own, give, every))
+    got = send(give, SWAP)
+    every = spreads(gathered(every), "y")
+    got, injg, every = lax.optimization_barrier((got, flip_call(injg), every))
+    every = spreads(gathered(every), "xc")
     final = final_call(place, s_own, got, inj, s1)
-    return (final, injg, part.reshape(16, SP)[:, :SH].reshape(W))
+    return (final, injg, gathered(every).reshape(16, SP)[:, :SH].reshape(W))
 
 
 def solution(mesh):

time: 154 us -> 151 us (0.981)
  blocking collectives: 17.2 us -> 0 us
  starting transfers between devices: 54.8 us -> 64.7 us
  local copies, waits for them, and re-layouts: 8.7 us -> 16.6 us
    all_to_all x1 -> x0, blocking collectives: 17.2 us -> none  [total(): lax.all_to_all(jnp.broadcast_to(part, (8, WP)), AXES, 0, 0, axis_index_gr...]
    all_to_all x2 -> x3, starting transfers between devices: 13.6 us -> 21.9 us  [spreads(): lax.all_to_all(jnp.broadcast_to(part, (8, WP)), AXES, 0, 0, axis_index_gr...]
    unnamed x12 -> x32, local copies, waits for them, and re-layouts: 5.57 us -> 12.9 us
    ppermute x14, starting transfers between devices: 41.2 us -> 42.8 us  [send(): return lax.ppermute(array, AXES, pairs)]
    all_to_all x2 -> x3, waiting for transfers between devices: 7.57 us -> 7.03 us  [spreads(): lax.all_to_all(jnp.broadcast_to(part, (8, WP)), AXES, 0, 0, axis_index_gr...]
  transfers between devices with their start and end apart: 16 -> 17, of which waited for: 10 -> 10; matrix products, arithmetic and copies ran while one was open for 2% -> 1% of each run, Pallas kernels for 6% -> 5%
where the time goes in v7:
time: 151 us; the launch traced here: 150 us
  starting transfers between devices  64.7 us (43%)
  waiting for transfers between devices  41.2 us (27%)
  Pallas kernels  25.7 us (17%)
  local copies, waits for them, and re-layouts  16.6 us (11%)
  between operations  1.74 us (1%)
    ppermute x14, starting transfers between devices, send(): return lax.ppermute(array, AXES, pairs)  42.8 us
    ppermute x14, waiting for transfers between devices, send(): return lax.ppermute(array, AXES, pairs)  34.2 us
    all_to_all x3, starting transfers between devices, spreads(): lax.all_to_all(jnp.broadcast_to(part, (8, WP)), AXES, 0, 0, axis_index_gr...  21.9 us
    unnamed x32, local copies, waits for them, and re-layouts  12.9 us
    pallas_call x1, Pallas kernels, first_call(): pl.pallas_call(first_kernel, out_shape=(shape(TOK, HALF), shape(TOK, WP),...  11.8 us
    all_to_all x3, waiting for transfers between devices, spreads(): lax.all_to_all(jnp.broadcast_to(part, (8, WP)), AXES, 0, 0, axis_index_gr...  7.03 us
    pallas_call x1, Pallas kernels, grads_call(): pl.pallas_call(grads_kernel, out_shape=shape(1, WP), in_specs=[SM] + [VM]...  3.3 us
  transfers between devices with their start and end apart: 17, of which 10 were waited for; matrix products, arithmetic and copies ran while one was open for 1% of the time, Pallas kernels for 5%

profile of v7, /device:TPU:1, one launch (start us, length us, event | category | flops | bytes accessed | tf_op | source)
XLA Modules:
  0.0 150.4 jit_solution(6919226800312003904)
XLA Ops:
  1.5 1.2 copy-done.8
  2.7 1.2 shard_map.86
  3.8 5.0 %collective-permute-start.2 = (bf16[176,1408]{1,0:T(8,128)(2,1)S(1)}, bf16[176,1408]{1,0:T(8,128)(2,1)S(1)}, u32[]{:S(2)}, u32[]{:S(2)}) collective-permute-start(bf16[176,1408]{1,0:T(8,128)(2,1)S(1)} %shard_map.86), channel_id=1, source_target_pairs={{0,2},{16,24},{32,34},{48,56},{64,66},{80,88},{96,98},{112,120},{1... | collective-permute-start | bytes 1486856 | tf_op jit(solution)/shard_map/ppermute | solution.py:46
  8.9 3.2 %collective-permute-start.1 = (bf16[176,1408]{1,0:T(8,128)(2,1)S(1)}, bf16[176,1408]{1,0:T(8,128)(2,1)S(1)}, u32[]{:S(2)}, u32[]{:S(2)}) collective-permute-start(bf16[176,1408]{1,0:T(8,128)(2,1)S(1)} %shard_map.86), channel_id=1, source_target_pairs={{0,1},{16,20},{32,33},{48,52},{64,65},{80,84},{96,97},{112,116},{1... | collective-permute-start | bytes 1486856 | tf_op jit(solution)/shard_map/ppermute | solution.py:46
  12.1 3.3 %collective-permute-start = (bf16[176,1408]{1,0:T(8,128)(2,1)S(1)}, bf16[176,1408]{1,0:T(8,128)(2,1)S(1)}, u32[]{:S(2)}, u32[]{:S(2)}) collective-permute-start(bf16[176,1408]{1,0:T(8,128)(2,1)S(1)} %shard_map.86), channel_id=1, source_target_pairs={{0,3},{16,284},{32,35},{48,316},{64,67},{80,348},{96,99},{112,380}... | collective-permute-start | bytes 1486856 | tf_op jit(solution)/shard_map/ppermute | solution.py:46
  15.4 0.8 reshape.33
  16.3 1.3 copy-done.7
  17.7 1.1 copy-done.13
  18.8 1.4 shard_map.85
  20.2 7.2 %collective-permute-done.1 = bf16[176,1408]{1,0:T(8,128)(2,1)S(1)} collective-permute-done((bf16[176,1408]{1,0:T(8,128)(2,1)S(1)}, bf16[176,1408]{1,0:T(8,128)(2,1)S(1)}, u32[]{:S(2)}, u32[]{:S(2)}) %collective-permute-start.1) | collective-permute-done | bytes 495648 | tf_op jit(solution)/shard_map/ppermute | solution.py:46
  27.4 2.7 %collective-permute-start.3 = (bf16[2,128,2816]{2,1,0:T(8,128)(2,1)S(1)}, bf16[2,128,2816]{2,1,0:T(8,128)(2,1)S(1)}, u32[]{:S(2)}, u32[]{:S(2)}) collective-permute-start(bf16[2,128,2816]{2,1,0:T(8,128)(2,1)S(1)} %get-tuple-element.41.acts_ref), channel_id=1, source_target_pairs={{0,16},{16,0},{32,48},{48,32},{64,80},{80,64},{96,112},{112,96},{1... | collective-permute-start | bytes 4325384 | tf_op jit(solution)/shard_map/ppermute | solution.py:46
  30.3 3.3 %collective-permute-start.8 = (bf16[2,176,1408]{2,1,0:T(8,128)(2,1)S(1)}, bf16[2,176,1408]{2,1,0:T(8,128)(2,1)S(1)}, u32[]{:S(2)}, u32[]{:S(2)}) collective-permute-start(bf16[2,176,1408]{2,1,0:T(8,128)(2,1)S(1)} %pad_maximum_fusion.1.rest_1_), channel_id=1, source_target_pairs={{0,268},{16,19},{32,300},{48,51},{64,332},{80,83},{96,364},{112,11... | collective-permute-start | bytes 2973704 | tf_op jit(solution)/shard_map/ppermute | solution.py:46
  33.7 2.0 %collective-permute-start.5 = (bf16[2,176,1408]{2,1,0:T(8,128)(2,1)S(1)}, bf16[2,176,1408]{2,1,0:T(8,128)(2,1)S(1)}, u32[]{:S(2)}, u32[]{:S(2)}) collective-permute-start(bf16[2,176,1408]{2,1,0:T(8,128)(2,1)S(1)} %pad_maximum_fusion.rest_0_), channel_id=1, source_target_pairs={{0,4},{16,17},{32,36},{48,49},{64,68},{80,81},{96,100},{112,113},{... | collective-permute-start | bytes 2973704 | tf_op jit(solution)/shard_map/ppermute | solution.py:46
  35.7 2.5 %collective-permute-start.4 = (f32[128,2816]{1,0:T(8,128)S(1)}, f32[128,2816]{1,0:T(8,128)S(1)}, u32[]{:S(2)}, u32[]{:S(2)}) collective-permute-start(f32[128,2816]{1,0:T(8,128)S(1)} %get-tuple-element.44.n0_ref), channel_id=1, source_target_pairs={{0,16},{16,0},{32,48},{48,32},{64,80},{80,64},{96,112},{112,96},{1... | collective-permute-start | bytes 4325384 | tf_op jit(solution)/shard_map/ppermute | solution.py:46
  38.2 2.5 %collective-permute-start.6 = (bf16[2,176,1408]{2,1,0:T(8,128)(2,1)S(1)}, bf16[2,176,1408]{2,1,0:T(8,128)(2,1)S(1)}, u32[]{:S(2)}, u32[]{:S(2)}) collective-permute-start(bf16[2,176,1408]{2,1,0:T(8,128)(2,1)S(1)} %pad_maximum_fusion.1.rest_1_), channel_id=1, source_target_pairs={{0,4},{16,17},{32,36},{48,49},{64,68},{80,81},{96,100},{112,113},{... | collective-permute-start | bytes 2973704 | tf_op jit(solution)/shard_map/ppermute | solution.py:46
  40.7 4.0 %collective-permute-start.7 = (bf16[2,176,1408]{2,1,0:T(8,128)(2,1)S(1)}, bf16[2,176,1408]{2,1,0:T(8,128)(2,1)S(1)}, u32[]{:S(2)}, u32[]{:S(2)}) collective-permute-start(bf16[2,176,1408]{2,1,0:T(8,128)(2,1)S(1)} %pad_maximum_fusion.rest_0_), channel_id=1, source_target_pairs={{0,268},{16,19},{32,300},{48,51},{64,332},{80,83},{96,364},{112,11... | collective-permute-start | bytes 2973704 | tf_op jit(solution)/shard_map/ppermute | solution.py:46
  44.7 0.8 collective-permute-done.8.rest_5_
  45.5 4.5 %collective-permute-start.10 = (bf16[2,176,1408]{2,1,0:T(8,128)(2,1)S(1)}, bf16[2,176,1408]{2,1,0:T(8,128)(2,1)S(1)}, u32[]{:S(2)}, u32[]{:S(2)}) collective-permute-start(bf16[2,176,1408]{2,1,0:T(8,128)(2,1)S(1)} %collective-permute-done.8.rest_5_), channel_id=1, source_target_pairs={{0,268},{16,19},{32,300},{48,51},{64,332},{80,83},{96,364},{112,11... | collective-permute-start | bytes 2973704 | tf_op jit(solution)/shard_map/ppermute | solution.py:46
  50.1 1.9 %collective-permute-start.9 = (bf16[2,176,1408]{2,1,0:T(8,128)(2,1)S(1)}, bf16[2,176,1408]{2,1,0:T(8,128)(2,1)S(1)}, u32[]{:S(2)}, u32[]{:S(2)}) collective-permute-start(bf16[2,176,1408]{2,1,0:T(8,128)(2,1)S(1)} %collective-permute-done.5.rest_2_), channel_id=1, source_target_pairs={{0,4},{16,17},{32,36},{48,49},{64,68},{80,81},{96,100},{112,113},{... | collective-permute-start | bytes 2973704 | tf_op jit(solution)/shard_map/ppermute | solution.py:46
  52.0 8.7 %collective-permute-done.6.rest_3_ = bf16[2,176,1408]{2,1,0:T(8,128)(2,1)S(1)} collective-permute-done((bf16[2,176,1408]{2,1,0:T(8,128)(2,1)S(1)}, bf16[2,176,1408]{2,1,0:T(8,128)(2,1)S(1)}, u32[]{:S(2)}, u32[]{:S(2)}) %collective-permute-start.6) | collective-permute-done | bytes 991264 | tf_op jit(solution)/shard_map/ppermute | solution.py:46
  60.7 6.0 %collective-permute-done.10.rest_7_ = bf16[2,176,1408]{2,1,0:T(8,128)(2,1)S(1)} collective-permute-done((bf16[2,176,1408]{2,1,0:T(8,128)(2,1)S(1)}, bf16[2,176,1408]{2,1,0:T(8,128)(2,1)S(1)}, u32[]{:S(2)}, u32[]{:S(2)}) %collective-permute-start.10) | collective-permute-done | bytes 991264 | tf_op jit(solution)/shard_map/ppermute | solution.py:46
  66.7 4.3 %collective-permute-done.9.rest_6_ = bf16[2,176,1408]{2,1,0:T(8,128)(2,1)S(1)} collective-permute-done((bf16[2,176,1408]{2,1,0:T(8,128)(2,1)S(1)}, bf16[2,176,1408]{2,1,0:T(8,128)(2,1)S(1)}, u32[]{:S(2)}, u32[]{:S(2)}) %collective-permute-start.9) | collective-permute-done | bytes 991264 | tf_op jit(solution)/shard_map/ppermute | solution.py:46
  71.1 11.8 %shard_map.87 = (f32[128,1408]{1,0:T(8,128)S(1)}, f32[128,2816]{1,0:T(8,128)S(1)}, f32[128,4224]{1,0:T(8,128)S(1)}, bf16[2816,1408]{1,0:T(8,128)(2,1)S(1)}) custom-call(s32[4]{0:T(128)S(1)} %pad_add_fusion.place, bf16[2,128,2816]{2,1,0:T(8,128)(2,1)S(1)} %get-tuple-element.41.acts_ref, bf16[2,128,2816]{2,1,0:T(8,128)(2,1)S(1)} %collective-permute-done.3.peer_ref, ...), custom_call_target="tpu_custom_call" | custom-call | flops 4060086272 | bytes 7929856 | tf_op jit(solution)/shard_map/pallas_call | solution.py:233
  82.9 2.0 %collective-permute-start.11 = (f32[128,4224]{1,0:T(8,128)S(1)}, f32[128,4224]{1,0:T(8,128)S(1)}, u32[]{:S(2)}, u32[]{:S(2)}) collective-permute-start(f32[128,4224]{1,0:T(8,128)S(1)} %get-tuple-element.51), channel_id=1, source_target_pairs={{0,16},{16,0},{32,48},{48,32},{64,80},{80,64},{96,112},{112,96},{1... | collective-permute-start | bytes 6488072 | tf_op jit(solution)/shard_map/ppermute | solution.py:46
  84.9 4.1 %collective-permute-done.11.got_ref = f32[128,4224]{1,0:T(8,128)S(1)} collective-permute-done((f32[128,4224]{1,0:T(8,128)S(1)}, f32[128,4224]{1,0:T(8,128)S(1)}, u32[]{:S(2)}, u32[]{:S(2)}) %collective-permute-start.11) | collective-permute-done | bytes 2162720 | tf_op jit(solution)/shard_map/ppermute | solution.py:46
  89.0 2.3 %shard_map.88 = (bf16[2,128,2816]{2,1,0:T(8,128)(2,1)S(1)}, bf16[128,2816]{1,0:T(8,128)(2,1)S(1)}, f32[1,2816]{1,0:T(1,128)S(1)}, f32[128,2816]{1,0:T(8,128)S(1)}) custom-call(s32[4]{0:T(128)S(1)} %pad_add_fusion.place, f32[128,1408]{1,0:T(8,128)S(1)} %get-tuple-element.49.s_ref, f32[128,2816]{1,0:T(8,128)S(1)} %get-tuple-element.50.back_ref, ...), custom_call_target="tpu_custom_call" | custom-call | flops 7208960 | bytes 10000000 | tf_op jit(solution)/shard_map/pallas_call | solution.py:245
  91.4 1.2 copy-done.4
  92.5 0.9 copy-done.9
  93.4 2.2 %collective-permute-start.12 = (bf16[2,128,2816]{2,1,0:T(8,128)(2,1)S(1)}, bf16[2,128,2816]{2,1,0:T(8,128)(2,1)S(1)}, u32[]{:S(2)}, u32[]{:S(2)}) collective-permute-start(bf16[2,128,2816]{2,1,0:T(8,128)(2,1)S(1)} %get-tuple-element.58.next_ref), channel_id=1, source_target_pairs={{0,16},{16,0},{32,48},{48,32},{64,80},{80,64},{96,112},{112,96},{1... | collective-permute-start | bytes 4325384 | tf_op jit(solution)/shard_map/ppermute | solution.py:46
  95.6 2.9 %collective-permute-done.12.peer_ref = bf16[2,128,2816]{2,1,0:T(8,128)(2,1)S(1)} collective-permute-done((bf16[2,128,2816]{2,1,0:T(8,128)(2,1)S(1)}, bf16[2,128,2816]{2,1,0:T(8,128)(2,1)S(1)}, u32[]{:S(2)}, u32[]{:S(2)}) %collective-permute-start.12) | collective-permute-done | bytes 1441824 | tf_op jit(solution)/shard_map/ppermute | solution.py:46
  98.5 3.3 %shard_map.89 = f32[1,2816]{1,0:T(1,128)S(1)} custom-call(s32[4]{0:T(128)S(1)} %pad_add_fusion.place, bf16[2,128,2816]{2,1,0:T(8,128)(2,1)S(1)} %get-tuple-element.58.next_ref, bf16[2,128,2816]{2,1,0:T(8,128)(2,1)S(1)} %collective-permute-done.12.peer_ref, f32[128,2816]{1,0:T(8,128)S(1)} %get-tuple-element.44.n0_ref, ...), custom_call_target="tpu_custom_call" | custom-call | flops 2030043136 | bytes 7929856 | tf_op jit(solution)/shard_map/pallas_call | solution.py:256
  101.9 0.7 broadcast_in_dim.6
  102.5 10.0 %all-to-all-start = ((f32[8,1,2816]{2,1,0:T(1,128)}), f32[8,1,2816]{2,1,0:T(1,128)S(1)}, u32[]{:S(2)}, u32[]{:S(2)}) async-start(f32[8,1,2816]{2,1,0:T(1,128)} %broadcast_in_dim.6), calls=%async_computation | async-start | bytes 180224 | tf_op jit(solution)/shard_map/all_to_all | solution.py:354
  112.6 3.2 %copy-done.1 = bf16[2816,1408]{1,0:T(8,128)(2,1)S(1)} copy-done((bf16[2816,1408]{1,0:T(8,128)(2,1)S(1)}, bf16[2816,1408]{1,0:T(8,128)(2,1)}, u32[]{:S(2)}) %copy-start.1) | copy-done | bytes 7929880
  115.8 2.4 %shard_map.90 = (f32[128,1408]{1,0:T(8,128)S(1)}, f32[128,1408]{1,0:T(8,128)S(1)}) custom-call(bf16[2,128,2816]{2,1,0:T(8,128)(2,1)S(1)} %get-tuple-element.58.next_ref, bf16[2,128,2816]{2,1,0:T(8,128)(2,1)S(1)} %collective-permute-done.12.peer_ref, bf16[2816,1408]{1,0:T(8,128)(2,1)S(1)} %copy-done.1), custom_call_target="tpu_custom_call" | custom-call | flops 2030043136 | bytes 7929856 | tf_op jit(solution)/shard_map/pallas_call | solution.py:267
  118.2 0.9 copy-done.11
  119.1 0.9 copy-done.14
  120.0 3.7 %collective-permute-start.13 = (f32[128,1408]{1,0:T(8,128)}, f32[128,1408]{1,0:T(8,128)S(1)}, u32[]{:S(2)}, u32[]{:S(2)}) collective-permute-start(f32[128,1408]{1,0:T(8,128)} %copy-done.14), channel_id=1, source_target_pairs={{0,16},{16,0},{32,48},{48,32},{64,80},{80,64},{96,112},{112,96},{1... | collective-permute-start | bytes 2162696 | tf_op jit(solution)/shard_map/ppermute | solution.py:46
  123.7 0.7 broadcast_in_dim.7
  124.4 6.0 %all-to-all-start.1 = ((f32[8,1,2816]{2,1,0:T(1,128)}), f32[8,1,2816]{2,1,0:T(1,128)S(1)}, u32[]{:S(2)}, u32[]{:S(2)}) async-start(f32[8,1,2816]{2,1,0:T(1,128)} %broadcast_in_dim.7), calls=%async_computation.1 | async-start | bytes 180224 | tf_op jit(solution)/shard_map/all_to_all | solution.py:354
  130.5 1.1 copy-done.10
  131.6 1.2 shard_map.91
  132.8 5.3 %all-to-all-done.1 = f32[8,1,2816]{2,1,0:T(1,128)S(1)} async-done(((f32[8,1,2816]{2,1,0:T(1,128)}), f32[8,1,2816]{2,1,0:T(1,128)S(1)}, u32[]{:S(2)}, u32[]{:S(2)}) %all-to-all-start.1) | async-done | bytes 90144 | tf_op jit(solution)/shard_map/all_to_all | solution.py:354
  138.8 5.8 %all-to-all-start.2 = ((f32[8,1,2816]{2,1,0:T(1,128)}), f32[8,1,2816]{2,1,0:T(1,128)S(1)}, u32[]{:S(2)}, u32[]{:S(2)}) async-start(f32[8,1,2816]{2,1,0:T(1,128)} %broadcast_in_dim.8), calls=%async_computation.2 | async-start | bytes 180224 | tf_op jit(solution)/shard_map/all_to_all | solution.py:354
  144.6 1.1 copy-done.12
  145.7 2.1 %shard_map.92 = bf16[2640,128]{1,0:T(8,128)(2,1)} custom-call(s32[4]{0:T(128)S(1)} %pad_add_fusion.place, f32[128,1408]{1,0:T(8,128)S(1)} %copy-done.12, f32[128,1408]{1,0:T(8,128)S(1)} %collective-permute-done.13.got_ref, bf16[128,2816]{1,0:T(8,128)(2,1)S(1)} %copy-done.3, f32[128,2816]{1,0:T(8,128)S(1)} %copy-done.5), custom_call_target="tpu_custom_call" | custom-call | flops 1000000 | bytes 5000000 | tf_op jit(solution)/shard_map/pallas_call | solution.py:318
  147.8 1.8 %all-to-all-done.2 = f32[8,1,2816]{2,1,0:T(1,128)S(1)} async-done(((f32[8,1,2816]{2,1,0:T(1,128)}), f32[8,1,2816]{2,1,0:T(1,128)S(1)}, u32[]{:S(2)}, u32[]{:S(2)}) %all-to-all-start.2) | async-done | bytes 90144 | tf_op jit(solution)/shard_map/all_to_all | solution.py:354
  149.7 0.7 reshape.35
  (41 shorter events, 1.5 us)
Async XLA Ops:
  0.6 15.7 %copy-start.6 = (f32[128,2640]{0,1:T(8,128)S(1)}, f32[128,2640]{0,1:T(8,128)}, u32[]{:S(2)}) copy-start(f32[128,2640]{0,1:T(8,128)} %param.6) | copy-start | bytes 4055044
  1.5 1.2 copy-start.8
  3.8 16.4 %collective-permute-start.2 = (bf16[176,1408]{1,0:T(8,128)(2,1)S(1)}, bf16[176,1408]{1,0:T(8,128)(2,1)S(1)}, u32[]{:S(2)}, u32[]{:S(2)}) collective-permute-start(bf16[176,1408]{1,0:T(8,128)(2,1)S(1)} %shard_map.86), channel_id=1, source_target_pairs={{0,2},{16,24},{32,34},{48,56},{64,66},{80,88},{96,98},{112,120},{1... | collective-permute-start | bytes 1486856 | tf_op jit(solution)/shard_map/ppermute | solution.py:46
  8.9 18.5 %collective-permute-start.1 = (bf16[176,1408]{1,0:T(8,128)(2,1)S(1)}, bf16[176,1408]{1,0:T(8,128)(2,1)S(1)}, u32[]{:S(2)}, u32[]{:S(2)}) collective-permute-start(bf16[176,1408]{1,0:T(8,128)(2,1)S(1)} %shard_map.86), channel_id=1, source_target_pairs={{0,1},{16,20},{32,33},{48,52},{64,65},{80,84},{96,97},{112,116},{1... | collective-permute-start | bytes 1486856 | tf_op jit(solution)/shard_map/ppermute | solution.py:46
  12.1 15.3 %collective-permute-start = (bf16[176,1408]{1,0:T(8,128)(2,1)S(1)}, bf16[176,1408]{1,0:T(8,128)(2,1)S(1)}, u32[]{:S(2)}, u32[]{:S(2)}) collective-permute-start(bf16[176,1408]{1,0:T(8,128)(2,1)S(1)} %shard_map.86), channel_id=1, source_target_pairs={{0,3},{16,284},{32,35},{48,316},{64,67},{80,348},{96,99},{112,380}... | collective-permute-start | bytes 1486856 | tf_op jit(solution)/shard_map/ppermute | solution.py:46
  16.3 1.3 copy-start.7
  17.7 1.1 copy-start.13
  20.2 68.8 %copy-start.2 = (bf16[128,2816]{1,0:T(8,128)(2,1)}, bf16[128,2816]{1,0:T(8,128)(2,1)S(1)}, u32[]{:S(2)}) copy-start(bf16[128,2816]{1,0:T(8,128)(2,1)S(1)} %get-tuple-element.52.inj_ref) | copy-start | bytes 2162692
  27.4 8.3 %collective-permute-start.3 = (bf16[2,128,2816]{2,1,0:T(8,128)(2,1)S(1)}, bf16[2,128,2816]{2,1,0:T(8,128)(2,1)S(1)}, u32[]{:S(2)}, u32[]{:S(2)}) collective-permute-start(bf16[2,128,2816]{2,1,0:T(8,128)(2,1)S(1)} %get-tuple-element.41.acts_ref), channel_id=1, source_target_pairs={{0,16},{16,0},{32,48},{48,32},{64,80},{80,64},{96,112},{112,96},{1... | collective-permute-start | bytes 4325384 | tf_op jit(solution)/shard_map/ppermute | solution.py:46
  30.3 15.2 %collective-permute-start.8 = (bf16[2,176,1408]{2,1,0:T(8,128)(2,1)S(1)}, bf16[2,176,1408]{2,1,0:T(8,128)(2,1)S(1)}, u32[]{:S(2)}, u32[]{:S(2)}) collective-permute-start(bf16[2,176,1408]{2,1,0:T(8,128)(2,1)S(1)} %pad_maximum_fusion.1.rest_1_), channel_id=1, source_target_pairs={{0,268},{16,19},{32,300},{48,51},{64,332},{80,83},{96,364},{112,11... | collective-permute-start | bytes 2973704 | tf_op jit(solution)/shard_map/ppermute | solution.py:46
  33.7 16.4 %collective-permute-start.5 = (bf16[2,176,1408]{2,1,0:T(8,128)(2,1)S(1)}, bf16[2,176,1408]{2,1,0:T(8,128)(2,1)S(1)}, u32[]{:S(2)}, u32[]{:S(2)}) collective-permute-start(bf16[2,176,1408]{2,1,0:T(8,128)(2,1)S(1)} %pad_maximum_fusion.rest_0_), channel_id=1, source_target_pairs={{0,4},{16,17},{32,36},{48,49},{64,68},{80,81},{96,100},{112,113},{... | collective-permute-start | bytes 2973704 | tf_op jit(solution)/shard_map/ppermute | solution.py:46
  35.7 16.3 %collective-permute-start.4 = (f32[128,2816]{1,0:T(8,128)S(1)}, f32[128,2816]{1,0:T(8,128)S(1)}, u32[]{:S(2)}, u32[]{:S(2)}) collective-permute-start(f32[128,2816]{1,0:T(8,128)S(1)} %get-tuple-element.44.n0_ref), channel_id=1, source_target_pairs={{0,16},{16,0},{32,48},{48,32},{64,80},{80,64},{96,112},{112,96},{1... | collective-permute-start | bytes 4325384 | tf_op jit(solution)/shard_map/ppermute | solution.py:46
  38.2 22.5 %collective-permute-start.6 = (bf16[2,176,1408]{2,1,0:T(8,128)(2,1)S(1)}, bf16[2,176,1408]{2,1,0:T(8,128)(2,1)S(1)}, u32[]{:S(2)}, u32[]{:S(2)}) collective-permute-start(bf16[2,176,1408]{2,1,0:T(8,128)(2,1)S(1)} %pad_maximum_fusion.1.rest_1_), channel_id=1, source_target_pairs={{0,4},{16,17},{32,36},{48,49},{64,68},{80,81},{96,100},{112,113},{... | collective-permute-start | bytes 2973704 | tf_op jit(solution)/shard_map/ppermute | solution.py:46
  40.7 20.0 %collective-permute-start.7 = (bf16[2,176,1408]{2,1,0:T(8,128)(2,1)S(1)}, bf16[2,176,1408]{2,1,0:T(8,128)(2,1)S(1)}, u32[]{:S(2)}, u32[]{:S(2)}) collective-permute-start(bf16[2,176,1408]{2,1,0:T(8,128)(2,1)S(1)} %pad_maximum_fusion.rest_0_), channel_id=1, source_target_pairs={{0,268},{16,19},{32,300},{48,51},{64,332},{80,83},{96,364},{112,11... | collective-permute-start | bytes 2973704 | tf_op jit(solution)/shard_map/ppermute | solution.py:46
  45.5 21.2 %collective-permute-start.10 = (bf16[2,176,1408]{2,1,0:T(8,128)(2,1)S(1)}, bf16[2,176,1408]{2,1,0:T(8,128)(2,1)S(1)}, u32[]{:S(2)}, u32[]{:S(2)}) collective-permute-start(bf16[2,176,1408]{2,1,0:T(8,128)(2,1)S(1)} %collective-permute-done.8.rest_5_), channel_id=1, source_target_pairs={{0,268},{16,19},{32,300},{48,51},{64,332},{80,83},{96,364},{112,11... | collective-permute-start | bytes 2973704 | tf_op jit(solution)/shard_map/ppermute | solution.py:46
  50.1 20.9 %collective-permute-start.9 = (bf16[2,176,1408]{2,1,0:T(8,128)(2,1)S(1)}, bf16[2,176,1408]{2,1,0:T(8,128)(2,1)S(1)}, u32[]{:S(2)}, u32[]{:S(2)}) collective-permute-start(bf16[2,176,1408]{2,1,0:T(8,128)(2,1)S(1)} %collective-permute-done.5.rest_2_), channel_id=1, source_target_pairs={{0,4},{16,17},{32,36},{48,49},{64,68},{80,81},{96,100},{112,113},{... | collective-permute-start | bytes 2973704 | tf_op jit(solution)/shard_map/ppermute | solution.py:46
  82.9 15.6 %copy-start = (bf16[2816,1408]{1,0:T(8,128)(2,1)}, bf16[2816,1408]{1,0:T(8,128)(2,1)S(1)}, u32[]{:S(2)}) copy-start(bf16[2816,1408]{1,0:T(8,128)(2,1)S(1)} %get-tuple-element.57.w_ref) | copy-start | bytes 23789572
  82.9 6.1 %collective-permute-start.11 = (f32[128,4224]{1,0:T(8,128)S(1)}, f32[128,4224]{1,0:T(8,128)S(1)}, u32[]{:S(2)}, u32[]{:S(2)}) collective-permute-start(f32[128,4224]{1,0:T(8,128)S(1)} %get-tuple-element.51), channel_id=1, source_target_pairs={{0,16},{16,0},{32,48},{48,32},{64,80},{80,64},{96,112},{112,96},{1... | collective-permute-start | bytes 6488072 | tf_op jit(solution)/shard_map/ppermute | solution.py:46
  91.3 1.2 copy-start.4
  92.5 0.9 copy-start.9
  93.4 5.1 %collective-permute-start.12 = (bf16[2,128,2816]{2,1,0:T(8,128)(2,1)S(1)}, bf16[2,128,2816]{2,1,0:T(8,128)(2,1)S(1)}, u32[]{:S(2)}, u32[]{:S(2)}) collective-permute-start(bf16[2,128,2816]{2,1,0:T(8,128)(2,1)S(1)} %get-tuple-element.58.next_ref), channel_id=1, source_target_pairs={{0,16},{16,0},{32,48},{48,32},{64,80},{80,64},{96,112},{112,96},{1... | collective-permute-start | bytes 4325384 | tf_op jit(solution)/shard_map/ppermute | solution.py:46
  102.5 17.4 %all-to-all-start = ((f32[8,1,2816]{2,1,0:T(1,128)}), f32[8,1,2816]{2,1,0:T(1,128)S(1)}, u32[]{:S(2)}, u32[]{:S(2)}) async-start(f32[8,1,2816]{2,1,0:T(1,128)} %broadcast_in_dim.6), calls=%async_computation | async-start | bytes 180224 | tf_op jit(solution)/shard_map/all_to_all | solution.py:354
  112.6 3.3 %copy-start.1 = (bf16[2816,1408]{1,0:T(8,128)(2,1)S(1)}, bf16[2816,1408]{1,0:T(8,128)(2,1)}, u32[]{:S(2)}) copy-start(bf16[2816,1408]{1,0:T(8,128)(2,1)} %copy-done) | copy-start | bytes 23789572
  118.2 0.9 copy-start.11
  119.1 0.9 copy-start.14
  120.0 24.6 %copy-start.3 = (bf16[128,2816]{1,0:T(8,128)(2,1)S(1)}, bf16[128,2816]{1,0:T(8,128)(2,1)}, u32[]{:S(2)}) copy-start(bf16[128,2816]{1,0:T(8,128)(2,1)} %copy-done.2) | copy-start | bytes 2162692
  120.0 24.6 %copy-start.5 = (f32[128,2816]{1,0:T(8,128)S(1)}, f32[128,2816]{1,0:T(8,128)}, u32[]{:S(2)}) copy-start(f32[128,2816]{1,0:T(8,128)} %copy-done.4) | copy-start | bytes 4325380
  120.0 18.1 %collective-permute-start.13 = (f32[128,1408]{1,0:T(8,128)}, f32[128,1408]{1,0:T(8,128)S(1)}, u32[]{:S(2)}, u32[]{:S(2)}) collective-permute-start(f32[128,1408]{1,0:T(8,128)} %copy-done.14), channel_id=1, source_target_pairs={{0,16},{16,0},{32,48},{48,32},{64,80},{80,64},{96,112},{112,96},{1... | collective-permute-start | bytes 2162696 | tf_op jit(solution)/shard_map/ppermute | solution.py:46
  124.4 13.6 %all-to-all-start.1 = ((f32[8,1,2816]{2,1,0:T(1,128)}), f32[8,1,2816]{2,1,0:T(1,128)S(1)}, u32[]{:S(2)}, u32[]{:S(2)}) async-start(f32[8,1,2816]{2,1,0:T(1,128)} %broadcast_in_dim.7), calls=%async_computation.1 | async-start | bytes 180224 | tf_op jit(solution)/shard_map/all_to_all | solution.py:354
  130.4 1.1 copy-start.10
  138.8 10.8 %all-to-all-start.2 = ((f32[8,1,2816]{2,1,0:T(1,128)}), f32[8,1,2816]{2,1,0:T(1,128)S(1)}, u32[]{:S(2)}, u32[]{:S(2)}) async-start(f32[8,1,2816]{2,1,0:T(1,128)} %broadcast_in_dim.8), calls=%async_computation.2 | async-start | bytes 180224 | tf_op jit(solution)/shard_map/all_to_all | solution.py:354
  144.6 1.1 copy-start.12

commit v8 on v7

--- a/solution.py
+++ b/solution.py
@@ -84,7 +84,7 @@
         compiler_params=pltpu.CompilerParams(vmem_limit_bytes=16 * 2**20),
     )(place, w)
 
-def prepare_kernel(state_ref, inj_ref, cot_ref, gain_ref, n0_ref, acts_ref, injw_ref, cotw_ref, wide_ref, tall_ref):
+def prepare_kernel(state_ref, inj_ref, cot_ref, gain_ref, n0_ref, n0b_ref, acts_ref, injw_ref, cotw_ref, wide_ref, tall_ref):
     def regroup(src_ref):
         for s in range(16):
             wide_ref[SP * s : SP * s + SH, :] = src_ref[SH * s : SH * s + SH, :]
@@ -103,6 +103,7 @@
         cols = slice(128 * t, 128 * t + 128)
         n0 = n0_ref[:, cols] * inv
         n0_ref[:, cols] = n0
+        n0b_ref[:, cols] = n0.astype(BF)
         acts_ref[0, :, cols] = (n0 * gain_ref[:, cols]).astype(BF)
     regroup(cot_ref)
     for t in range(WP // 128):
@@ -121,9 +122,9 @@
     wide = lambda dt: jax.ShapeDtypeStruct((TOK, WP), dt)
     return pl.pallas_call(
         prepare_kernel,
-        out_shape=(wide(F32), jax.ShapeDtypeStruct((2, TOK, WP), BF), wide(BF), wide(F32)),
+        out_shape=(wide(F32), wide(BF), jax.ShapeDtypeStruct((2, TOK, WP), BF), wide(BF), wide(F32)),
         in_specs=[vm] * 4,
-        out_specs=(vm,) * 4,
+        out_specs=(vm,) * 5,
         scratch_shapes=[pltpu.VMEM((WP, TOK), F32), pltpu.VMEM((W, TOK), F32)],
         compiler_params=pltpu.CompilerParams(vmem_limit_bytes=24 * 2**20),
         cost_estimate=pl.CostEstimate(flops=10**6, bytes_accessed=10**7, transcendentals=0),
@@ -159,19 +160,19 @@
         c.wait()
     s1 = jnp.dot(both_ref[...], w_ref[...], preferred_element_type=F32)
     s_ref[...] = s1[:TOK]
-    give_ref[:, :HALF] = s1[TOK:]
+    give_ref[:, :HALF] = s1[TOK:].astype(BF)
     for t in range(2):
         rows = slice(t * HALF, t * HALF + HALF)
         back = nt(grads, w_ref[rows, :])
         back_ref[:, rows] = back[:TOK]
-        give_ref[:, HALF + t * HALF : 2 * HALF + t * HALF] = back[TOK:]
-
-
-def middle_kernel(place, s_ref, back_ref, got_ref, n0_ref, inj_ref, cot_ref, gain_ref, next_ref, injg_ref, part_ref, s1_ref):
+        give_ref[:, HALF + t * HALF : 2 * HALF + t * HALF] = back[TOK:].astype(BF)
+
+
+def middle_kernel(place, s_ref, back_ref, got_ref, n0_ref, inj_ref, cot_ref, gain_ref, next_ref, injg_ref, part_ref, s1_out_ref, s1_ref):
     pc, deep = place[2], place[3] >= 2
     mine, other = half_of(pc), half_of(1 - pc)
     s1_ref[:, mine] = s_ref[...] + inj_ref[:, mine].astype(F32)
-    s1_ref[:, other] = got_ref[:, :HALF] + inj_ref[:, other].astype(F32)
+    s1_ref[:, other] = got_ref[:, :HALF].astype(F32) + inj_ref[:, other].astype(F32)
     acc = jnp.zeros((TOK, 128), F32)
     for t in range(WP // 128):
         s1 = s1_ref[:, 128 * t : 128 * t + 128]
@@ -181,7 +182,7 @@
     def second(t, acc):
         cols = pl.ds(pl.multiple_of(t * TILE, TILE), TILE)
         n1 = s1_ref[:, cols] * inv1
-        back = back_ref[:, cols] + got_ref[:, pl.ds(pl.multiple_of(HALF + t * TILE, 128), TILE)]
+        back = back_ref[:, cols] + got_ref[:, pl.ds(pl.multiple_of(HALF + t * TILE, 128), TILE)].astype(F32)
         gain = gain_ref[:, cols]
         next_ref[0, :, cols] = (n1 * gain).astype(BF)
         part_ref[:, cols] = jnp.sum(back * jnp.where(deep, n1, n0_ref[:, cols]), axis=0, keepdims=True)
@@ -193,10 +194,11 @@
     def third(t, carry):
         cols = pl.ds(pl.multiple_of(t * TILE, TILE), TILE)
         n1 = s1_ref[:, cols] * inv1
-        back = back_ref[:, cols] + got_ref[:, pl.ds(pl.multiple_of(HALF + t * TILE, 128), TILE)]
+        back = back_ref[:, cols] + got_ref[:, pl.ds(pl.multiple_of(HALF + t * TILE, 128), TILE)].astype(F32)
         d1 = jnp.where(deep, inv1 * (back * gain_ref[:, cols] - n1 * mean1), 0.0)
         next_ref[1, :, cols] = d1.astype(BF)
         injg_ref[:, cols] = (cot_ref[:, cols] + d1).astype(BF)
+        s1_out_ref[:, cols] = s1_ref[:, cols].astype(BF)
         return carry
 
     lax.fori_loop(0, WP // TILE, third, 0)
@@ -208,7 +210,7 @@
     for t in range(2):
         rows = slice(t * HALF, t * HALF + HALF)
         back = nt(grads, w_ref[rows, :])
-        sums = jnp.sum(back[:TOK] * n0_ref[:, rows] + back[TOK:] * n0_peer_ref[:, rows], axis=0, keepdims=True)
+        sums = jnp.sum(back[:TOK] * n0_ref[:, rows] + back[TOK:] * n0_peer_ref[:, rows].astype(F32), axis=0, keepdims=True)
         part_ref[:, rows] = part1_ref[:, rows] + sums
 
 
@@ -232,7 +234,7 @@
 def first_call(place, acts, peer, pieces):
     return pl.pallas_call(
         first_kernel,
-        out_shape=(shape(TOK, HALF), shape(TOK, WP), shape(TOK, HALF + WP), shape(WP, HALF, dtype=BF)),
+        out_shape=(shape(TOK, HALF), shape(TOK, WP), shape(TOK, HALF + WP, dtype=BF), shape(WP, HALF, dtype=BF)),
         in_specs=[SM, VM, VM] + [HB] * 8,
         out_specs=(VM,) * 4,
         scratch_shapes=[pltpu.VMEM((ALL, WP), BF), pltpu.SemaphoreType.DMA((16,))],
@@ -244,9 +246,10 @@
 def middle_call(place, s_own, back, got, n0, inj, cot, gain):
     return pl.pallas_call(
         middle_kernel,
-        out_shape=(shape(2, TOK, WP, dtype=BF), shape(TOK, WP, dtype=BF), shape(1, WP), shape(TOK, WP)),
+        out_shape=(shape(2, TOK, WP, dtype=BF), shape(TOK, WP, dtype=BF), shape(1, WP), shape(TOK, WP, dtype=BF)),
         in_specs=[SM] + [VM] * 7,
         out_specs=(VM,) * 4,
+        scratch_shapes=[pltpu.VMEM((TOK, WP), F32)],
         compiler_params=pltpu.CompilerParams(vmem_limit_bytes=20 * 2**20),
         cost_estimate=pl.CostEstimate(flops=20 * TOK * WP, bytes_accessed=10**7, transcendentals=0),
     )(place, s_own, back, got, n0, inj, cot, gain)
@@ -295,7 +298,7 @@
     for t in range(WP // 128):
         cols = slice(128 * t, 128 * t + 128)
         s2 = s2_ref[:, cols] + inj_ref[:, cols].astype(F32)
-        wide_ref[cols, :] = jnp.where(deep, s2, s1_ref[:, cols]).T
+        wide_ref[cols, :] = jnp.where(deep, s2, s1_ref[:, cols].astype(F32)).T
     tighten(wide_ref, tall_ref, out_ref)
 
 
@@ -364,19 +367,20 @@
     place = jnp.stack([fs % 4, fs // 4, pc, counts[0]]).astype(jnp.int32)
     gain_w = jnp.pad(gain.reshape(16, SH), ((0, 0), (0, SP - SH))).reshape(1, WP)
     acts = prepare(state0, injected, cotangent, gain_w)
-    (n0, acts, inj, cot), pieces = gather(spread(place, core_weight), acts)
-    peer, n0 = lax.optimization_barrier((send(acts, SWAP), n0))
-    peer, n0_peer = lax.optimization_barrier((peer, send(n0, SWAP)))
+    (n0, n0_small, acts, inj, cot), pieces = gather(spread(place, core_weight), acts)
+    peer = send(acts, SWAP)
     s_own, back, give, half = first_call(place, acts, peer, pieces)
-    nexts, injg, part1, s1 = middle_call(place, s_own, back, send(give, SWAP), n0, inj, cot, gain_w)
+    n0_small, give = lax.optimization_barrier((n0_small, give))
+    n0_peer, got = lax.optimization_barrier((send(n0_small, SWAP), send(give, SWAP)))
+    nexts, injg, part1, s1 = middle_call(place, s_own, back, got, n0, inj, cot, gain_w)
     peer = send(nexts, SWAP)
     part = grads_call(place, nexts, peer, n0, n0_peer, part1, half)
-    nexts, peer, part = lax.optimization_barrier((nexts, peer, part))
-    every = spreads(part, "z")
     s_own, give = state_call(nexts, peer, half)
-    s_own, give, every = lax.optimization_barrier((s_own, give, every))
+    s_own, give, part = lax.optimization_barrier((s_own, give, part))
+    part = gathered(spreads(part, "z"))
+    give, part = lax.optimization_barrier((give, part))
     got = send(give, SWAP)
-    every = spreads(gathered(every), "y")
+    every = spreads(part, "y")
     got, injg, every = lax.optimization_barrier((got, flip_call(injg), every))
     every = spreads(gathered(every), "xc")
     final = final_call(place, s_own, got, inj, s1)

time: 151 us -> 149 us (0.987)
  blocking collectives: 0 us -> 17.2 us
  local copies, waits for them, and re-layouts: 16.6 us -> 6.72 us
  starting transfers between devices: 64.7 us -> 55.2 us
  waiting for transfers between devices: 41.2 us -> 39.4 us
    all_to_all x0 -> x1, blocking collectives: none -> 17.2 us  [spreads(): lax.all_to_all(jnp.broadcast_to(part, (8, WP)), AXES, 0, 0, axis_index_gr...]
    all_to_all x3 -> x2, starting transfers between devices: 21.9 us -> 10.8 us  [spreads(): lax.all_to_all(jnp.broadcast_to(part, (8, WP)), AXES, 0, 0, axis_index_gr...]
    unnamed x32 -> x11, local copies, waits for them, and re-layouts: 12.9 us -> 3.61 us
    ppermute x14, waiting for transfers between devices: 34.2 us -> 30.7 us  [send(): return lax.ppermute(array, AXES, pairs)]
    all_to_all x3 -> x2, waiting for transfers between devices: 7.03 us -> 8.68 us  [spreads(): lax.all_to_all(jnp.broadcast_to(part, (8, WP)), AXES, 0, 0, axis_index_gr...]
    ppermute x14, starting transfers between devices: 42.8 us -> 44.4 us  [send(): return lax.ppermute(array, AXES, pairs)]
  transfers between devices with their start and end apart: 17 -> 16, of which waited for: 10 -> 9; matrix products, arithmetic and copies ran while one was open for 1% -> 1% of each run, Pallas kernels for 5% -> 4%
where the time goes in v8:
time: 149 us; the launch traced here: 148 us
  starting transfers between devices  55.2 us (37%)
  waiting for transfers between devices  39.4 us (26%)
  Pallas kernels  26.6 us (18%)
  blocking collectives  17.2 us (12%)
  local copies, waits for them, and re-layouts  6.72 us (5%)
  other arithmetic  1.7 us (1%)
  between operations  1.7 us (1%)
    ppermute x14, starting transfers between devices, send(): return lax.ppermute(array, AXES, pairs)  44.4 us
    ppermute x14, waiting for transfers between devices, send(): return lax.ppermute(array, AXES, pairs)  30.7 us
    all_to_all x1, blocking collectives, spreads(): lax.all_to_all(jnp.broadcast_to(part, (8, WP)), AXES, 0, 0, axis_index_gr...  17.2 us
    pallas_call x1, Pallas kernels, first_call(): pl.pallas_call(first_kernel, out_shape=(shape(TOK, HALF), shape(TOK, WP),...  11.8 us
    all_to_all x2, starting transfers between devices, spreads(): lax.all_to_all(jnp.broadcast_to(part, (8, WP)), AXES, 0, 0, axis_index_gr...  10.8 us
    all_to_all x2, waiting for transfers between devices, spreads(): lax.all_to_all(jnp.broadcast_to(part, (8, WP)), AXES, 0, 0, axis_index_gr...  8.68 us
    unnamed x11, local copies, waits for them, and re-layouts  3.61 us
    pallas_call x1, Pallas kernels, grads_call(): pl.pallas_call(grads_kernel, out_shape=shape(1, WP), in_specs=[SM] + [VM]...  3.31 us
  transfers between devices with their start and end apart: 16, of which 9 were waited for; matrix products, arithmetic and copies ran while one was open for 1% of the time, Pallas kernels for 4%

profile of v8, /device:TPU:1, one launch (start us, length us, event | category | flops | bytes accessed | tf_op | source)
XLA Modules:
  0.0 148.5 jit_solution(4647505378659617682)
XLA Ops:
  1.4 0.1 pad_add_fusion.place
  1.5 1.2 copy-done.2
  2.7 1.2 shard_map.86
  3.8 5.0 %collective-permute-start.2 = (bf16[176,1408]{1,0:T(8,128)(2,1)S(1)}, bf16[176,1408]{1,0:T(8,128)(2,1)}, u32[]{:S(2)}, u32[]{:S(2)}) collective-permute-start(bf16[176,1408]{1,0:T(8,128)(2,1)S(1)} %shard_map.86), channel_id=1, source_target_pairs={{0,2},{16,24},{32,34},{48,56},{64,66},{80,88},{96,98},{112,120},{1... | collective-permute-start | bytes 1486856 | tf_op jit(solution)/shard_map/ppermute | solution.py:46
  8.9 3.2 %collective-permute-start.1 = (bf16[176,1408]{1,0:T(8,128)(2,1)S(1)}, bf16[176,1408]{1,0:T(8,128)(2,1)S(1)}, u32[]{:S(2)}, u32[]{:S(2)}) collective-permute-start(bf16[176,1408]{1,0:T(8,128)(2,1)S(1)} %shard_map.86), channel_id=1, source_target_pairs={{0,1},{16,20},{32,33},{48,52},{64,65},{80,84},{96,97},{112,116},{1... | collective-permute-start | bytes 1486856 | tf_op jit(solution)/shard_map/ppermute | solution.py:46
  12.1 3.3 %collective-permute-start = (bf16[176,1408]{1,0:T(8,128)(2,1)S(1)}, bf16[176,1408]{1,0:T(8,128)(2,1)}, u32[]{:S(2)}, u32[]{:S(2)}) collective-permute-start(bf16[176,1408]{1,0:T(8,128)(2,1)S(1)} %shard_map.86), channel_id=1, source_target_pairs={{0,3},{16,284},{32,35},{48,316},{64,67},{80,348},{96,99},{112,380}... | collective-permute-start | bytes 1486856 | tf_op jit(solution)/shard_map/ppermute | solution.py:46
  15.4 0.8 reshape.33
  16.2 0.1 reshape.34.gain_ref
  16.3 1.3 copy-done.1
  17.7 1.1 copy-done.3
  18.8 1.5 %shard_map.85 = (f32[128,2816]{1,0:T(8,128)S(1)}, bf16[128,2816]{1,0:T(8,128)(2,1)S(1)}, bf16[2,128,2816]{2,1,0:T(8,128)(2,1)S(1)}, bf16[128,2816]{1,0:T(8,128)(2,1)S(1)}, f32[128,2816]{1,0:T(8,128)S(1)}) custom-call(f32[2640,128]{1,0:T(8,128)S(1)} %bitcast.17, bf16[2640,128]{1,0:T(8,128)(2,1)S(1)} %bitcast.19, f32[2640,128]{1,0:T(8,128)S(1)} %bitcast.18, ...), custom_call_target="tpu_custom_call" | custom-call | flops 1000000 | bytes 10000000 | tf_op jit(solution)/shard_map/pallas_call | solution.py:123
  20.3 7.1 %collective-permute-done.1 = bf16[176,1408]{1,0:T(8,128)(2,1)S(1)} collective-permute-done((bf16[176,1408]{1,0:T(8,128)(2,1)S(1)}, bf16[176,1408]{1,0:T(8,128)(2,1)S(1)}, u32[]{:S(2)}, u32[]{:S(2)}) %collective-permute-start.1) | collective-permute-done | bytes 495648 | tf_op jit(solution)/shard_map/ppermute | solution.py:46
  27.4 1.3 pad_maximum_fusion.1.rest_1_
  28.7 4.1 %collective-permute-start.7 = (bf16[2,176,1408]{2,1,0:T(8,128)(2,1)S(1)}, bf16[2,176,1408]{2,1,0:T(8,128)(2,1)S(1)}, u32[]{:S(2)}, u32[]{:S(2)}) collective-permute-start(bf16[2,176,1408]{2,1,0:T(8,128)(2,1)S(1)} %pad_maximum_fusion.1.rest_1_), channel_id=1, source_target_pairs={{0,268},{16,19},{32,300},{48,51},{64,332},{80,83},{96,364},{112,11... | collective-permute-start | bytes 2973704 | tf_op jit(solution)/shard_map/ppermute | solution.py:46
  32.8 0.1 pad_maximum_fusion.rest_0_
  32.9 1.9 %collective-permute-start.4 = (bf16[2,176,1408]{2,1,0:T(8,128)(2,1)S(1)}, bf16[2,176,1408]{2,1,0:T(8,128)(2,1)S(1)}, u32[]{:S(2)}, u32[]{:S(2)}) collective-permute-start(bf16[2,176,1408]{2,1,0:T(8,128)(2,1)S(1)} %pad_maximum_fusion.rest_0_), channel_id=1, source_target_pairs={{0,4},{16,17},{32,36},{48,49},{64,68},{80,81},{96,100},{112,113},{... | collective-permute-start | bytes 2973704 | tf_op jit(solution)/shard_map/ppermute | solution.py:46
  34.9 2.6 %collective-permute-start.3 = (bf16[2,128,2816]{2,1,0:T(8,128)(2,1)S(1)}, bf16[2,128,2816]{2,1,0:T(8,128)(2,1)S(1)}, u32[]{:S(2)}, u32[]{:S(2)}) collective-permute-start(bf16[2,128,2816]{2,1,0:T(8,128)(2,1)S(1)} %get-tuple-element.43.acts_ref), channel_id=1, source_target_pairs={{0,16},{16,0},{32,48},{48,32},{64,80},{80,64},{96,112},{112,96},{1... | collective-permute-start | bytes 4325384 | tf_op jit(solution)/shard_map/ppermute | solution.py:46
  37.4 2.2 %collective-permute-start.5 = (bf16[2,176,1408]{2,1,0:T(8,128)(2,1)S(1)}, bf16[2,176,1408]{2,1,0:T(8,128)(2,1)S(1)}, u32[]{:S(2)}, u32[]{:S(2)}) collective-permute-start(bf16[2,176,1408]{2,1,0:T(8,128)(2,1)S(1)} %pad_maximum_fusion.1.rest_1_), channel_id=1, source_target_pairs={{0,4},{16,17},{32,36},{48,49},{64,68},{80,81},{96,100},{112,113},{... | collective-permute-start | bytes 2973704 | tf_op jit(solution)/shard_map/ppermute | solution.py:46
  39.7 4.3 %collective-permute-start.6 = (bf16[2,176,1408]{2,1,0:T(8,128)(2,1)S(1)}, bf16[2,176,1408]{2,1,0:T(8,128)(2,1)S(1)}, u32[]{:S(2)}, u32[]{:S(2)}) collective-permute-start(bf16[2,176,1408]{2,1,0:T(8,128)(2,1)S(1)} %pad_maximum_fusion.rest_0_), channel_id=1, source_target_pairs={{0,268},{16,19},{32,300},{48,51},{64,332},{80,83},{96,364},{112,11... | collective-permute-start | bytes 2973704 | tf_op jit(solution)/shard_map/ppermute | solution.py:46
  44.0 5.3 %collective-permute-start.9 = (bf16[2,176,1408]{2,1,0:T(8,128)(2,1)S(1)}, bf16[2,176,1408]{2,1,0:T(8,128)(2,1)S(1)}, u32[]{:S(2)}, u32[]{:S(2)}) collective-permute-start(bf16[2,176,1408]{2,1,0:T(8,128)(2,1)S(1)} %collective-permute-done.7.rest_5_), channel_id=1, source_target_pairs={{0,268},{16,19},{32,300},{48,51},{64,332},{80,83},{96,364},{112,11... | collective-permute-start | bytes 2973704 | tf_op jit(solution)/shard_map/ppermute | solution.py:46
  49.2 0.1 collective-permute-done.4.rest_2_
  49.4 1.9 %collective-permute-start.8 = (bf16[2,176,1408]{2,1,0:T(8,128)(2,1)S(1)}, bf16[2,176,1408]{2,1,0:T(8,128)(2,1)S(1)}, u32[]{:S(2)}, u32[]{:S(2)}) collective-permute-start(bf16[2,176,1408]{2,1,0:T(8,128)(2,1)S(1)} %collective-permute-done.4.rest_2_), channel_id=1, source_target_pairs={{0,4},{16,17},{32,36},{48,49},{64,68},{80,81},{96,100},{112,113},{... | collective-permute-start | bytes 2973704 | tf_op jit(solution)/shard_map/ppermute | solution.py:46
  51.3 8.7 %collective-permute-done.5.rest_3_ = bf16[2,176,1408]{2,1,0:T(8,128)(2,1)S(1)} collective-permute-done((bf16[2,176,1408]{2,1,0:T(8,128)(2,1)S(1)}, bf16[2,176,1408]{2,1,0:T(8,128)(2,1)S(1)}, u32[]{:S(2)}, u32[]{:S(2)}) %collective-permute-start.5) | collective-permute-done | bytes 991264 | tf_op jit(solution)/shard_map/ppermute | solution.py:46
  60.0 5.7 %collective-permute-done.9.rest_7_ = bf16[2,176,1408]{2,1,0:T(8,128)(2,1)S(1)} collective-permute-done((bf16[2,176,1408]{2,1,0:T(8,128)(2,1)S(1)}, bf16[2,176,1408]{2,1,0:T(8,128)(2,1)S(1)}, u32[]{:S(2)}, u32[]{:S(2)}) %collective-permute-start.9) | collective-permute-done | bytes 991264 | tf_op jit(solution)/shard_map/ppermute | solution.py:46
  65.7 4.6 %collective-permute-done.8.rest_6_ = bf16[2,176,1408]{2,1,0:T(8,128)(2,1)S(1)} collective-permute-done((bf16[2,176,1408]{2,1,0:T(8,128)(2,1)S(1)}, bf16[2,176,1408]{2,1,0:T(8,128)(2,1)S(1)}, u32[]{:S(2)}, u32[]{:S(2)}) %collective-permute-start.8) | collective-permute-done | bytes 991264 | tf_op jit(solution)/shard_map/ppermute | solution.py:46
  70.3 11.8 %shard_map.87 = (f32[128,1408]{1,0:T(8,128)S(1)}, f32[128,2816]{1,0:T(8,128)S(1)}, bf16[128,4224]{1,0:T(8,128)(2,1)S(1)}, bf16[2816,1408]{1,0:T(8,128)(2,1)S(1)}) custom-call(s32[4]{0:T(128)S(1)} %pad_add_fusion.place, bf16[2,128,2816]{2,1,0:T(8,128)(2,1)S(1)} %get-tuple-element.43.acts_ref, bf16[2,128,2816]{2,1,0:T(8,128)(2,1)S(1)} %collective-permute-done.3.peer_ref, ...), custom_call_target="tpu_custom_call" | custom-call | flops 4060086272 | bytes 7929856 | tf_op jit(solution)/shard_map/pallas_call | solution.py:235
  82.1 1.9 %collective-permute-start.11 = (bf16[128,4224]{1,0:T(8,128)(2,1)S(1)}, bf16[128,4224]{1,0:T(8,128)(2,1)S(1)}, u32[]{:S(2)}, u32[]{:S(2)}) collective-permute-start(bf16[128,4224]{1,0:T(8,128)(2,1)S(1)} %get-tuple-element.52), channel_id=1, source_target_pairs={{0,16},{16,0},{32,48},{48,32},{64,80},{80,64},{96,112},{112,96},{1... | collective-permute-start | bytes 3244040 | tf_op jit(solution)/shard_map/ppermute | solution.py:46
  84.0 2.4 %collective-permute-start.10 = (bf16[128,2816]{1,0:T(8,128)(2,1)S(1)}, bf16[128,2816]{1,0:T(8,128)(2,1)S(1)}, u32[]{:S(2)}, u32[]{:S(2)}) collective-permute-start(bf16[128,2816]{1,0:T(8,128)(2,1)S(1)} %get-tuple-element.51), channel_id=1, source_target_pairs={{0,16},{16,0},{32,48},{48,32},{64,80},{80,64},{96,112},{112,96},{1... | collective-permute-start | bytes 2162696 | tf_op jit(solution)/shard_map/ppermute | solution.py:46
  86.5 1.8 %collective-permute-done.10.n0_peer_ref = bf16[128,2816]{1,0:T(8,128)(2,1)S(1)} collective-permute-done((bf16[128,2816]{1,0:T(8,128)(2,1)S(1)}, bf16[128,2816]{1,0:T(8,128)(2,1)S(1)}, u32[]{:S(2)}, u32[]{:S(2)}) %collective-permute-start.10) | collective-permute-done | bytes 720928 | tf_op jit(solution)/shard_map/ppermute | solution.py:46
  88.3 2.4 %shard_map.88 = (bf16[2,128,2816]{2,1,0:T(8,128)(2,1)S(1)}, bf16[128,2816]{1,0:T(8,128)(2,1)S(1)}, f32[1,2816]{1,0:T(1,128)S(1)}, bf16[128,2816]{1,0:T(8,128)(2,1)S(1)}) custom-call(s32[4]{0:T(128)S(1)} %pad_add_fusion.place, f32[128,1408]{1,0:T(8,128)S(1)} %get-tuple-element.47.s_ref, f32[128,2816]{1,0:T(8,128)S(1)} %get-tuple-element.48.back_ref, ...), custom_call_target="tpu_custom_call" | custom-call | flops 7208960 | bytes 10000000 | tf_op jit(solution)/shard_map/pallas_call | solution.py:247
  90.7 2.5 %collective-permute-start.12 = (bf16[2,128,2816]{2,1,0:T(8,128)(2,1)S(1)}, bf16[2,128,2816]{2,1,0:T(8,128)(2,1)S(1)}, u32[]{:S(2)}, u32[]{:S(2)}) collective-permute-start(bf16[2,128,2816]{2,1,0:T(8,128)(2,1)S(1)} %get-tuple-element.57.next_ref), channel_id=1, source_target_pairs={{0,16},{16,0},{32,48},{48,32},{64,80},{80,64},{96,112},{112,96},{1... | collective-permute-start | bytes 4325384 | tf_op jit(solution)/shard_map/ppermute | solution.py:46
  93.2 2.6 %collective-permute-done.12.peer_ref = bf16[2,128,2816]{2,1,0:T(8,128)(2,1)S(1)} collective-permute-done((bf16[2,128,2816]{2,1,0:T(8,128)(2,1)S(1)}, bf16[2,128,2816]{2,1,0:T(8,128)(2,1)S(1)}, u32[]{:S(2)}, u32[]{:S(2)}) %collective-permute-start.12) | collective-permute-done | bytes 1441824 | tf_op jit(solution)/shard_map/ppermute | solution.py:46
  95.8 2.4 %shard_map.89 = (f32[128,1408]{1,0:T(8,128)S(1)}, f32[128,1408]{1,0:T(8,128)S(1)}) custom-call(bf16[2,128,2816]{2,1,0:T(8,128)(2,1)S(1)} %get-tuple-element.57.next_ref, bf16[2,128,2816]{2,1,0:T(8,128)(2,1)S(1)} %collective-permute-done.12.peer_ref, bf16[2816,1408]{1,0:T(8,128)(2,1)S(1)} %get-tuple-element.58.w_ref), custom_call_target="tpu_custom_call" | custom-call | flops 2030043136 | bytes 7929856 | tf_op jit(solution)/shard_map/pallas_call | solution.py:270
  98.3 3.3 %shard_map.90 = f32[1,2816]{1,0:T(1,128)S(1)} custom-call(s32[4]{0:T(128)S(1)} %pad_add_fusion.place, bf16[2,128,2816]{2,1,0:T(8,128)(2,1)S(1)} %get-tuple-element.57.next_ref, bf16[2,128,2816]{2,1,0:T(8,128)(2,1)S(1)} %collective-permute-done.12.peer_ref, f32[128,2816]{1,0:T(8,128)S(1)} %get-tuple-element.54.n0_ref, ...), custom_call_target="tpu_custom_call" | custom-call | flops 2030043136 | bytes 7929856 | tf_op jit(solution)/shard_map/pallas_call | solution.py:259
  101.7 17.2 %all_to_all.21 = f32[8,1,2816]{2,1,0:T(1,128)S(1)} all-to-all(f32[8,1,2816]{2,1,0:T(1,128)S(1)} %broadcast_in_dim.8), channel_id=1, replica_groups={{0,32,64,96,128,160,192,224},{16,48,80,112,144,176,208,240},{4,36,68,10..., dimensions={0} | all-to-all | bytes 180224 | tf_op jit(solution)/shard_map/all_to_all | solution.py:357
  118.9 0.1 reduce_sum.27
  119.0 3.8 %collective-permute-start.13 = (f32[128,1408]{1,0:T(8,128)}, f32[128,1408]{1,0:T(8,128)}, u32[]{:S(2)}, u32[]{:S(2)}) collective-permute-start(f32[128,1408]{1,0:T(8,128)} %copy-done.4), channel_id=1, source_target_pairs={{0,16},{16,0},{32,48},{48,32},{64,80},{80,64},{96,112},{112,96},{1... | collective-permute-start | bytes 2162696 | tf_op jit(solution)/shard_map/ppermute | solution.py:46
  122.9 0.7 broadcast_in_dim.10
  123.5 6.0 %all-to-all-start.1 = ((f32[8,1,2816]{2,1,0:T(1,128)}), f32[8,1,2816]{2,1,0:T(1,128)S(1)}, u32[]{:S(2)}, u32[]{:S(2)}) async-start(f32[8,1,2816]{2,1,0:T(1,128)} %broadcast_in_dim.10), calls=%async_computation.1 | async-start | bytes 180224 | tf_op jit(solution)/shard_map/all_to_all | solution.py:357
  129.5 1.2 shard_map.91
  130.7 6.4 %all-to-all-done.1 = f32[8,1,2816]{2,1,0:T(1,128)S(1)} async-done(((f32[8,1,2816]{2,1,0:T(1,128)}), f32[8,1,2816]{2,1,0:T(1,128)S(1)}, u32[]{:S(2)}, u32[]{:S(2)}) %all-to-all-start.1) | async-done | bytes 90144 | tf_op jit(solution)/shard_map/all_to_all | solution.py:357
  137.1 0.7 broadcast_in_dim.22
  137.8 4.8 %all-to-all-start.2 = ((f32[8,1,2816]{2,1,0:T(1,128)}), f32[8,1,2816]{2,1,0:T(1,128)S(1)}, u32[]{:S(2)}, u32[]{:S(2)}) async-start(f32[8,1,2816]{2,1,0:T(1,128)} %broadcast_in_dim.22), calls=%async_computation.2 | async-start | bytes 180224 | tf_op jit(solution)/shard_map/all_to_all | solution.py:357
  142.6 2.7 %shard_map.92 = bf16[2640,128]{1,0:T(8,128)(2,1)} custom-call(s32[4]{0:T(128)S(1)} %pad_add_fusion.place, f32[128,1408]{1,0:T(8,128)S(1)} %get-tuple-element.63.s_ref, f32[128,1408]{1,0:T(8,128)} %collective-permute-done.13.got_ref, bf16[128,2816]{1,0:T(8,128)(2,1)S(1)} %get-tuple-element.55.inj_ref, bf16[128,2816]{1,0:T(8,128)(2,1)S(1)} %get-tuple-element.70.s1_ref), custom_call_target="tpu_custom_call" | custom-call | flops 1000000 | bytes 5000000 | tf_op jit(solution)/shard_map/pallas_call | solution.py:321
  145.3 2.3 %all-to-all-done.2 = f32[8,1,2816]{2,1,0:T(1,128)S(1)} async-done(((f32[8,1,2816]{2,1,0:T(1,128)}), f32[8,1,2816]{2,1,0:T(1,128)S(1)}, u32[]{:S(2)}, u32[]{:S(2)}) %all-to-all-start.2) | async-done | bytes 90144 | tf_op jit(solution)/shard_map/all_to_all | solution.py:357
  147.6 0.1 reduce_sum.29
  147.7 0.1 reshape_broadcast_in_dim.3
  147.8 0.7 reshape.35
  (21 shorter events, 0.2 us)
Async XLA Ops:
  0.6 15.7 %copy-start = (f32[128,2640]{0,1:T(8,128)S(1)}, f32[128,2640]{0,1:T(8,128)}, u32[]{:S(2)}) copy-start(f32[128,2640]{0,1:T(8,128)} %param.6) | copy-start | bytes 4055044
  1.5 1.2 copy-start.2
  3.8 16.5 %collective-permute-start.2 = (bf16[176,1408]{1,0:T(8,128)(2,1)S(1)}, bf16[176,1408]{1,0:T(8,128)(2,1)}, u32[]{:S(2)}, u32[]{:S(2)}) collective-permute-start(bf16[176,1408]{1,0:T(8,128)(2,1)S(1)} %shard_map.86), channel_id=1, source_target_pairs={{0,2},{16,24},{32,34},{48,56},{64,66},{80,88},{96,98},{112,120},{1... | collective-permute-start | bytes 1486856 | tf_op jit(solution)/shard_map/ppermute | solution.py:46
  8.9 18.5 %collective-permute-start.1 = (bf16[176,1408]{1,0:T(8,128)(2,1)S(1)}, bf16[176,1408]{1,0:T(8,128)(2,1)S(1)}, u32[]{:S(2)}, u32[]{:S(2)}) collective-permute-start(bf16[176,1408]{1,0:T(8,128)(2,1)S(1)} %shard_map.86), channel_id=1, source_target_pairs={{0,1},{16,20},{32,33},{48,52},{64,65},{80,84},{96,97},{112,116},{1... | collective-permute-start | bytes 1486856 | tf_op jit(solution)/shard_map/ppermute | solution.py:46
  12.1 15.3 %collective-permute-start = (bf16[176,1408]{1,0:T(8,128)(2,1)S(1)}, bf16[176,1408]{1,0:T(8,128)(2,1)}, u32[]{:S(2)}, u32[]{:S(2)}) collective-permute-start(bf16[176,1408]{1,0:T(8,128)(2,1)S(1)} %shard_map.86), channel_id=1, source_target_pairs={{0,3},{16,284},{32,35},{48,316},{64,67},{80,348},{96,99},{112,380}... | collective-permute-start | bytes 1486856 | tf_op jit(solution)/shard_map/ppermute | solution.py:46
  16.3 1.3 copy-start.1
  17.7 1.1 copy-start.3
  28.7 15.2 %collective-permute-start.7 = (bf16[2,176,1408]{2,1,0:T(8,128)(2,1)S(1)}, bf16[2,176,1408]{2,1,0:T(8,128)(2,1)S(1)}, u32[]{:S(2)}, u32[]{:S(2)}) collective-permute-start(bf16[2,176,1408]{2,1,0:T(8,128)(2,1)S(1)} %pad_maximum_fusion.1.rest_1_), channel_id=1, source_target_pairs={{0,268},{16,19},{32,300},{48,51},{64,332},{80,83},{96,364},{112,11... | collective-permute-start | bytes 2973704 | tf_op jit(solution)/shard_map/ppermute | solution.py:46
  32.9 16.4 %collective-permute-start.4 = (bf16[2,176,1408]{2,1,0:T(8,128)(2,1)S(1)}, bf16[2,176,1408]{2,1,0:T(8,128)(2,1)S(1)}, u32[]{:S(2)}, u32[]{:S(2)}) collective-permute-start(bf16[2,176,1408]{2,1,0:T(8,128)(2,1)S(1)} %pad_maximum_fusion.rest_0_), channel_id=1, source_target_pairs={{0,4},{16,17},{32,36},{48,49},{64,68},{80,81},{96,100},{112,113},{... | collective-permute-start | bytes 2973704 | tf_op jit(solution)/shard_map/ppermute | solution.py:46
  34.9 25.1 %collective-permute-start.3 = (bf16[2,128,2816]{2,1,0:T(8,128)(2,1)S(1)}, bf16[2,128,2816]{2,1,0:T(8,128)(2,1)S(1)}, u32[]{:S(2)}, u32[]{:S(2)}) collective-permute-start(bf16[2,128,2816]{2,1,0:T(8,128)(2,1)S(1)} %get-tuple-element.43.acts_ref), channel_id=1, source_target_pairs={{0,16},{16,0},{32,48},{48,32},{64,80},{80,64},{96,112},{112,96},{1... | collective-permute-start | bytes 4325384 | tf_op jit(solution)/shard_map/ppermute | solution.py:46
  37.4 22.5 %collective-permute-start.5 = (bf16[2,176,1408]{2,1,0:T(8,128)(2,1)S(1)}, bf16[2,176,1408]{2,1,0:T(8,128)(2,1)S(1)}, u32[]{:S(2)}, u32[]{:S(2)}) collective-permute-start(bf16[2,176,1408]{2,1,0:T(8,128)(2,1)S(1)} %pad_maximum_fusion.1.rest_1_), channel_id=1, source_target_pairs={{0,4},{16,17},{32,36},{48,49},{64,68},{80,81},{96,100},{112,113},{... | collective-permute-start | bytes 2973704 | tf_op jit(solution)/shard_map/ppermute | solution.py:46
  39.7 20.3 %collective-permute-start.6 = (bf16[2,176,1408]{2,1,0:T(8,128)(2,1)S(1)}, bf16[2,176,1408]{2,1,0:T(8,128)(2,1)S(1)}, u32[]{:S(2)}, u32[]{:S(2)}) collective-permute-start(bf16[2,176,1408]{2,1,0:T(8,128)(2,1)S(1)} %pad_maximum_fusion.rest_0_), channel_id=1, source_target_pairs={{0,268},{16,19},{32,300},{48,51},{64,332},{80,83},{96,364},{112,11... | collective-permute-start | bytes 2973704 | tf_op jit(solution)/shard_map/ppermute | solution.py:46
  44.0 21.7 %collective-permute-start.9 = (bf16[2,176,1408]{2,1,0:T(8,128)(2,1)S(1)}, bf16[2,176,1408]{2,1,0:T(8,128)(2,1)S(1)}, u32[]{:S(2)}, u32[]{:S(2)}) collective-permute-start(bf16[2,176,1408]{2,1,0:T(8,128)(2,1)S(1)} %collective-permute-done.7.rest_5_), channel_id=1, source_target_pairs={{0,268},{16,19},{32,300},{48,51},{64,332},{80,83},{96,364},{112,11... | collective-permute-start | bytes 2973704 | tf_op jit(solution)/shard_map/ppermute | solution.py:46
  49.4 20.9 %collective-permute-start.8 = (bf16[2,176,1408]{2,1,0:T(8,128)(2,1)S(1)}, bf16[2,176,1408]{2,1,0:T(8,128)(2,1)S(1)}, u32[]{:S(2)}, u32[]{:S(2)}) collective-permute-start(bf16[2,176,1408]{2,1,0:T(8,128)(2,1)S(1)} %collective-permute-done.4.rest_2_), channel_id=1, source_target_pairs={{0,4},{16,17},{32,36},{48,49},{64,68},{80,81},{96,100},{112,113},{... | collective-permute-start | bytes 2973704 | tf_op jit(solution)/shard_map/ppermute | solution.py:46
  82.1 6.1 %collective-permute-start.11 = (bf16[128,4224]{1,0:T(8,128)(2,1)S(1)}, bf16[128,4224]{1,0:T(8,128)(2,1)S(1)}, u32[]{:S(2)}, u32[]{:S(2)}) collective-permute-start(bf16[128,4224]{1,0:T(8,128)(2,1)S(1)} %get-tuple-element.52), channel_id=1, source_target_pairs={{0,16},{16,0},{32,48},{48,32},{64,80},{80,64},{96,112},{112,96},{1... | collective-permute-start | bytes 3244040 | tf_op jit(solution)/shard_map/ppermute | solution.py:46
  84.0 4.2 %collective-permute-start.10 = (bf16[128,2816]{1,0:T(8,128)(2,1)S(1)}, bf16[128,2816]{1,0:T(8,128)(2,1)S(1)}, u32[]{:S(2)}, u32[]{:S(2)}) collective-permute-start(bf16[128,2816]{1,0:T(8,128)(2,1)S(1)} %get-tuple-element.51), channel_id=1, source_target_pairs={{0,16},{16,0},{32,48},{48,32},{64,80},{80,64},{96,112},{112,96},{1... | collective-permute-start | bytes 2162696 | tf_op jit(solution)/shard_map/ppermute | solution.py:46
  90.7 5.1 %collective-permute-start.12 = (bf16[2,128,2816]{2,1,0:T(8,128)(2,1)S(1)}, bf16[2,128,2816]{2,1,0:T(8,128)(2,1)S(1)}, u32[]{:S(2)}, u32[]{:S(2)}) collective-permute-start(bf16[2,128,2816]{2,1,0:T(8,128)(2,1)S(1)} %get-tuple-element.57.next_ref), channel_id=1, source_target_pairs={{0,16},{16,0},{32,48},{48,32},{64,80},{80,64},{96,112},{112,96},{1... | collective-permute-start | bytes 4325384 | tf_op jit(solution)/shard_map/ppermute | solution.py:46
  98.3 3.3 %copy-start.4 = (f32[128,1408]{1,0:T(8,128)}, f32[128,1408]{1,0:T(8,128)S(1)}, u32[]{:S(2)}) copy-start(f32[128,1408]{1,0:T(8,128)S(1)} %get-tuple-element.66) | copy-start | bytes 2162692
  119.0 18.1 %collective-permute-start.13 = (f32[128,1408]{1,0:T(8,128)}, f32[128,1408]{1,0:T(8,128)}, u32[]{:S(2)}, u32[]{:S(2)}) collective-permute-start(f32[128,1408]{1,0:T(8,128)} %copy-done.4), channel_id=1, source_target_pairs={{0,16},{16,0},{32,48},{48,32},{64,80},{80,64},{96,112},{112,96},{1... | collective-permute-start | bytes 2162696 | tf_op jit(solution)/shard_map/ppermute | solution.py:46
  123.5 13.6 %all-to-all-start.1 = ((f32[8,1,2816]{2,1,0:T(1,128)}), f32[8,1,2816]{2,1,0:T(1,128)S(1)}, u32[]{:S(2)}, u32[]{:S(2)}) async-start(f32[8,1,2816]{2,1,0:T(1,128)} %broadcast_in_dim.10), calls=%async_computation.1 | async-start | bytes 180224 | tf_op jit(solution)/shard_map/all_to_all | solution.py:357
  137.8 9.8 %all-to-all-start.2 = ((f32[8,1,2816]{2,1,0:T(1,128)}), f32[8,1,2816]{2,1,0:T(1,128)S(1)}, u32[]{:S(2)}, u32[]{:S(2)}) async-start(f32[8,1,2816]{2,1,0:T(1,128)} %broadcast_in_dim.22), calls=%async_computation.2 | async-start | bytes 180224 | tf_op jit(solution)/shard_map/all_to_all | solution.py:357

commit v9 on v8

--- a/solution.py
+++ b/solution.py
@@ -148,24 +148,26 @@
         for j in range(4):
             sx = jnp.where(pc == 0, px + 4 - j, px + 4 - k) % 4
             sy = jnp.where(pc == 0, py + 4 - k, py + 4 - j) % 4
-            row = pl.multiple_of((sy * 4 + sx) * SP, SP)
+            shard = sy * 4 + sx
+            row = pl.multiple_of(shard * SP, SP)
             src = pieces[PLACE[k] + j // 2].at[j % 2]
-            copies.append(pltpu.make_async_copy(src, w_ref.at[pl.ds(row, SP), :], sems.at[len(copies)]))
-    for c in copies:
-        c.start()
+            copies.append((shard, pltpu.make_async_copy(src, w_ref.at[pl.ds(row, SP), :], sems.at[shard])))
+    for late in range(2):
+        for shard, copy in copies:
+            pl.when(shard // 8 == late)(copy.start)
     both_ref[:TOK] = acts_ref[0]
     both_ref[TOK:] = peer_ref[0]
     grads = jnp.concatenate([acts_ref[1, :, half_of(pc)], peer_ref[1, :, half_of(pc)]], axis=0)
-    for c in copies:
-        c.wait()
-    s1 = jnp.dot(both_ref[...], w_ref[...], preferred_element_type=F32)
-    s_ref[...] = s1[:TOK]
-    give_ref[:, :HALF] = s1[TOK:].astype(BF)
     for t in range(2):
+        for shard in range(8 * t, 8 * t + 8):
+            pltpu.make_async_copy(pieces[0].at[0], w_ref.at[SP * shard : SP * shard + SP, :], sems.at[shard]).wait()
         rows = slice(t * HALF, t * HALF + HALF)
         back = nt(grads, w_ref[rows, :])
         back_ref[:, rows] = back[:TOK]
         give_ref[:, HALF + t * HALF : 2 * HALF + t * HALF] = back[TOK:].astype(BF)
+    s1 = jnp.dot(both_ref[...], w_ref[...], preferred_element_type=F32)
+    s_ref[...] = s1[:TOK]
+    give_ref[:, :HALF] = s1[TOK:].astype(BF)
 
 
 def middle_kernel(place, s_ref, back_ref, got_ref, n0_ref, inj_ref, cot_ref, gain_ref, next_ref, injg_ref, part_ref, s1_out_ref, s1_ref):

time: 149 us -> 150 us (level)
  no operation moved by 1% of the time
where the time goes in v9:
time: 150 us; the launch traced here: 149 us
  starting transfers between devices  55.2 us (37%)
  waiting for transfers between devices  39.4 us (26%)
  Pallas kernels  27.2 us (18%)
  blocking collectives  17.2 us (11%)
  local copies, waits for them, and re-layouts  6.72 us (4%)
  other arithmetic  1.7 us (1%)
  between operations  1.7 us (1%)
    ppermute x14, starting transfers between devices, send(): return lax.ppermute(array, AXES, pairs)  44.4 us
    ppermute x14, waiting for transfers between devices, send(): return lax.ppermute(array, AXES, pairs)  30.7 us
    all_to_all x1, blocking collectives, spreads(): lax.all_to_all(jnp.broadcast_to(part, (8, WP)), AXES, 0, 0, axis_index_gr...  17.2 us
    pallas_call x1, Pallas kernels, first_call(): pl.pallas_call(first_kernel, out_shape=(shape(TOK, HALF), shape(TOK, WP),...  12.4 us
    all_to_all x2, starting transfers between devices, spreads(): lax.all_to_all(jnp.broadcast_to(part, (8, WP)), AXES, 0, 0, axis_index_gr...  10.8 us
    all_to_all x2, waiting for transfers between devices, spreads(): lax.all_to_all(jnp.broadcast_to(part, (8, WP)), AXES, 0, 0, axis_index_gr...  8.68 us
    unnamed x11, local copies, waits for them, and re-layouts  3.61 us
    pallas_call x1, Pallas kernels, grads_call(): pl.pallas_call(grads_kernel, out_shape=shape(1, WP), in_specs=[SM] + [VM]...  3.31 us
  transfers between devices with their start and end apart: 16, of which 9 were waited for; matrix products, arithmetic and copies ran while one was open for 1% of the time, Pallas kernels for 4%

profile of v9, /device:TPU:1, one launch (start us, length us, event | category | flops | bytes accessed | tf_op | source)
XLA Modules:
  0.0 149.1 jit_solution(7924335894901948739)
XLA Ops:
  1.4 0.1 pad_add_fusion.place
  1.5 1.2 copy-done.2
  2.7 1.2 shard_map.86
  3.8 5.0 %collective-permute-start.2 = (bf16[176,1408]{1,0:T(8,128)(2,1)S(1)}, bf16[176,1408]{1,0:T(8,128)(2,1)}, u32[]{:S(2)}, u32[]{:S(2)}) collective-permute-start(bf16[176,1408]{1,0:T(8,128)(2,1)S(1)} %shard_map.86), channel_id=1, source_target_pairs={{0,2},{16,24},{32,34},{48,56},{64,66},{80,88},{96,98},{112,120},{1... | collective-permute-start | bytes 1486856 | tf_op jit(solution)/shard_map/ppermute | solution.py:46
  8.9 3.2 %collective-permute-start.1 = (bf16[176,1408]{1,0:T(8,128)(2,1)S(1)}, bf16[176,1408]{1,0:T(8,128)(2,1)S(1)}, u32[]{:S(2)}, u32[]{:S(2)}) collective-permute-start(bf16[176,1408]{1,0:T(8,128)(2,1)S(1)} %shard_map.86), channel_id=1, source_target_pairs={{0,1},{16,20},{32,33},{48,52},{64,65},{80,84},{96,97},{112,116},{1... | collective-permute-start | bytes 1486856 | tf_op jit(solution)/shard_map/ppermute | solution.py:46
  12.1 3.3 %collective-permute-start = (bf16[176,1408]{1,0:T(8,128)(2,1)S(1)}, bf16[176,1408]{1,0:T(8,128)(2,1)}, u32[]{:S(2)}, u32[]{:S(2)}) collective-permute-start(bf16[176,1408]{1,0:T(8,128)(2,1)S(1)} %shard_map.86), channel_id=1, source_target_pairs={{0,3},{16,284},{32,35},{48,316},{64,67},{80,348},{96,99},{112,380}... | collective-permute-start | bytes 1486856 | tf_op jit(solution)/shard_map/ppermute | solution.py:46
  15.4 0.8 reshape.33
  16.2 0.1 reshape.34.gain_ref
  16.3 1.3 copy-done.1
  17.7 1.1 copy-done.3
  18.8 1.5 %shard_map.85 = (f32[128,2816]{1,0:T(8,128)S(1)}, bf16[128,2816]{1,0:T(8,128)(2,1)S(1)}, bf16[2,128,2816]{2,1,0:T(8,128)(2,1)S(1)}, bf16[128,2816]{1,0:T(8,128)(2,1)S(1)}, f32[128,2816]{1,0:T(8,128)S(1)}) custom-call(f32[2640,128]{1,0:T(8,128)S(1)} %bitcast.17, bf16[2640,128]{1,0:T(8,128)(2,1)S(1)} %bitcast.19, f32[2640,128]{1,0:T(8,128)S(1)} %bitcast.18, ...), custom_call_target="tpu_custom_call" | custom-call | flops 1000000 | bytes 10000000 | tf_op jit(solution)/shard_map/pallas_call | solution.py:123
  20.3 7.1 %collective-permute-done.1 = bf16[176,1408]{1,0:T(8,128)(2,1)S(1)} collective-permute-done((bf16[176,1408]{1,0:T(8,128)(2,1)S(1)}, bf16[176,1408]{1,0:T(8,128)(2,1)S(1)}, u32[]{:S(2)}, u32[]{:S(2)}) %collective-permute-start.1) | collective-permute-done | bytes 495648 | tf_op jit(solution)/shard_map/ppermute | solution.py:46
  27.4 1.3 pad_maximum_fusion.1.rest_1_
  28.7 4.1 %collective-permute-start.7 = (bf16[2,176,1408]{2,1,0:T(8,128)(2,1)S(1)}, bf16[2,176,1408]{2,1,0:T(8,128)(2,1)S(1)}, u32[]{:S(2)}, u32[]{:S(2)}) collective-permute-start(bf16[2,176,1408]{2,1,0:T(8,128)(2,1)S(1)} %pad_maximum_fusion.1.rest_1_), channel_id=1, source_target_pairs={{0,268},{16,19},{32,300},{48,51},{64,332},{80,83},{96,364},{112,11... | collective-permute-start | bytes 2973704 | tf_op jit(solution)/shard_map/ppermute | solution.py:46
  32.8 0.1 pad_maximum_fusion.rest_0_
  32.9 1.9 %collective-permute-start.4 = (bf16[2,176,1408]{2,1,0:T(8,128)(2,1)S(1)}, bf16[2,176,1408]{2,1,0:T(8,128)(2,1)S(1)}, u32[]{:S(2)}, u32[]{:S(2)}) collective-permute-start(bf16[2,176,1408]{2,1,0:T(8,128)(2,1)S(1)} %pad_maximum_fusion.rest_0_), channel_id=1, source_target_pairs={{0,4},{16,17},{32,36},{48,49},{64,68},{80,81},{96,100},{112,113},{... | collective-permute-start | bytes 2973704 | tf_op jit(solution)/shard_map/ppermute | solution.py:46
  34.9 2.6 %collective-permute-start.3 = (bf16[2,128,2816]{2,1,0:T(8,128)(2,1)S(1)}, bf16[2,128,2816]{2,1,0:T(8,128)(2,1)S(1)}, u32[]{:S(2)}, u32[]{:S(2)}) collective-permute-start(bf16[2,128,2816]{2,1,0:T(8,128)(2,1)S(1)} %get-tuple-element.43.acts_ref), channel_id=1, source_target_pairs={{0,16},{16,0},{32,48},{48,32},{64,80},{80,64},{96,112},{112,96},{1... | collective-permute-start | bytes 4325384 | tf_op jit(solution)/shard_map/ppermute | solution.py:46
  37.4 2.2 %collective-permute-start.5 = (bf16[2,176,1408]{2,1,0:T(8,128)(2,1)S(1)}, bf16[2,176,1408]{2,1,0:T(8,128)(2,1)S(1)}, u32[]{:S(2)}, u32[]{:S(2)}) collective-permute-start(bf16[2,176,1408]{2,1,0:T(8,128)(2,1)S(1)} %pad_maximum_fusion.1.rest_1_), channel_id=1, source_target_pairs={{0,4},{16,17},{32,36},{48,49},{64,68},{80,81},{96,100},{112,113},{... | collective-permute-start | bytes 2973704 | tf_op jit(solution)/shard_map/ppermute | solution.py:46
  39.7 4.3 %collective-permute-start.6 = (bf16[2,176,1408]{2,1,0:T(8,128)(2,1)S(1)}, bf16[2,176,1408]{2,1,0:T(8,128)(2,1)S(1)}, u32[]{:S(2)}, u32[]{:S(2)}) collective-permute-start(bf16[2,176,1408]{2,1,0:T(8,128)(2,1)S(1)} %pad_maximum_fusion.rest_0_), channel_id=1, source_target_pairs={{0,268},{16,19},{32,300},{48,51},{64,332},{80,83},{96,364},{112,11... | collective-permute-start | bytes 2973704 | tf_op jit(solution)/shard_map/ppermute | solution.py:46
  44.0 5.3 %collective-permute-start.9 = (bf16[2,176,1408]{2,1,0:T(8,128)(2,1)S(1)}, bf16[2,176,1408]{2,1,0:T(8,128)(2,1)S(1)}, u32[]{:S(2)}, u32[]{:S(2)}) collective-permute-start(bf16[2,176,1408]{2,1,0:T(8,128)(2,1)S(1)} %collective-permute-done.7.rest_5_), channel_id=1, source_target_pairs={{0,268},{16,19},{32,300},{48,51},{64,332},{80,83},{96,364},{112,11... | collective-permute-start | bytes 2973704 | tf_op jit(solution)/shard_map/ppermute | solution.py:46
  49.2 0.1 collective-permute-done.4.rest_2_
  49.4 1.9 %collective-permute-start.8 = (bf16[2,176,1408]{2,1,0:T(8,128)(2,1)S(1)}, bf16[2,176,1408]{2,1,0:T(8,128)(2,1)S(1)}, u32[]{:S(2)}, u32[]{:S(2)}) collective-permute-start(bf16[2,176,1408]{2,1,0:T(8,128)(2,1)S(1)} %collective-permute-done.4.rest_2_), channel_id=1, source_target_pairs={{0,4},{16,17},{32,36},{48,49},{64,68},{80,81},{96,100},{112,113},{... | collective-permute-start | bytes 2973704 | tf_op jit(solution)/shard_map/ppermute | solution.py:46
  51.3 8.7 %collective-permute-done.5.rest_3_ = bf16[2,176,1408]{2,1,0:T(8,128)(2,1)S(1)} collective-permute-done((bf16[2,176,1408]{2,1,0:T(8,128)(2,1)S(1)}, bf16[2,176,1408]{2,1,0:T(8,128)(2,1)S(1)}, u32[]{:S(2)}, u32[]{:S(2)}) %collective-permute-start.5) | collective-permute-done | bytes 991264 | tf_op jit(solution)/shard_map/ppermute | solution.py:46
  60.0 5.7 %collective-permute-done.9.rest_7_ = bf16[2,176,1408]{2,1,0:T(8,128)(2,1)S(1)} collective-permute-done((bf16[2,176,1408]{2,1,0:T(8,128)(2,1)S(1)}, bf16[2,176,1408]{2,1,0:T(8,128)(2,1)S(1)}, u32[]{:S(2)}, u32[]{:S(2)}) %collective-permute-start.9) | collective-permute-done | bytes 991264 | tf_op jit(solution)/shard_map/ppermute | solution.py:46
  65.7 4.6 %collective-permute-done.8.rest_6_ = bf16[2,176,1408]{2,1,0:T(8,128)(2,1)S(1)} collective-permute-done((bf16[2,176,1408]{2,1,0:T(8,128)(2,1)S(1)}, bf16[2,176,1408]{2,1,0:T(8,128)(2,1)S(1)}, u32[]{:S(2)}, u32[]{:S(2)}) %collective-permute-start.8) | collective-permute-done | bytes 991264 | tf_op jit(solution)/shard_map/ppermute | solution.py:46
  70.3 12.4 %shard_map.87 = (f32[128,1408]{1,0:T(8,128)S(1)}, f32[128,2816]{1,0:T(8,128)S(1)}, bf16[128,4224]{1,0:T(8,128)(2,1)S(1)}, bf16[2816,1408]{1,0:T(8,128)(2,1)S(1)}) custom-call(s32[4]{0:T(128)S(1)} %pad_add_fusion.place, bf16[2,128,2816]{2,1,0:T(8,128)(2,1)S(1)} %get-tuple-element.43.acts_ref, bf16[2,128,2816]{2,1,0:T(8,128)(2,1)S(1)} %collective-permute-done.3.peer_ref, ...), custom_call_target="tpu_custom_call" | custom-call | flops 4060086272 | bytes 7929856 | tf_op jit(solution)/shard_map/pallas_call | solution.py:237
  82.7 1.9 %collective-permute-start.11 = (bf16[128,4224]{1,0:T(8,128)(2,1)S(1)}, bf16[128,4224]{1,0:T(8,128)(2,1)S(1)}, u32[]{:S(2)}, u32[]{:S(2)}) collective-permute-start(bf16[128,4224]{1,0:T(8,128)(2,1)S(1)} %get-tuple-element.52), channel_id=1, source_target_pairs={{0,16},{16,0},{32,48},{48,32},{64,80},{80,64},{96,112},{112,96},{1... | collective-permute-start | bytes 3244040 | tf_op jit(solution)/shard_map/ppermute | solution.py:46
  84.7 2.4 %collective-permute-start.10 = (bf16[128,2816]{1,0:T(8,128)(2,1)S(1)}, bf16[128,2816]{1,0:T(8,128)(2,1)S(1)}, u32[]{:S(2)}, u32[]{:S(2)}) collective-permute-start(bf16[128,2816]{1,0:T(8,128)(2,1)S(1)} %get-tuple-element.51), channel_id=1, source_target_pairs={{0,16},{16,0},{32,48},{48,32},{64,80},{80,64},{96,112},{112,96},{1... | collective-permute-start | bytes 2162696 | tf_op jit(solution)/shard_map/ppermute | solution.py:46
  87.1 1.8 %collective-permute-done.10.n0_peer_ref = bf16[128,2816]{1,0:T(8,128)(2,1)S(1)} collective-permute-done((bf16[128,2816]{1,0:T(8,128)(2,1)S(1)}, bf16[128,2816]{1,0:T(8,128)(2,1)S(1)}, u32[]{:S(2)}, u32[]{:S(2)}) %collective-permute-start.10) | collective-permute-done | bytes 720928 | tf_op jit(solution)/shard_map/ppermute | solution.py:46
  88.9 2.4 %shard_map.88 = (bf16[2,128,2816]{2,1,0:T(8,128)(2,1)S(1)}, bf16[128,2816]{1,0:T(8,128)(2,1)S(1)}, f32[1,2816]{1,0:T(1,128)S(1)}, bf16[128,2816]{1,0:T(8,128)(2,1)S(1)}) custom-call(s32[4]{0:T(128)S(1)} %pad_add_fusion.place, f32[128,1408]{1,0:T(8,128)S(1)} %get-tuple-element.47.s_ref, f32[128,2816]{1,0:T(8,128)S(1)} %get-tuple-element.48.back_ref, ...), custom_call_target="tpu_custom_call" | custom-call | flops 7208960 | bytes 10000000 | tf_op jit(solution)/shard_map/pallas_call | solution.py:249
  91.3 2.5 %collective-permute-start.12 = (bf16[2,128,2816]{2,1,0:T(8,128)(2,1)S(1)}, bf16[2,128,2816]{2,1,0:T(8,128)(2,1)S(1)}, u32[]{:S(2)}, u32[]{:S(2)}) collective-permute-start(bf16[2,128,2816]{2,1,0:T(8,128)(2,1)S(1)} %get-tuple-element.57.next_ref), channel_id=1, source_target_pairs={{0,16},{16,0},{32,48},{48,32},{64,80},{80,64},{96,112},{112,96},{1... | collective-permute-start | bytes 4325384 | tf_op jit(solution)/shard_map/ppermute | solution.py:46
  93.8 2.6 %collective-permute-done.12.peer_ref = bf16[2,128,2816]{2,1,0:T(8,128)(2,1)S(1)} collective-permute-done((bf16[2,128,2816]{2,1,0:T(8,128)(2,1)S(1)}, bf16[2,128,2816]{2,1,0:T(8,128)(2,1)S(1)}, u32[]{:S(2)}, u32[]{:S(2)}) %collective-permute-start.12) | collective-permute-done | bytes 1441824 | tf_op jit(solution)/shard_map/ppermute | solution.py:46
  96.4 2.4 %shard_map.89 = (f32[128,1408]{1,0:T(8,128)S(1)}, f32[128,1408]{1,0:T(8,128)S(1)}) custom-call(bf16[2,128,2816]{2,1,0:T(8,128)(2,1)S(1)} %get-tuple-element.57.next_ref, bf16[2,128,2816]{2,1,0:T(8,128)(2,1)S(1)} %collective-permute-done.12.peer_ref, bf16[2816,1408]{1,0:T(8,128)(2,1)S(1)} %get-tuple-element.58.w_ref), custom_call_target="tpu_custom_call" | custom-call | flops 2030043136 | bytes 7929856 | tf_op jit(solution)/shard_map/pallas_call | solution.py:272
  98.9 3.3 %shard_map.90 = f32[1,2816]{1,0:T(1,128)S(1)} custom-call(s32[4]{0:T(128)S(1)} %pad_add_fusion.place, bf16[2,128,2816]{2,1,0:T(8,128)(2,1)S(1)} %get-tuple-element.57.next_ref, bf16[2,128,2816]{2,1,0:T(8,128)(2,1)S(1)} %collective-permute-done.12.peer_ref, f32[128,2816]{1,0:T(8,128)S(1)} %get-tuple-element.54.n0_ref, ...), custom_call_target="tpu_custom_call" | custom-call | flops 2030043136 | bytes 7929856 | tf_op jit(solution)/shard_map/pallas_call | solution.py:261
  102.3 17.2 %all_to_all.21 = f32[8,1,2816]{2,1,0:T(1,128)S(1)} all-to-all(f32[8,1,2816]{2,1,0:T(1,128)S(1)} %broadcast_in_dim.8), channel_id=1, replica_groups={{0,32,64,96,128,160,192,224},{16,48,80,112,144,176,208,240},{4,36,68,10..., dimensions={0} | all-to-all | bytes 180224 | tf_op jit(solution)/shard_map/all_to_all | solution.py:359
  119.5 0.1 reduce_sum.27
  119.6 3.8 %collective-permute-start.13 = (f32[128,1408]{1,0:T(8,128)}, f32[128,1408]{1,0:T(8,128)}, u32[]{:S(2)}, u32[]{:S(2)}) collective-permute-start(f32[128,1408]{1,0:T(8,128)} %copy-done.4), channel_id=1, source_target_pairs={{0,16},{16,0},{32,48},{48,32},{64,80},{80,64},{96,112},{112,96},{1... | collective-permute-start | bytes 2162696 | tf_op jit(solution)/shard_map/ppermute | solution.py:46
  123.5 0.7 broadcast_in_dim.10
  124.2 6.0 %all-to-all-start.1 = ((f32[8,1,2816]{2,1,0:T(1,128)}), f32[8,1,2816]{2,1,0:T(1,128)S(1)}, u32[]{:S(2)}, u32[]{:S(2)}) async-start(f32[8,1,2816]{2,1,0:T(1,128)} %broadcast_in_dim.10), calls=%async_computation.1 | async-start | bytes 180224 | tf_op jit(solution)/shard_map/all_to_all | solution.py:359
  130.1 1.2 shard_map.91
  131.3 6.4 %all-to-all-done.1 = f32[8,1,2816]{2,1,0:T(1,128)S(1)} async-done(((f32[8,1,2816]{2,1,0:T(1,128)}), f32[8,1,2816]{2,1,0:T(1,128)S(1)}, u32[]{:S(2)}, u32[]{:S(2)}) %all-to-all-start.1) | async-done | bytes 90144 | tf_op jit(solution)/shard_map/all_to_all | solution.py:359
  137.8 0.7 broadcast_in_dim.22
  138.4 4.8 %all-to-all-start.2 = ((f32[8,1,2816]{2,1,0:T(1,128)}), f32[8,1,2816]{2,1,0:T(1,128)S(1)}, u32[]{:S(2)}, u32[]{:S(2)}) async-start(f32[8,1,2816]{2,1,0:T(1,128)} %broadcast_in_dim.22), calls=%async_computation.2 | async-start | bytes 180224 | tf_op jit(solution)/shard_map/all_to_all | solution.py:359
  143.3 2.7 %shard_map.92 = bf16[2640,128]{1,0:T(8,128)(2,1)} custom-call(s32[4]{0:T(128)S(1)} %pad_add_fusion.place, f32[128,1408]{1,0:T(8,128)S(1)} %get-tuple-element.63.s_ref, f32[128,1408]{1,0:T(8,128)} %collective-permute-done.13.got_ref, bf16[128,2816]{1,0:T(8,128)(2,1)S(1)} %get-tuple-element.55.inj_ref, bf16[128,2816]{1,0:T(8,128)(2,1)S(1)} %get-tuple-element.70.s1_ref), custom_call_target="tpu_custom_call" | custom-call | flops 1000000 | bytes 5000000 | tf_op jit(solution)/shard_map/pallas_call | solution.py:323
  145.9 2.3 %all-to-all-done.2 = f32[8,1,2816]{2,1,0:T(1,128)S(1)} async-done(((f32[8,1,2816]{2,1,0:T(1,128)}), f32[8,1,2816]{2,1,0:T(1,128)S(1)}, u32[]{:S(2)}, u32[]{:S(2)}) %all-to-all-start.2) | async-done | bytes 90144 | tf_op jit(solution)/shard_map/all_to_all | solution.py:359
  148.2 0.1 reduce_sum.29
  148.3 0.1 reshape_broadcast_in_dim.3
  148.4 0.7 reshape.35
  (21 shorter events, 0.2 us)
Async XLA Ops:
  0.6 15.7 %copy-start = (f32[128,2640]{0,1:T(8,128)S(1)}, f32[128,2640]{0,1:T(8,128)}, u32[]{:S(2)}) copy-start(f32[128,2640]{0,1:T(8,128)} %param.6) | copy-start | bytes 4055044
  1.5 1.2 copy-start.2
  3.8 16.5 %collective-permute-start.2 = (bf16[176,1408]{1,0:T(8,128)(2,1)S(1)}, bf16[176,1408]{1,0:T(8,128)(2,1)}, u32[]{:S(2)}, u32[]{:S(2)}) collective-permute-start(bf16[176,1408]{1,0:T(8,128)(2,1)S(1)} %shard_map.86), channel_id=1, source_target_pairs={{0,2},{16,24},{32,34},{48,56},{64,66},{80,88},{96,98},{112,120},{1... | collective-permute-start | bytes 1486856 | tf_op jit(solution)/shard_map/ppermute | solution.py:46
  8.9 18.5 %collective-permute-start.1 = (bf16[176,1408]{1,0:T(8,128)(2,1)S(1)}, bf16[176,1408]{1,0:T(8,128)(2,1)S(1)}, u32[]{:S(2)}, u32[]{:S(2)}) collective-permute-start(bf16[176,1408]{1,0:T(8,128)(2,1)S(1)} %shard_map.86), channel_id=1, source_target_pairs={{0,1},{16,20},{32,33},{48,52},{64,65},{80,84},{96,97},{112,116},{1... | collective-permute-start | bytes 1486856 | tf_op jit(solution)/shard_map/ppermute | solution.py:46
  12.1 15.3 %collective-permute-start = (bf16[176,1408]{1,0:T(8,128)(2,1)S(1)}, bf16[176,1408]{1,0:T(8,128)(2,1)}, u32[]{:S(2)}, u32[]{:S(2)}) collective-permute-start(bf16[176,1408]{1,0:T(8,128)(2,1)S(1)} %shard_map.86), channel_id=1, source_target_pairs={{0,3},{16,284},{32,35},{48,316},{64,67},{80,348},{96,99},{112,380}... | collective-permute-start | bytes 1486856 | tf_op jit(solution)/shard_map/ppermute | solution.py:46
  16.3 1.3 copy-start.1
  17.7 1.1 copy-start.3
  28.7 15.2 %collective-permute-start.7 = (bf16[2,176,1408]{2,1,0:T(8,128)(2,1)S(1)}, bf16[2,176,1408]{2,1,0:T(8,128)(2,1)S(1)}, u32[]{:S(2)}, u32[]{:S(2)}) collective-permute-start(bf16[2,176,1408]{2,1,0:T(8,128)(2,1)S(1)} %pad_maximum_fusion.1.rest_1_), channel_id=1, source_target_pairs={{0,268},{16,19},{32,300},{48,51},{64,332},{80,83},{96,364},{112,11... | collective-permute-start | bytes 2973704 | tf_op jit(solution)/shard_map/ppermute | solution.py:46
  32.9 16.4 %collective-permute-start.4 = (bf16[2,176,1408]{2,1,0:T(8,128)(2,1)S(1)}, bf16[2,176,1408]{2,1,0:T(8,128)(2,1)S(1)}, u32[]{:S(2)}, u32[]{:S(2)}) collective-permute-start(bf16[2,176,1408]{2,1,0:T(8,128)(2,1)S(1)} %pad_maximum_fusion.rest_0_), channel_id=1, source_target_pairs={{0,4},{16,17},{32,36},{48,49},{64,68},{80,81},{96,100},{112,113},{... | collective-permute-start | bytes 2973704 | tf_op jit(solution)/shard_map/ppermute | solution.py:46
  34.9 25.1 %collective-permute-start.3 = (bf16[2,128,2816]{2,1,0:T(8,128)(2,1)S(1)}, bf16[2,128,2816]{2,1,0:T(8,128)(2,1)S(1)}, u32[]{:S(2)}, u32[]{:S(2)}) collective-permute-start(bf16[2,128,2816]{2,1,0:T(8,128)(2,1)S(1)} %get-tuple-element.43.acts_ref), channel_id=1, source_target_pairs={{0,16},{16,0},{32,48},{48,32},{64,80},{80,64},{96,112},{112,96},{1... | collective-permute-start | bytes 4325384 | tf_op jit(solution)/shard_map/ppermute | solution.py:46
  37.4 22.5 %collective-permute-start.5 = (bf16[2,176,1408]{2,1,0:T(8,128)(2,1)S(1)}, bf16[2,176,1408]{2,1,0:T(8,128)(2,1)S(1)}, u32[]{:S(2)}, u32[]{:S(2)}) collective-permute-start(bf16[2,176,1408]{2,1,0:T(8,128)(2,1)S(1)} %pad_maximum_fusion.1.rest_1_), channel_id=1, source_target_pairs={{0,4},{16,17},{32,36},{48,49},{64,68},{80,81},{96,100},{112,113},{... | collective-permute-start | bytes 2973704 | tf_op jit(solution)/shard_map/ppermute | solution.py:46
  39.7 20.3 %collective-permute-start.6 = (bf16[2,176,1408]{2,1,0:T(8,128)(2,1)S(1)}, bf16[2,176,1408]{2,1,0:T(8,128)(2,1)S(1)}, u32[]{:S(2)}, u32[]{:S(2)}) collective-permute-start(bf16[2,176,1408]{2,1,0:T(8,128)(2,1)S(1)} %pad_maximum_fusion.rest_0_), channel_id=1, source_target_pairs={{0,268},{16,19},{32,300},{48,51},{64,332},{80,83},{96,364},{112,11... | collective-permute-start | bytes 2973704 | tf_op jit(solution)/shard_map/ppermute | solution.py:46
  44.0 21.7 %collective-permute-start.9 = (bf16[2,176,1408]{2,1,0:T(8,128)(2,1)S(1)}, bf16[2,176,1408]{2,1,0:T(8,128)(2,1)S(1)}, u32[]{:S(2)}, u32[]{:S(2)}) collective-permute-start(bf16[2,176,1408]{2,1,0:T(8,128)(2,1)S(1)} %collective-permute-done.7.rest_5_), channel_id=1, source_target_pairs={{0,268},{16,19},{32,300},{48,51},{64,332},{80,83},{96,364},{112,11... | collective-permute-start | bytes 2973704 | tf_op jit(solution)/shard_map/ppermute | solution.py:46
  49.4 20.9 %collective-permute-start.8 = (bf16[2,176,1408]{2,1,0:T(8,128)(2,1)S(1)}, bf16[2,176,1408]{2,1,0:T(8,128)(2,1)S(1)}, u32[]{:S(2)}, u32[]{:S(2)}) collective-permute-start(bf16[2,176,1408]{2,1,0:T(8,128)(2,1)S(1)} %collective-permute-done.4.rest_2_), channel_id=1, source_target_pairs={{0,4},{16,17},{32,36},{48,49},{64,68},{80,81},{96,100},{112,113},{... | collective-permute-start | bytes 2973704 | tf_op jit(solution)/shard_map/ppermute | solution.py:46
  82.7 6.1 %collective-permute-start.11 = (bf16[128,4224]{1,0:T(8,128)(2,1)S(1)}, bf16[128,4224]{1,0:T(8,128)(2,1)S(1)}, u32[]{:S(2)}, u32[]{:S(2)}) collective-permute-start(bf16[128,4224]{1,0:T(8,128)(2,1)S(1)} %get-tuple-element.52), channel_id=1, source_target_pairs={{0,16},{16,0},{32,48},{48,32},{64,80},{80,64},{96,112},{112,96},{1... | collective-permute-start | bytes 3244040 | tf_op jit(solution)/shard_map/ppermute | solution.py:46
  84.7 4.2 %collective-permute-start.10 = (bf16[128,2816]{1,0:T(8,128)(2,1)S(1)}, bf16[128,2816]{1,0:T(8,128)(2,1)S(1)}, u32[]{:S(2)}, u32[]{:S(2)}) collective-permute-start(bf16[128,2816]{1,0:T(8,128)(2,1)S(1)} %get-tuple-element.51), channel_id=1, source_target_pairs={{0,16},{16,0},{32,48},{48,32},{64,80},{80,64},{96,112},{112,96},{1... | collective-permute-start | bytes 2162696 | tf_op jit(solution)/shard_map/ppermute | solution.py:46
  91.3 5.1 %collective-permute-start.12 = (bf16[2,128,2816]{2,1,0:T(8,128)(2,1)S(1)}, bf16[2,128,2816]{2,1,0:T(8,128)(2,1)S(1)}, u32[]{:S(2)}, u32[]{:S(2)}) collective-permute-start(bf16[2,128,2816]{2,1,0:T(8,128)(2,1)S(1)} %get-tuple-element.57.next_ref), channel_id=1, source_target_pairs={{0,16},{16,0},{32,48},{48,32},{64,80},{80,64},{96,112},{112,96},{1... | collective-permute-start | bytes 4325384 | tf_op jit(solution)/shard_map/ppermute | solution.py:46
  98.9 3.3 %copy-start.4 = (f32[128,1408]{1,0:T(8,128)}, f32[128,1408]{1,0:T(8,128)S(1)}, u32[]{:S(2)}) copy-start(f32[128,1408]{1,0:T(8,128)S(1)} %get-tuple-element.66) | copy-start | bytes 2162692
  119.6 18.1 %collective-permute-start.13 = (f32[128,1408]{1,0:T(8,128)}, f32[128,1408]{1,0:T(8,128)}, u32[]{:S(2)}, u32[]{:S(2)}) collective-permute-start(f32[128,1408]{1,0:T(8,128)} %copy-done.4), channel_id=1, source_target_pairs={{0,16},{16,0},{32,48},{48,32},{64,80},{80,64},{96,112},{112,96},{1... | collective-permute-start | bytes 2162696 | tf_op jit(solution)/shard_map/ppermute | solution.py:46
  124.2 13.6 %all-to-all-start.1 = ((f32[8,1,2816]{2,1,0:T(1,128)}), f32[8,1,2816]{2,1,0:T(1,128)S(1)}, u32[]{:S(2)}, u32[]{:S(2)}) async-start(f32[8,1,2816]{2,1,0:T(1,128)} %broadcast_in_dim.10), calls=%async_computation.1 | async-start | bytes 180224 | tf_op jit(solution)/shard_map/all_to_all | solution.py:359
  138.4 9.8 %all-to-all-start.2 = ((f32[8,1,2816]{2,1,0:T(1,128)}), f32[8,1,2816]{2,1,0:T(1,128)S(1)}, u32[]{:S(2)}, u32[]{:S(2)}) async-start(f32[8,1,2816]{2,1,0:T(1,128)} %broadcast_in_dim.22), calls=%async_computation.2 | async-start | bytes 180224 | tf_op jit(solution)/shard_map/all_to_all | solution.py:359
